TPU v7x, 128 devices: a whole 4x4x4 slice. The times are simulated.
128 devices in a mesh: tile: 32 (over y, z, core), tm: 4 (over x).
Axes of the slice: x: 4, y: 4, z: 4, core: 2. Of those that a mesh axis runs over, the one named last changes fastest.
Arguments:
- features: bfloat16 [128, 128, 128, 128], P('tm', 'tile'), may hold values from -6 to 6
- norm_gain: float32 [128], replicated, may hold values from 0.5 to 2
- conv_weight: bfloat16 [128, 81], replicated, may hold values from -0.109375 to 0.109375
- colour_bias: float32 [3], replicated, may hold values from -3 to 3
- observed_frames: int32 [4, 32, 3], P('tm'), may hold values from 0 to 31, as said below
- observed_counts: int32 [4, 32], P('tm'), may hold values from 0 to 3, as said below
- key_rows: int32 [128, 17], P('tm'), may hold values from 0 to 31
- key_columns: int32 [128, 17], P('tm'), may hold values from 0 to 31
- key_visible: int32 [128, 17], P('tm'), may hold values 0 or 1
- position_table: bfloat16 [64, 1280], replicated, may hold values from -6 to 6
- patch_weight: bfloat16 [768, 1280], replicated, may hold values from -0.21875 to 0.21875
- layer_gain: float32 [1280], replicated, may hold values from 0.5 to 2
- up_weight: bfloat16 [1280, 2560], replicated, may hold values from -0.15625 to 0.15625
- down_weight: bfloat16 [2560, 1280], replicated, may hold values from -0.125 to 0.125
- head_weight: bfloat16 [1280, 272], replicated, may hold values from -0.15625 to 0.15625
Outputs:
- feature_grad: bfloat16 [128, 128, 128, 128], P('tm', 'tile')
Inputs may be any that keep to these rules, and one draw needn't show every extreme that they name: `observed_frames`: slot j of pose device d in block g is used when j < observed_counts[g, d]; the used slots of one block name 32 different frames; unused slots hold 0. `observed_counts`: the counts of one block sum to 32; in every block some device holds 3.
All inputs are finite; a program needn't handle non-finite values. No bound on the sum of `key_visible` on one device may be relied on, other than what follows from the above.
Results may differ from a plain program's by a relative error of at most 0.015.
Values may be sent and summed in bfloat16 or wider, within the bound.
No kernel may reach another device: no remote copies, remote signals or barrier semaphores. Data moves between devices by JAX's collectives and lax.ppermute only.
A program may use at most 128 MiB of HBM per device.

v0:
```python
import jax
import jax.numpy as jnp
from jax import lax
from jax.sharding import PartitionSpec as P

PATCH = 16


norm_eps = 1e-06
spread_sq = 8.0


def shifted(value, axis, steps):
    count = lax.axis_size(axis)
    first, last = (max(0, -steps), min(count, count - steps))
    return lax.ppermute(value, axis, [(source, source + steps) for source in range(first, last)])


def extended_2(x, sides, width):
    for axis, dim in sides:
        size, length = (lax.axis_size(axis), x.shape[dim])
        up = [(i, (i + 1) % size) for i in range(size - 1)]
        down = [(j, i) for i, j in up]
        last = lax.slice_in_dim(x, length - width, length, axis=dim)
        first = lax.slice_in_dim(x, 0, width, axis=dim)
        before = lax.ppermute(last, axis, up)
        after = lax.ppermute(first, axis, down)
        x = jnp.concatenate([before, x, after], axis=dim)
    return x


def decoder_norm(features, norm_gain):
    widened = features.astype(jnp.float32)
    rescale = lax.rsqrt(jnp.mean(widened * widened, axis=-1, keepdims=True) + norm_eps)
    normed = widened * rescale
    return (normed, rescale, normed * norm_gain)


def silu_slope(preact):
    sigmoid = jax.nn.sigmoid(preact)
    return sigmoid * (1.0 + preact * (1.0 - sigmoid))


def gelu_slope(preact):
    return (
        0.5 * (1.0 + lax.erf(preact * 0.7071067811865476))
        + preact * jnp.exp(-0.5 * preact * preact) * 0.3989422804014327
    )


def tap_sum(partial_value, frame_count, row_count, column_count):
    summed = jnp.zeros((frame_count, row_count, column_count, 3), jnp.float32)
    for t_shift in range(3):
        for r_shift in range(3):
            for c_shift in range(3):
                tap_index = (t_shift * 3 + r_shift) * 3 + c_shift
                summed = (
                    summed
                    + partial_value[
                        t_shift : t_shift + frame_count,
                        r_shift : r_shift + row_count,
                        c_shift : c_shift + column_count,
                        3 * tap_index : 3 * tap_index + 3,
                    ]
                )
    return summed


def tap_columns(padded, frame_count, row_count, column_count):
    pieces = []
    for t_shift in range(3):
        for r_shift in range(3):
            for c_shift in range(3):
                pieces.append(
                    padded[
                        2 - t_shift : 2 - t_shift + frame_count,
                        2 - r_shift : 2 - r_shift + row_count,
                        2 - c_shift : 2 - c_shift + column_count,
                        :,
                    ]
                )
    return jnp.concatenate(pieces, axis=-1)


def spread_keys(table, keypoint_ids, key_total):
    selector = (jnp.arange(key_total, dtype=jnp.int32)[:, None] == keypoint_ids[None, :]).astype(
        jnp.float32
    )
    return jnp.dot(table.astype(jnp.float32), selector, precision=lax.Precision.HIGHEST)


def pick_integers(table, picker):
    return jnp.sum(jnp.where(picker[:, :, None], table[None, :, :], 0), axis=1)


def pose_grad(
    images,
    key_rows,
    key_columns,
    key_visible,
    weight,
    position_table,
    patch_weight,
    layer_gain,
    up_weight,
    down_weight,
    head_weight,
):
    frame_total, height, width, _ = images.shape
    grid_rows = height // PATCH
    grid_cols = width // PATCH
    token_total = grid_rows * grid_cols
    sub_size = PATCH // 4
    key_total = key_rows.shape[1]
    head_total = head_weight.shape[1]
    model_width = patch_weight.shape[1]
    patches = (
        images.reshape(frame_total, grid_rows, PATCH, grid_cols, PATCH, 3)
        .transpose(0, 1, 3, 2, 4, 5)
        .reshape(frame_total * token_total, PATCH * PATCH * 3)
    )
    embedded = jnp.dot(patches, patch_weight, preferred_element_type=jnp.float32).reshape(
        frame_total, token_total, model_width
    ) + position_table.astype(jnp.float32)
    centred = embedded - jnp.mean(embedded, axis=-1, keepdims=True)
    inverse = lax.rsqrt(jnp.mean(centred * centred, axis=-1, keepdims=True) + norm_eps)
    unit_rows = centred * inverse
    normed_tokens = (unit_rows * layer_gain).astype(jnp.bfloat16).reshape(-1, model_width)
    hidden_pre = jnp.dot(normed_tokens, up_weight, preferred_element_type=jnp.float32)
    hidden = jax.nn.gelu(hidden_pre, approximate=False).astype(jnp.bfloat16)
    block_out = embedded.reshape(-1, model_width) + jnp.dot(
        hidden, down_weight, preferred_element_type=jnp.float32
    )
    heatmap = jnp.dot(
        block_out.astype(jnp.bfloat16), head_weight, preferred_element_type=jnp.float32
    ).reshape(frame_total, token_total, head_total)
    token_ids = jnp.arange(token_total, dtype=jnp.int32)
    column_ids = jnp.arange(head_total, dtype=jnp.int32)
    keypoint_ids = column_ids % key_total
    pixel_rows = (
        (token_ids // grid_cols)[:, None] * sub_size
        + (column_ids // (sub_size * key_total))[None, :]
    ).astype(jnp.float32)
    pixel_cols = (
        (token_ids % grid_cols)[:, None] * sub_size + (column_ids // key_total % sub_size)[None, :]
    ).astype(jnp.float32)
    row_goal = spread_keys(key_rows, keypoint_ids, key_total)
    col_goal = spread_keys(key_columns, keypoint_ids, key_total)
    row_gap = pixel_rows[None, :, :] - row_goal[:, None, :]
    col_gap = pixel_cols[None, :, :] - col_goal[:, None, :]
    target = jnp.exp(-(row_gap * row_gap + col_gap * col_gap) / spread_sq)
    loss_mask = spread_keys(key_visible, keypoint_ids, key_total) * weight[:, None]
    heat_grad = (
        ((heatmap - target) * loss_mask[:, None, :]).astype(jnp.bfloat16).reshape(-1, head_total)
    )
    out_grad = jnp.dot(heat_grad, head_weight.T, preferred_element_type=jnp.float32)
    hidden_grad = jnp.dot(
        out_grad.astype(jnp.bfloat16), down_weight.T, preferred_element_type=jnp.float32
    )
    pre_grad = (hidden_grad * gelu_slope(hidden_pre)).astype(jnp.bfloat16)
    normed_grad = jnp.dot(pre_grad, up_weight.T, preferred_element_type=jnp.float32).reshape(
        frame_total, token_total, model_width
    )
    unit_grad = normed_grad * layer_gain
    embed_grad = out_grad.reshape(frame_total, token_total, model_width) + inverse * (
        unit_grad
        - jnp.mean(unit_grad, axis=-1, keepdims=True)
        - unit_rows * jnp.mean(unit_grad * unit_rows, axis=-1, keepdims=True)
    )
    colour_grad = jnp.dot(
        embed_grad.astype(jnp.bfloat16).reshape(-1, model_width),
        patch_weight.T,
        preferred_element_type=jnp.float32,
    ).astype(jnp.bfloat16)
    return (
        colour_grad.reshape(frame_total, grid_rows, grid_cols, PATCH, PATCH, 3)
        .transpose(0, 1, 3, 2, 4, 5)
        .reshape(frame_total, height, width, 3)
    )


def per_device(
    features,
    norm_gain,
    conv_weight,
    colour_bias,
    observed_frames,
    observed_counts,
    key_rows,
    key_columns,
    key_visible,
    position_table,
    patch_weight,
    layer_gain,
    up_weight,
    down_weight,
    head_weight,
):
    frame_count, row_count, column_count, channels = features.shape
    tile_count = lax.axis_size("tile")
    own_index = lax.axis_index("tile")
    normed, rescale, preact = decoder_norm(features, norm_gain)
    activated = jax.nn.silu(preact).astype(jnp.bfloat16)
    prior_rims = shifted(activated[frame_count - 2 :], "tm", 1)
    extended = jnp.concatenate((prior_rims, activated), axis=0)
    extended = extended_2(extended, (("tile", 1),), 1)
    partial_value = jnp.dot(
        extended.reshape(-1, channels), conv_weight, preferred_element_type=jnp.float32
    )
    partial_value = partial_value.reshape(frame_count + 2, row_count + 2, column_count, 81)
    partial_value = jnp.pad(partial_value, ((0, 0), (0, 0), (1, 1), (0, 0)))
    colour_sums = tap_sum(partial_value, frame_count, row_count, column_count)
    colours = (colour_sums + colour_bias).astype(jnp.bfloat16)
    strips = colours.reshape(frame_count, -1)
    listing = observed_frames[0]
    counts = observed_counts[0]
    slot_ids = jnp.arange(listing.shape[1], dtype=jnp.int32)
    in_use = slot_ids[None, :] < counts[:, None]
    slot_total = listing.shape[1]
    own_frames = lax.dynamic_index_in_dim(listing, own_index, 0, keepdims=False)
    own_live = lax.dynamic_index_in_dim(in_use, own_index, 0, keepdims=False)
    frame_ids = jnp.arange(frame_count, dtype=jnp.int32)
    own_picker = own_frames[:, None] == frame_ids[None, :]
    everything = lax.all_gather(strips, "tile", axis=1, tiled=True)
    arrived = jnp.dot(
        own_picker.astype(jnp.bfloat16), everything, preferred_element_type=jnp.float32
    ).astype(jnp.bfloat16)
    images = arrived.reshape(slot_total, tile_count * row_count, column_count, 3)
    own_rows = pick_integers(key_rows, own_picker)
    own_columns = pick_integers(key_columns, own_picker)
    own_visible = pick_integers(key_visible, own_picker)
    colour_grad = pose_grad(
        images,
        own_rows,
        own_columns,
        own_visible,
        own_live.astype(jnp.float32),
        position_table,
        patch_weight,
        layer_gain,
        up_weight,
        down_weight,
        head_weight,
    )
    grad_rows = colour_grad.reshape(slot_total, tile_count, -1)
    matches = own_picker & own_live[:, None]
    spread = jnp.dot(
        matches.T.astype(jnp.bfloat16),
        grad_rows.reshape(slot_total, -1),
        preferred_element_type=jnp.float32,
    )
    strip_grad = lax.psum_scatter(
        spread.astype(jnp.bfloat16), "tile", scatter_dimension=1, tiled=True
    )
    strip_colours = strip_grad.reshape(frame_count, row_count, column_count * 3)
    later_rims = shifted(strip_colours[:2], "tm", -1)
    grad_ext = jnp.concatenate((strip_colours, later_rims), axis=0)
    grad_ext = extended_2(grad_ext, (("tile", 1),), 1)
    grad_ext = grad_ext.reshape(frame_count + 2, row_count + 2, column_count, 3)
    grad_ext = jnp.pad(grad_ext, ((0, 0), (0, 0), (1, 1), (0, 0)))
    columns = tap_columns(grad_ext, frame_count, row_count, column_count).reshape(-1, 81)
    activated_grad = jnp.dot(columns, conv_weight.T, preferred_element_type=jnp.float32).reshape(
        frame_count, row_count, column_count, channels
    )
    scaled = activated_grad * silu_slope(preact) * norm_gain
    feature_grad = rescale * (scaled - normed * jnp.mean(scaled * normed, axis=-1, keepdims=True))
    return feature_grad.astype(jnp.bfloat16)


def solution(mesh):
    in_specs = (
        P("tm", "tile", None, None),
        P(),
        P(),
        P(),
        P("tm", None, None),
        P("tm", None),
        P("tm", None),
        P("tm", None),
        P("tm", None),
        P(),
        P(),
        P(),
        P(),
        P(),
        P(),
    )
    out_specs = P("tm", "tile", None, None)
    return jax.shard_map(
        per_device, mesh=mesh, in_specs=in_specs, out_specs=out_specs, check_vma=False
    )
```

profile of v0, /device:TPU:1, one launch (start us, length us, event | category | flops | bytes accessed | tf_op | source)
XLA Modules:
  0.0 493.0 jit_solution(14147421178952931342)
XLA Ops:
  6.5 4.6 fusion.18
  14.5 4.0 collective-permute-start
  18.4 4.9 %collective-permute-done = bf16[2,4,128,128]{3,2,1,0:T(8,128)(2,1)S(1)} collective-permute-done((bf16[2,4,128,128]{3,2,1,0:T(8,128)(2,1)S(1)}, bf16[2,4,128,128]{3,2,1,0:T(8,128)(2,1)S(1)}, u32[]{:S(2)}, u32[]{:S(2)}) %collective-permute-start) | collective-permute-done | bytes 262176 | tf_op jit(solution)/shard_map/ppermute | solution.py:16
  23.6 5.0 %collective-permute-start.1 = (bf16[34,1,128,128]{3,2,1,0:T(8,128)(2,1)S(1)}, bf16[34,1,128,128]{3,2,1,0:T(8,128)(2,1)S(1)}, u32[]{:S(2)}, u32[]{:S(2)}) collective-permute-start(bf16[34,1,128,128]{3,2,1,0:T(8,128)(2,1)S(1)} %get-tuple-element.8), channel_id=1, source_target_pairs={{0,4},{4,8},{8,12},{12,16},{16,20},{20,24},{24,28},{28,32},{32,36}... | collective-permute-start | bytes 3342344 | tf_op jit(solution)/shard_map/ppermute | solution.py:26
  30.5 10.5 %collective-permute-done.1 = bf16[34,1,128,128]{3,2,1,0:T(8,128)(2,1)S(1)} collective-permute-done((bf16[34,1,128,128]{3,2,1,0:T(8,128)(2,1)S(1)}, bf16[34,1,128,128]{3,2,1,0:T(8,128)(2,1)S(1)}, u32[]{:S(2)}, u32[]{:S(2)}) %collective-permute-start.1) | collective-permute-done | bytes 1114144 | tf_op jit(solution)/shard_map/ppermute | solution.py:26
  41.0 4.4 collective-permute-done.2
  45.4 4.2 fusion.19
  60.3 59.8 %all-gather.2.cloned.1.call-done = bf16[32,49152]{0,1:T(8,128)(2,1)} async-done(((bf16[32,1536]{0,1:T(8,128)(2,1)}), bf16[32,49152]{0,1:T(8,128)(2,1)}) %all-gather.2.cloned.1.call-update) | async-done | bytes 3145744 | tf_op jit(solution)/shard_map/all_gather | solution.py:224
  120.1 8.0 %convolution_convert_fusion.1 = bf16[3,49152]{1,0:T(4,128)(2,1)S(1)} fusion(bf16[32,49152]{0,1:T(8,128)(2,1)} %all-gather.2.cloned.1.call-done, s32[3]{0:T(128)S(1)} %dynamic-slice_reduce_fusion), kind=kOutput, calls=%fused_computation.19 | convolution fusion | flops 9584736 | bytes 3440652 | tf_op jit(solution)/shard_map/dot_general | solution.py:225
  128.0 33.2 %reshape_reshape.3 = bf16[3,8,16,8,16,3]{5,4,3,2,1,0:T(8,128)(2,1)} reshape(bf16[3,49152]{1,0:T(4,128)(2,1)S(1)} %convolution_convert_fusion.1) | data formatting | bytes 589824 | tf_op jit(solution)/shard_map/reshape;reshape | solution.py:118
  161.2 39.8 %copy.94 = bf16[3,8,8,16,16,3]{2,1,5,4,3,0:T(8,128)(2,1)} copy(bf16[3,8,8,16,16,3]{5,4,2,3,1,0:T(8,128)(2,1)} %bitcast.54) | data formatting | bytes 589824 | tf_op jit(solution)/shard_map/transpose | solution.py:119
  201.1 5.7 %dot_general.49 = bf16[3,64,768]{1,2,0:T(8,128)(2,1)S(1)} reshape(bf16[3,8,8,16,16,3]{2,1,5,4,3,0:T(8,128)(2,1)} %copy.94) | data formatting | bytes 589824 | tf_op jit(solution)/shard_map/dot_general | solution.py:122
  208.9 4.5 fusion.170
  214.8 7.1 %fusion.28 = bf16[192,1280]{1,0:T(8,128)(2,1)} fusion(f32[192,1280]{1,0:T(8,128)S(1)} %bitcast.55, bf16[2560,1280]{1,0:T(8,128)(2,1)S(1)} %bitcast.65, f32[192,2560]{1,0:T(8,128)S(1)} %fusion.170), kind=kOutput, calls=%fused_computation.55 | convolution fusion | flops 1290731520 | bytes 9994240 | tf_op jit(solution)/shard_map/dot_general | solution.py:131
  221.9 3.6 fusion.46
  225.5 10.8 %multiply_reduce_fusion.1 = (f32[192]{0:T(256)S(1)}, f32[192,1280]{1,0:T(8,128)}) fusion(f32[1280]{0:T(1024)S(1)} %copy-done.9, bf16[1280,2560]{1,0:T(8,128)(2,1)} %param.27, bf16[2560,1280]{1,0:T(8,128)(2,1)} %param.28, f32[192,2560]{1,0:T(8,128)} %copy-done.3, f32[192,1280]{1,0:T(8,128)} %fusion.46), kind=kOutput, calls=%fused_computation.89 | convolution fusion | flops 2522234624 | bytes 17045248 | tf_op jit(solution)/shard_map/dot_general | solution.py:161
  240.7 4.7 reshape.266
  245.4 39.3 %copy.99 = bf16[3,8,16,8,16,3]{5,4,3,2,1,0:T(8,128)(2,1)} copy(bf16[3,8,16,8,16,3]{3,1,0,5,4,2:T(8,128)(2,1)} %bitcast.56) | data formatting | bytes 589824 | tf_op jit(solution)/shard_map/transpose | solution.py:177
  284.7 32.3 %reshape_reshape_reshape.3 = bf16[3,49152]{1,0:T(4,128)(2,1)S(1)} reshape(bf16[3,8,16,8,16,3]{5,4,3,2,1,0:T(8,128)(2,1)} %copy.99) | data formatting | bytes 589824 | tf_op jit(solution)/shard_map/reshape;reshape;reshape | solution.py:249
  319.9 78.1 %reduce-scatter.2.cloned.1.call-done = bf16[32,1536]{1,0:T(8,128)(2,1)} async-done(((bf16[32,49152]{1,0:T(8,128)(2,1)}), bf16[32,1536]{1,0:T(8,128)(2,1)}) %reduce-scatter.2.cloned.1.call-update) | async-done | bytes 98320 | tf_op jit(solution)/shard_map/reduce_scatter | solution.py:252
  403.2 6.1 %collective-permute-start.4 = (bf16[34,1,384]{2,1,0:T(2,128)(2,1)S(1)}, bf16[34,1,384]{2,1,0:T(2,128)(2,1)S(1)}, u32[]{:S(2)}, u32[]{:S(2)}) collective-permute-start(bf16[34,1,384]{2,1,0:T(2,128)(2,1)S(1)} %get-tuple-element.37), channel_id=1, source_target_pairs={{0,4},{4,8},{8,12},{12,16},{16,20},{20,24},{24,28},{28,32},{32,36}... | collective-permute-start | bytes 78344 | tf_op jit(solution)/shard_map/ppermute | solution.py:26
  419.8 51.6 %concatenate.19 = bf16[32,4,128,81]{2,3,1,0:T(8,128)(2,1)} concatenate(bf16[32,4,128,3]{2,3,1,0:T(4,128)(2,1)} %get-tuple-element.36, bf16[32,4,128,3]{2,3,1,0:T(4,128)(2,1)} %get-tuple-element.35, bf16[32,4,128,3]{2,3,1,0:T(4,128)(2,1)S(1)} %get-tuple-element.11, bf16[32,4,128,3]{2,3,1,0:T(4,128)(2,1)S(1)} %get-tuple-element.12, bf16[32,4,128,3]{2,3,1,0:T(4,128)(2,1)} %get-tuple-element.34, ...), dimensions={3} | concatenate | bytes 5308416 | tf_op jit(solution)/shard_map/concatenate | solution.py:82
  471.4 8.5 %fusion.14 = (f32[32,4,128]{2,1,0:T(4,128)S(1)}, f32[32,4,128,128]{3,2,1,0:T(8,128)S(1)}) fusion(bf16[32,4,128,128]{3,2,1,0:T(8,128)(2,1)} %param.15, f32[32,4,128]{2,1,0:T(4,128)S(1)} %copy-done.7, f32[128]{0:T(128)S(1)} %copy-done.15, bf16[32,4,128,81]{2,3,1,0:T(8,128)(2,1)} %concatenate.19, bf16[128,81]{0,1:T(8,128)(2,1)S(1)} %copy-done.18), kind=kOutput, calls=%fused_computation.36 | convolution fusion | flops 369082368 | bytes 15389440 | tf_op jit(solution)/shard_map/dot_general | solution.py:262
  479.9 5.8 %fusion.17 = bf16[32,4,128,128]{3,2,1,0:T(8,128)(2,1)} fusion(f32[32,4,128,128]{3,2,1,0:T(8,128)S(1)} %get-tuple-element.44, bf16[32,4,128,128]{3,2,1,0:T(8,128)(2,1)S(1)} %copy-done.2, f32[32,4,128]{2,1,0:T(4,128)S(1)} %broadcast_multiply_fusion, f32[32,4,128]{2,1,0:T(4,128)S(1)} %copy-done.7), kind=kLoop, calls=%fused_computation.39 | loop fusion | flops 12582912 | bytes 16908288 | tf_op jit(solution)/shard_map/convert_element_type | solution.py:267
  (107 shorter events, 42.2 us)
Async XLA Ops:
  6.5 200.2 %copy-start = (bf16[768,1280]{1,0:T(8,128)(2,1)S(1)}, bf16[768,1280]{1,0:T(8,128)(2,1)}, u32[]{:S(2)}) copy-start(bf16[768,1280]{1,0:T(8,128)(2,1)} %param.25) | copy-start | bytes 5898244
  6.5 4.6 copy-start.15
  6.5 113.5 %all-gather.2.cloned.1.call-start = ((), (), s32[]{:S(2)}) async-start(), calls=%async_computation.1 | async-start | bytes 12976128 | tf_op jit(solution)/shard_map/all_gather | solution.py:224
  6.5 4.6 copy-start.1
  11.2 3.2 copy-start.6
  14.4 30.9 %copy-start.17 = (bf16[128,81]{0,1:T(8,128)(2,1)S(1)}, bf16[128,81]{0,1:T(8,128)(2,1)}, u32[]{:S(2)}) copy-start(bf16[128,81]{0,1:T(8,128)(2,1)} %param.17) | copy-start | bytes 62212
  14.5 8.9 %collective-permute-start = (bf16[2,4,128,128]{3,2,1,0:T(8,128)(2,1)S(1)}, bf16[2,4,128,128]{3,2,1,0:T(8,128)(2,1)S(1)}, u32[]{:S(2)}, u32[]{:S(2)}) collective-permute-start(bf16[2,4,128,128]{3,2,1,0:T(8,128)(2,1)S(1)} %slice.262), channel_id=1, source_target_pairs={{0,1},{1,2},{2,3},{4,5},{5,6},{6,7},{8,9},{9,10},{10,11},{12,13},{... | collective-permute-start | bytes 786440 | tf_op jit(solution)/shard_map/ppermute | solution.py:16
  23.6 17.4 %collective-permute-start.1 = (bf16[34,1,128,128]{3,2,1,0:T(8,128)(2,1)S(1)}, bf16[34,1,128,128]{3,2,1,0:T(8,128)(2,1)S(1)}, u32[]{:S(2)}, u32[]{:S(2)}) collective-permute-start(bf16[34,1,128,128]{3,2,1,0:T(8,128)(2,1)S(1)} %get-tuple-element.8), channel_id=1, source_target_pairs={{0,4},{4,8},{8,12},{12,16},{16,20},{20,24},{24,28},{28,32},{32,36}... | collective-permute-start | bytes 3342344 | tf_op jit(solution)/shard_map/ppermute | solution.py:26
  28.5 21.0 %copy-start.14 = (f32[3]{0:T(128)S(1)}, f32[3]{0:T(128)}, u32[]{:S(2)}) copy-start(f32[3]{0:T(128)} %param.18) | copy-start | bytes 40
  28.6 16.8 %collective-permute-start.2 = (bf16[34,1,128,128]{3,2,1,0:T(8,128)(2,1)S(1)}, bf16[34,1,128,128]{3,2,1,0:T(8,128)(2,1)S(1)}, u32[]{:S(2)}, u32[]{:S(2)}) collective-permute-start(bf16[34,1,128,128]{3,2,1,0:T(8,128)(2,1)S(1)} %get-tuple-element.9), channel_id=1, source_target_pairs={{4,0},{8,4},{12,8},{16,12},{20,16},{24,20},{28,24},{32,28},{36,32}... | collective-permute-start | bytes 3342344 | tf_op jit(solution)/shard_map/ppermute | solution.py:27
  52.1 2.8 copy-start.10
  52.1 5.2 %copy-start.19 = (s32[1,32]{1,0:T(1,128)S(1)}, s32[1,32]{1,0:T(1,128)}, u32[]{:S(2)}) copy-start(s32[1,32]{1,0:T(1,128)} %param.20) | copy-start | bytes 388
  53.5 344.4 %reduce-scatter.2.cloned.1.call-start = ((), (), s32[]{:S(2)}) async-start(), calls=%async_computation.2 | async-start | bytes 3244032 | tf_op jit(solution)/shard_map/reduce_scatter | solution.py:252
  208.4 6.3 %slice-start = ((s8[6553600]{0:T(1024)(128)(4,1)}), s8[4194304]{0:T(1024)(128)(4,1)S(1)}, s32[]{:S(2)}) async-start(s8[6553600]{0:T(1024)(128)(4,1)} %bitcast.64), calls=%async_computation.3 | async-start | bytes 8388608
  208.9 5.8 %slice-start.1 = ((s8[6553600]{0:T(1024)(128)(4,1)}), s8[2359296]{0:T(1024)(128)(4,1)S(1)}, s32[]{:S(2)}) async-start(s8[6553600]{0:T(1024)(128)(4,1)} %bitcast.64), calls=%async_computation.4 | async-start | bytes 4718592
  214.8 7.1 %copy-start.4 = (f32[192,272]{0,1:T(8,128)S(1)}, f32[192,272]{0,1:T(8,128)}, u32[]{:S(2)}) copy-start(f32[192,272]{0,1:T(8,128)} %copy.96) | copy-start | bytes 626692
  214.8 7.2 %copy-start.5 = (f32[192,272]{0,1:T(8,128)S(1)}, f32[192,272]{0,1:T(8,128)}, u32[]{:S(2)}) copy-start(f32[192,272]{0,1:T(8,128)} %copy.97) | copy-start | bytes 626692
  284.7 32.3 %copy-start.16 = (pred[3]{0:T(512)(128)(4,1)S(1)}, pred[3]{0:T(512)(128)(4,1)}, u32[]{:S(2)}) copy-start(pred[3]{0:T(512)(128)(4,1)} %get-tuple-element.45) | copy-start | bytes 13
  398.7 4.4 collective-permute-start.3
  403.2 8.1 %collective-permute-start.4 = (bf16[34,1,384]{2,1,0:T(2,128)(2,1)S(1)}, bf16[34,1,384]{2,1,0:T(2,128)(2,1)S(1)}, u32[]{:S(2)}, u32[]{:S(2)}) collective-permute-start(bf16[34,1,384]{2,1,0:T(2,128)(2,1)S(1)} %get-tuple-element.37), channel_id=1, source_target_pairs={{0,4},{4,8},{8,12},{12,16},{16,20},{20,24},{24,28},{28,32},{32,36}... | collective-permute-start | bytes 78344 | tf_op jit(solution)/shard_map/ppermute | solution.py:26
  409.3 5.4 %collective-permute-start.5 = (bf16[34,1,384]{2,1,0:T(2,128)(2,1)S(1)}, bf16[34,1,384]{2,1,0:T(2,128)(2,1)S(1)}, u32[]{:S(2)}, u32[]{:S(2)}) collective-permute-start(bf16[34,1,384]{2,1,0:T(2,128)(2,1)S(1)} %get-tuple-element.38), channel_id=1, source_target_pairs={{4,0},{8,4},{12,8},{16,12},{20,16},{24,20},{28,24},{32,28},{36,32}... | collective-permute-start | bytes 78344 | tf_op jit(solution)/shard_map/ppermute | solution.py:27
  419.8 51.7 %copy-start.7 = (f32[32,4,128]{2,1,0:T(4,128)S(1)}, f32[32,4,128]{2,1,0:T(4,128)}, u32[]{:S(2)}) copy-start(f32[32,4,128]{2,1,0:T(4,128)} %copy-done.6) | copy-start | bytes 196612
  419.8 51.7 %copy-start.18 = (bf16[128,81]{0,1:T(8,128)(2,1)S(1)}, bf16[128,81]{0,1:T(8,128)(2,1)}, u32[]{:S(2)}) copy-start(bf16[128,81]{0,1:T(8,128)(2,1)} %param.17) | copy-start | bytes 62212
  471.4 8.5 %copy-start.2 = (bf16[32,4,128,128]{3,2,1,0:T(8,128)(2,1)S(1)}, bf16[32,4,128,128]{3,2,1,0:T(8,128)(2,1)}, u32[]{:S(2)}) copy-start(bf16[32,4,128,128]{3,2,1,0:T(8,128)(2,1)} %param.15) | copy-start | bytes 12582916
  (6 other events, 13.0 us)
Sparse Core Ops, SparseCore 0:
  53.7 66.3 all-gather.1
  320.0 77.9 reduce-scatter.1
where the time goes:
time: 503 us; the launch traced here: 493 us
  local copies, waits for them, and re-layouts  219 us (44%)
  waiting for transfers between devices  163 us (32%)
  matrix products  52.4 us (10%)
  other arithmetic  23.6 us (5%)
  starting transfers between devices  20.4 us (4%)
  between operations  14.3 us (3%)
    reduce_scatter x1, waiting for transfers between devices, per_device(): lax.psum_scatter(spread.astype(jnp.bfloat16), 'tile', scatter_dimension=1...  78.1 us
    all_gather x1, waiting for transfers between devices, per_device(): everything = lax.all_gather(strips, 'tile', axis=1, tiled=True)  59.8 us
    concatenate x1, local copies, waits for them, and re-layouts, tap_columns(): return jnp.concatenate(pieces, axis=-1)  51.6 us
    transpose x1, local copies, waits for them, and re-layouts, pose_grad(): patches = images.reshape(frame_total, grid_rows, PATCH, grid_cols, PATCH,...  39.8 us
    transpose x1, local copies, waits for them, and re-layouts, pose_grad(): return colour_grad.reshape(frame_total, grid_rows, grid_cols, PATCH, PATC...  39.3 us
    another operation x1, local copies, waits for them, and re-layouts, pose_grad(): images.reshape(frame_total, grid_rows, PATCH, grid_cols, PATCH, 3)  33.2 us
    another operation x1, local copies, waits for them, and re-layouts, per_device(): grad_rows.reshape(slot_total, -1)  32.3 us
    ppermute x2, starting transfers between devices, extended_2(): before = lax.ppermute(last, axis, up)  11.1 us
  transfers between devices with their start and end apart: 8, of which 7 were waited for; matrix products, arithmetic and copies ran while one was open for 2% of the time, Pallas kernels for 0%

commit v1 on v0

v1 whole, which is shorter than its diff:
```python
import functools

import jax
import jax.numpy as jnp
import ml_dtypes
import numpy as np
from jax import lax
from jax.experimental import pallas as pl
from jax.experimental.pallas import tpu as pltpu
from jax.sharding import PartitionSpec as P

CH = 128
DP = 1280
HID = 2560
PATCH = 16
KP = 17
HEAD = 272
COLS = 128
ROWS = 4
NORM_EPS = 1e-06
F32 = jnp.float32
BF16 = jnp.bfloat16


def slot_of(c, o, k):
    group = 3 * c + o
    if group < 8:
        return 8 * group + k
    return 8 * (k // 2) + 6 + k % 2


def make_selector():
    table = np.zeros((81, 2, ROWS, 256), np.float32)
    for tau in range(2):
        for r in range(ROWS):
            for f in range(4):
                a = tau + 2 - f
                if not 0 <= a <= 2:
                    continue
                for k in range(6):
                    b = r + 2 - k
                    if not 0 <= b <= 2:
                        continue
                    for c in range(3):
                        for o in range(3):
                            table[3 * (9 * a + 3 * b + c) + o, tau, r, 64 * f + slot_of(c, o, k)] = 1
    return table.reshape(81, 2048)


def make_pixel_order():
    table = np.zeros((768, 768), np.float32)
    for o in range(3):
        for pixel in range(256):
            table[256 * o + pixel, 3 * pixel + o] = 1
    return table


def make_key_spread():
    table = np.zeros((KP, HEAD), np.float32)
    table[np.arange(HEAD) % KP, np.arange(HEAD)] = 1
    return table


SELECTOR = make_selector().astype(ml_dtypes.bfloat16)
SELECTOR_T = np.ascontiguousarray(make_selector().T).astype(ml_dtypes.bfloat16)
PIXEL_ORDER = make_pixel_order().astype(ml_dtypes.bfloat16)
PIXEL_ORDER_T = np.ascontiguousarray(make_pixel_order().T).astype(ml_dtypes.bfloat16)
KEY_SPREAD = make_key_spread().astype(ml_dtypes.bfloat16)
MEAN_PAIR = (np.kron(np.eye(2), np.ones((CH, CH))) / CH).astype(ml_dtypes.bfloat16)


def dot(a, b):
    return jnp.dot(a, b, preferred_element_type=F32)


def dot_nt(a, b):
    return lax.dot_general(a, b, (((1,), (1,)), ((), ())), preferred_element_type=F32)


def roll(x, shift, axis):
    shift %= x.shape[axis]
    return pltpu.roll(x, shift, axis) if shift else x


def channel_mean(first, second, mean_pair):
    both = jnp.concatenate([first.astype(BF16), second.astype(BF16)], axis=1)
    means = dot(both, mean_pair)
    return means[:, :CH], means[:, CH:]


def lanes_of(shape):
    return lax.broadcasted_iota(jnp.int32, shape, len(shape) - 1)


def sublanes_of(shape):
    return lax.broadcasted_iota(jnp.int32, shape, len(shape) - 2)


def from_left(x):
    return jnp.where(lanes_of(x.shape) >= 1, roll(x, 1, x.ndim - 1), 0.0)


def from_right(x):
    return jnp.where(lanes_of(x.shape) < COLS - 1, roll(x, -1, x.ndim - 1), 0.0)


def activated_rows(feat_ref, frame, half_gain, mean_pair):
    acts = []
    for pair in range(ROWS // 2):
        xs = [feat_ref[frame, 2 * pair + i].astype(F32) for i in range(2)]
        means = channel_mean(xs[0] * xs[0], xs[1] * xs[1], mean_pair)
        for x, mean in zip(xs, means):
            half = x * lax.rsqrt(mean + NORM_EPS) * half_gain
            acts.append((half + half * jnp.tanh(half)).astype(BF16))
    return acts


def frame_sums(taps, out_ref, frame):
    groups = [taps[8 * g : 8 * g + 8] for g in range(8)]
    row = sublanes_of((8, COLS))
    groups.append(
        jnp.where(
            row < 2,
            roll(groups[0], 2, 0),
            jnp.where(row < 4, roll(groups[1], 4, 0), roll(groups[2], 6, 0)),
        )
    )
    for o in range(3):
        out_ref[frame, o] = from_left(groups[o]) + groups[3 + o] + from_right(groups[6 + o])


def spread_weights(conv_ref, sel_ref, weight_scr):
    conv = conv_ref[...]
    for block in range(8):
        weight_scr[CH * block : CH * block + CH, :] = dot(
            conv, sel_ref[:, 256 * block : 256 * block + 256]
        ).astype(BF16)


def conv_kernel(feat_ref, gain_ref, mean_ref, conv_ref, sel_ref, out_ref, weight_scr, carry):
    @pl.when(pl.program_id(0) == 0)
    def _():
        spread_weights(conv_ref, sel_ref, weight_scr)
        carry[...] = jnp.zeros_like(carry)

    half_gain = 0.5 * gain_ref[...]
    mean_pair = mean_ref[...]
    for pair in range(feat_ref.shape[0] // 2):
        acts = []
        for tau in range(2):
            acts += activated_rows(feat_ref, 2 * pair + tau, half_gain, mean_pair)
        sums = dot(jnp.concatenate(acts, axis=1), weight_scr[...])
        taps = (sums[:, :128] + carry[...]).T
        carry[...] = sums[:, 128:]
        for f in range(2):
            frame_sums(taps[64 * f : 64 * f + 64], out_ref, 2 * pair + f)


def tail_kernel(feat_ref, gain_ref, mean_ref, conv_ref, sel_ref, out_ref, weight_scr):
    spread_weights(conv_ref, sel_ref, weight_scr)
    half_gain = 0.5 * gain_ref[...]
    mean_pair = mean_ref[...]
    acts = []
    for tau in range(2):
        acts += activated_rows(feat_ref, tau, half_gain, mean_pair)
    taps = dot(jnp.concatenate(acts, axis=1), weight_scr[:, 128:]).T
    for f in range(2):
        frame_sums(taps[64 * f : 64 * f + 64], out_ref, f)


def whole(shape):
    return pl.BlockSpec(shape, lambda *_: (0,) * len(shape))


def conv_forward(features, gain, conv_weight, block):
    frames = features.shape[0]
    common = [whole((1, CH)), whole((256, 256)), whole((CH, 81)), whole((81, 2048))]
    consts = (gain, jnp.asarray(MEAN_PAIR), conv_weight, jnp.asarray(SELECTOR))
    tail = pl.pallas_call(
        tail_kernel,
        grid=(1,),
        in_specs=[pl.BlockSpec((2, ROWS, COLS, CH), lambda i: (frames // 2 - 1, 0, 0, 0))] + common,
        out_specs=whole((2, 3, 8, COLS)),
        out_shape=jax.ShapeDtypeStruct((2, 3, 8, COLS), F32),
        scratch_shapes=[pltpu.VMEM((1024, 256), BF16)],
        name="conv_tail",
    )(features, *consts)
    main = pl.pallas_call(
        conv_kernel,
        grid=(frames // block,),
        in_specs=[pl.BlockSpec((block, ROWS, COLS, CH), lambda i: (i, 0, 0, 0))] + common,
        out_specs=pl.BlockSpec((block, 3, 8, COLS), lambda i: (i, 0, 0, 0)),
        out_shape=jax.ShapeDtypeStruct((frames, 3, 8, COLS), F32),
        scratch_shapes=[pltpu.VMEM((1024, 256), BF16), pltpu.VMEM((COLS, 128), F32)],
        compiler_params=pltpu.CompilerParams(vmem_limit_bytes=32 * 1024 * 1024),
        cost_estimate=pl.CostEstimate(
            flops=2 * 16384 * 1024, bytes_accessed=5 * 1024 * 1024, transcendentals=2 * 2097152
        ),
        name="conv_main",
    )(features, *consts)
    return tail, main


def swap_blocks(x):
    row, group = sublanes_of(x.shape), lanes_of(x.shape) // 16
    for bit in (4, 2, 1):
        low = (row & bit) == 0
        same = low == ((group & bit) == 0)
        moved = jnp.where(
            low,
            roll(roll(x, -bit, 1), 16 * bit, 2),
            roll(roll(x, bit, 1), -16 * bit, 2),
        )
        x = jnp.where(same, x, moved)
    return x


def gather_patches(x_ref, bias_ref):
    row = sublanes_of((16, 8, COLS))
    zero = jnp.zeros((1, 8, COLS), F32)
    pieces = []
    for o in range(3):
        strips = x_ref[:, o].reshape(16, 2, 8, COLS)
        even = roll(strips[:, 0], -1, 1)
        odd = roll(strips[:, 1], 3, 1)
        even_next = jnp.concatenate([even[1:], zero], axis=0)
        odd_prior = jnp.concatenate([zero, odd[:-1]], axis=0)
        total = (
            jnp.where(row <= 4, even, jnp.where(row == 7, even_next, 0.0))
            + jnp.where(row >= 3, odd, jnp.where(row == 0, odd_prior, 0.0))
            + bias_ref[o]
        )
        blocks = swap_blocks(total).reshape(8, 2, 8, 128)
        for half in range(2):
            pieces.append(blocks[:, half].reshape(64, 128).astype(BF16))
    return jnp.concatenate(pieces, axis=1)


def scatter_patches(grad, out_ref):
    row = sublanes_of((16, 8, COLS))
    zero = jnp.zeros((1, 8, COLS), F32)
    for o in range(3):
        halves = [
            grad[:, 256 * o + 128 * half : 256 * o + 128 * half + 128].reshape(8, 1, 8, 128)
            for half in range(2)
        ]
        rows = swap_blocks(jnp.concatenate(halves, axis=1).reshape(16, 8, 128))
        down = roll(rows, 1, 1)
        up = roll(rows, -3, 1)
        down_prior = jnp.concatenate([zero, down[:-1]], axis=0)
        up_next = jnp.concatenate([up[1:], zero], axis=0)
        even = jnp.where(row == 0, down_prior, down)
        odd = jnp.where(row == 5, up_next, up)
        out_ref[:, o] = jnp.concatenate([even[:, None], odd[:, None]], axis=1).reshape(32, 8, COLS)


def normal_cdf(x):
    return 0.5 * (1.0 + lax.erf(x * 0.7071067811865476))


def pose_kernel(
    own_ref,
    bias_ref,
    x_ref,
    frames_ref,
    counts_ref,
    key_rows_ref,
    key_cols_ref,
    key_vis_ref,
    key_spread_ref,
    gain_ref,
    order_hbm,
    order_t_hbm,
    position_hbm,
    patch_hbm,
    up_hbm,
    down_hbm,
    head_hbm,
    out_ref,
    order,
    order_t,
    position,
    patch,
    up,
    down,
    head,
    hidden_pre,
    hidden,
    pre_grad,
    sems,
):
    pairs = [
        (order_hbm, order),
        (patch_hbm, patch),
        (position_hbm, position),
        (up_hbm, up),
        (down_hbm, down),
        (head_hbm, head),
        (order_t_hbm, order_t),
    ]
    copies = [pltpu.make_async_copy(src, dst, sems.at[i]) for i, (src, dst) in enumerate(pairs)]
    for copy in copies:
        copy.start()
    own = own_ref[0]

    slot = lanes_of((32, 3))
    diagonal = sublanes_of((32, 32)) == lanes_of((32, 32))
    counts = jnp.sum(jnp.where(diagonal, counts_ref[...], 0), axis=1, keepdims=True)
    hit = jnp.where((frames_ref[...] == own) & (slot < counts), 1.0, 0.0)
    weight = jnp.max(jnp.max(hit, axis=1, keepdims=True), axis=0, keepdims=True)
    mine = sublanes_of((32, HEAD)) == own
    spread = key_spread_ref[...]

    def own_keys(ref):
        table = dot(ref[...].astype(F32).astype(BF16), spread)
        return jnp.sum(jnp.where(mine, table, 0.0), axis=0, keepdims=True)

    token = sublanes_of((64, HEAD))
    column = lanes_of((64, HEAD))
    pixel_row = (token // 8) * 4 + column // (4 * KP)
    pixel_col = (token % 8) * 4 + (column // KP) % 4
    row_gap = pixel_row.astype(F32) - own_keys(key_rows_ref)
    col_gap = pixel_col.astype(F32) - own_keys(key_cols_ref)
    target = jnp.exp((row_gap * row_gap + col_gap * col_gap) * -0.125)
    mask = own_keys(key_vis_ref) * weight

    raw = gather_patches(x_ref, bias_ref)
    copies[0].wait()
    patches = dot(raw, order[...]).astype(BF16)
    copies[1].wait()
    copies[2].wait()
    embedded = dot(patches, patch[...]) + position[...].astype(F32)
    centred = embedded - jnp.mean(embedded, axis=-1, keepdims=True)
    inverse = lax.rsqrt(jnp.mean(centred * centred, axis=-1, keepdims=True) + NORM_EPS)
    unit_rows = centred * inverse
    gain = gain_ref[...]
    normed_tokens = (unit_rows * gain).astype(BF16)
    copies[3].wait()

    @pl.loop(0, HID // 256)
    def _(i):
        at = pl.ds(pl.multiple_of(i * 256, 256), 256)
        value = dot(normed_tokens, up[:, at])
        hidden_pre[:, at] = value
        hidden[:, at] = (value * normal_cdf(value)).astype(BF16)

    copies[4].wait()
    block = dot(hidden[...], down[...])
    block_round = (embedded + block).astype(BF16)
    copies[5].wait()
    heatmap = dot(block_round, head[...])
    heat_grad = ((heatmap - target) * mask).astype(BF16)
    out_grad = dot_nt(heat_grad, head[...])
    out_round = out_grad.astype(BF16)

    @pl.loop(0, HID // 256)
    def _(i):
        at = pl.ds(pl.multiple_of(i * 256, 256), 256)
        grad = dot_nt(out_round, down[at, :])
        pre = hidden_pre[:, at]
        slope = normal_cdf(pre) + pre * jnp.exp(-0.5 * pre * pre) * 0.3989422804014327
        pre_grad[:, at] = (grad * slope).astype(BF16)

    normed_grad = dot_nt(pre_grad[...], up[...])
    unit_grad = normed_grad * gain
    embed_grad = out_grad + inverse * (
        unit_grad
        - jnp.mean(unit_grad, axis=-1, keepdims=True)
        - unit_rows * jnp.mean(unit_grad * unit_rows, axis=-1, keepdims=True)
    )
    colour_grad = dot_nt(embed_grad.astype(BF16), patch[...]).astype(BF16)
    copies[6].wait()
    scatter_patches(dot(colour_grad, order_t[...]), out_ref)


def pose(own, bias, x, frames, counts, key_rows, key_cols, key_vis, gain, position, patch, up, down, head):
    smem = pl.BlockSpec(memory_space=pltpu.SMEM)
    vmem = pl.BlockSpec(memory_space=pltpu.VMEM)
    anywhere = pl.BlockSpec(memory_space=pl.ANY)
    return pl.pallas_call(
        pose_kernel,
        in_specs=[smem] * 2 + [vmem] * 8 + [anywhere] * 7,
        out_specs=vmem,
        out_shape=jax.ShapeDtypeStruct((32, 3, 8, COLS), F32),
        scratch_shapes=[
            pltpu.VMEM((768, 768), BF16),
            pltpu.VMEM((768, 768), BF16),
            pltpu.VMEM((64, DP), BF16),
            pltpu.VMEM((768, DP), BF16),
            pltpu.VMEM((DP, HID), BF16),
            pltpu.VMEM((HID, DP), BF16),
            pltpu.VMEM((DP, HEAD), BF16),
            pltpu.VMEM((64, HID), F32),
            pltpu.VMEM((64, HID), BF16),
            pltpu.VMEM((64, HID), BF16),
            pltpu.SemaphoreType.DMA((7,)),
        ],
        compiler_params=pltpu.CompilerParams(vmem_limit_bytes=48 * 1024 * 1024),
        cost_estimate=pl.CostEstimate(
            flops=2 * 64 * 15800000, bytes_accessed=17 * 1024 * 1024, transcendentals=64 * HID * 3
        ),
        name="pose",
    )(
        own,
        bias,
        x,
        frames,
        counts,
        key_rows,
        key_cols,
        key_vis,
        jnp.asarray(KEY_SPREAD),
        gain,
        jnp.asarray(PIXEL_ORDER),
        jnp.asarray(PIXEL_ORDER_T),
        position,
        patch,
        up,
        down,
        head,
    )


def frame_taps(groups):
    row = sublanes_of((8, COLS))
    taps = [from_right(g) for g in groups] + list(groups) + [from_left(g) for g in groups]
    last = taps.pop()
    for i in range(3):
        taps[i] = jnp.where(row >= 6, roll(last, 6 - 2 * i, 0), taps[i])
    return taps


def pair_taps(ref, frame):
    rows = []
    for f in range(2):
        rows += frame_taps([ref[frame + f, o] for o in range(3)])
    return jnp.concatenate(rows, axis=0).T


def back_kernel(
    feat_ref, grad_ref, next_ref, gain_ref, mean_ref, conv_ref, sel_ref, out_ref, weight_scr, carry
):
    step = pl.program_id(0)
    block = feat_ref.shape[0]

    @pl.when(step == 0)
    def _():
        conv = conv_ref[...]
        for i in range(8):
            weight_scr[:, CH * i : CH * i + CH] = dot_nt(
                sel_ref[256 * i : 256 * i + 256, :], conv
            ).astype(BF16)
        carry[...] = pair_taps(grad_ref, 0)

    gain = gain_ref[...]
    half_gain = 0.5 * gain
    mean_pair = mean_ref[...]
    for pair in range(block // 2):
        now = carry[...]
        if pair < block // 2 - 1:
            carry[...] = pair_taps(grad_ref, step * block + 2 * pair + 2)
        else:

            @pl.when(step < pl.num_programs(0) - 1)
            def _():
                carry[...] = pair_taps(grad_ref, (step + 1) * block)

            @pl.when(step == pl.num_programs(0) - 1)
            def _():
                carry[...] = pair_taps(next_ref, 0)

        taps = jnp.concatenate([now, carry[...]], axis=1).astype(BF16)
        grads = dot(taps, weight_scr[...])
        for tau in range(2):
            frame = 2 * pair + tau
            for half in range(ROWS // 2):
                rows = [2 * half, 2 * half + 1]
                xs = [feat_ref[frame, r].astype(F32) for r in rows]
                means = channel_mean(xs[0] * xs[0], xs[1] * xs[1], mean_pair)
                kept = []
                for x, mean, r in zip(xs, means, rows):
                    rescale = lax.rsqrt(mean + NORM_EPS)
                    normed = x * rescale
                    half_pre = normed * half_gain
                    sigma = 0.5 + 0.5 * jnp.tanh(half_pre)
                    slope = sigma * (1.0 + (half_pre + half_pre) * (1.0 - sigma)) * gain
                    at = CH * (ROWS * tau + r)
                    kept.append((rescale, normed, grads[:, at : at + CH] * slope))
                dots = channel_mean(kept[0][2] * kept[0][1], kept[1][2] * kept[1][1], mean_pair)
                for (rescale, normed, scaled), along, r in zip(kept, dots, rows):
                    out_ref[frame, r] = (rescale * (scaled - normed * along)).astype(BF16)


def conv_backward(features, grads, later, gain, conv_weight, block):
    frames = features.shape[0]
    return pl.pallas_call(
        back_kernel,
        grid=(frames // block,),
        in_specs=[
            pl.BlockSpec((block, ROWS, COLS, CH), lambda i: (i, 0, 0, 0)),
            whole((frames, 3, 8, COLS)),
            whole((2, 3, 8, COLS)),
            whole((1, CH)),
            whole((256, 256)),
            whole((CH, 81)),
            whole((2048, 81)),
        ],
        out_specs=pl.BlockSpec((block, ROWS, COLS, CH), lambda i: (i, 0, 0, 0)),
        out_shape=jax.ShapeDtypeStruct((frames, ROWS, COLS, CH), BF16),
        scratch_shapes=[pltpu.VMEM((256, 1024), BF16), pltpu.VMEM((COLS, 128), F32)],
        compiler_params=pltpu.CompilerParams(vmem_limit_bytes=32 * 1024 * 1024),
        cost_estimate=pl.CostEstimate(
            flops=2 * 16384 * 1024, bytes_accessed=9 * 1024 * 1024, transcendentals=2 * 2097152
        ),
        name="conv_back",
    )(features, grads, later, gain, jnp.asarray(MEAN_PAIR), conv_weight, jnp.asarray(SELECTOR_T))


def per_device(
    features,
    norm_gain,
    conv_weight,
    colour_bias,
    observed_frames,
    observed_counts,
    key_rows,
    key_columns,
    key_visible,
    position_table,
    patch_weight,
    layer_gain,
    up_weight,
    down_weight,
    head_weight,
):
    tm_count = lax.axis_size("tm")
    own = lax.axis_index("tile").reshape(1)
    gain = norm_gain.reshape(1, CH)
    tail, sums = conv_forward(features, gain, conv_weight, 8)
    prior = lax.ppermute(tail, "tm", [(i, i + 1) for i in range(tm_count - 1)])
    sums = sums.at[:2].add(prior)
    strips = lax.all_to_all(sums, "tile", 0, 0, tiled=True)
    colour_grad = pose(
        own,
        colour_bias,
        strips,
        observed_frames[0],
        observed_counts,
        key_rows,
        key_columns,
        key_visible,
        layer_gain.reshape(1, DP),
        position_table,
        patch_weight,
        up_weight,
        down_weight,
        head_weight,
    )
    grads = lax.all_to_all(colour_grad, "tile", 0, 0, tiled=True)
    later = lax.ppermute(grads[:2], "tm", [(i + 1, i) for i in range(tm_count - 1)])
    return conv_backward(features, grads, later, gain, conv_weight, 8)


def solution(mesh):
    in_specs = (
        P("tm", "tile", None, None),
        P(),
        P(),
        P(),
        P("tm", None, None),
        P("tm", None),
        P("tm", None),
        P("tm", None),
        P("tm", None),
        P(),
        P(),
        P(),
        P(),
        P(),
        P(),
    )
    return jax.shard_map(
        per_device,
        mesh=mesh,
        in_specs=in_specs,
        out_specs=P("tm", "tile", None, None),
        check_vma=False,
    )
```

time: 503 us -> 84.6 us (0.17); the launches traced: 493 us -> 84.1 us
  local copies, waits for them, and re-layouts: 219 us -> 6.9 us
  waiting for transfers between devices: 163 us -> 11.7 us
  matrix products: 52.4 us -> 0 us
  Pallas kernels: 0 us -> 36.1 us
  other arithmetic: 23.6 us -> 1.35 us
  between operations: 14.3 us -> 0.2 us
  blocking collectives: 0 us -> 13.6 us
  starting transfers between devices: 20.4 us -> 14.3 us
    transpose x2 -> x0, local copies, waits for them, and re-layouts: 79.2 us -> none  [the longest x1 39.8 us: pose_grad(): patches = images.reshape(frame_total, grid_rows, PATCH, grid_cols, PATCH,...]
    reduce_scatter x1 -> x0, waiting for transfers between devices: 78.1 us -> none  [per_device(): lax.psum_scatter(spread.astype(jnp.bfloat16), 'tile', scatter_dimension=1...]
    another operation x2 -> x0, local copies, waits for them, and re-layouts: 65.5 us -> none  [the longest x1 33.2 us: pose_grad(): images.reshape(frame_total, grid_rows, PATCH, grid_cols, PATCH, 3)]
    all_gather x1 -> x0, waiting for transfers between devices: 59.8 us -> none  [per_device(): everything = lax.all_gather(strips, 'tile', axis=1, tiled=True)]
    dot_general x13 -> x0, matrix products: 52.4 us -> none  [the longest x1 10.8 us: pose_grad(): jnp.dot(pre_grad, up_weight.T, preferred_element_type=jnp.float32)]
    concatenate x3 -> x0, local copies, waits for them, and re-layouts: 52.1 us -> none  [the longest x1 51.6 us: tap_columns(): return jnp.concatenate(pieces, axis=-1)]
    pallas_call x0 -> x4, Pallas kernels: none -> 36.1 us  [the longest x1 16.9 us: pose(): pl.pallas_call(pose_kernel, in_specs=[smem] * 2 + [vmem] * 8 + [anywhere]...]
    ppermute x6 -> x2, waiting for transfers between devices: 25.4 us -> 3.27 us  [the longest x1 3.27 us: per_device(): lax.ppermute(grads[:2], 'tm', [(i + 1, i) for i in range(tm_count - 1)])]
  transfers between devices with their start and end apart: 8 -> 3, of which waited for: 7 -> 2; matrix products, arithmetic and copies ran while one was open for 2% -> 2% of each run, Pallas kernels for 0% -> 6%
where the time goes in v1:
time: 84.6 us; the launch traced here: 84.1 us
  Pallas kernels  36.1 us (43%)
  starting transfers between devices  14.3 us (17%)
  blocking collectives  13.6 us (16%)
  waiting for transfers between devices  11.7 us (14%)
  local copies, waits for them, and re-layouts  6.9 us (8%)
  other arithmetic  1.35 us (2%)
    pallas_call x1, Pallas kernels, pose(): pl.pallas_call(pose_kernel, in_specs=[smem] * 2 + [vmem] * 8 + [anywhere]...  16.9 us
    all_to_all x1, blocking collectives, per_device(): grads = lax.all_to_all(colour_grad, 'tile', 0, 0, tiled=True)  13.6 us
    pallas_call x1, Pallas kernels, conv_backward(): pl.pallas_call(back_kernel, grid=(frames // block,), in_specs=[pl.BlockSp...  11.3 us
    all_to_all x1, starting transfers between devices, per_device(): strips = lax.all_to_all(sums, 'tile', 0, 0, tiled=True)  9.05 us
    all_to_all x1, waiting for transfers between devices, per_device(): strips = lax.all_to_all(sums, 'tile', 0, 0, tiled=True)  8.39 us
    unnamed x41, local copies, waits for them, and re-layouts  6.8 us
    pallas_call x1, Pallas kernels, conv_forward(): pl.pallas_call(conv_kernel, grid=(frames // block,), in_specs=[pl.BlockSp...  5.45 us
    ppermute x1, starting transfers between devices, per_device(): prior = lax.ppermute(tail, 'tm', [(i, i + 1) for i in range(tm_count - 1)])  3.93 us
  transfers between devices with their start and end apart: 3, of which 2 were waited for; matrix products, arithmetic and copies ran while one was open for 2% of the time, Pallas kernels for 6%

profile of v1, /device:TPU:1, one launch (start us, length us, event | category | flops | bytes accessed | tf_op | source)
XLA Modules:
  0.0 84.1 jit_solution(4153502854604806373)
XLA Ops:
  0.0 1.5 %copy.22.conv_ref = bf16[128,81]{1,0:T(8,128)(2,1)} copy(bf16[128,81]{0,1:T(8,128)(2,1)} %param.25) | data formatting | bytes 41472 | tf_op args[2]
  1.5 2.5 %conv_tail.1 = f32[2,3,8,128]{3,2,1,0:T(8,128)} custom-call(bf16[32,4,128,128]{3,2,1,0:T(8,128)(2,1)} %feat_ref.5, f32[1,128]{1,0:T(1,128)} %bitcast.4, bf16[256,256]{1,0:T(8,128)(2,1)} %constant.45.clone.mean_ref, bf16[128,81]{1,0:T(8,128)(2,1)} %copy.22.conv_ref, bf16[81,2048]{1,0:T(8,128)(2,1)} %constant.46.clone.sel_ref), custom_call_target="tpu_custom_call" | custom-call | tf_op jit(solution)/shard_map/conv_tail/pallas_call | solution.py:179
  4.0 3.9 %collective-permute-start = (f32[2,3,8,128]{3,2,1,0:T(8,128)}, f32[2,3,8,128]{3,2,1,0:T(8,128)S(1)}, u32[]{:S(2)}, u32[]{:S(2)}) collective-permute-start(f32[2,3,8,128]{3,2,1,0:T(8,128)} %conv_tail.1), channel_id=1, source_target_pairs={{0,1},{1,2},{2,3},{4,5},{5,6},{6,7},{8,9},{9,10},{10,11},{12,13},{... | collective-permute-start | bytes 73736 | tf_op jit(solution)/shard_map/ppermute | solution.py:540
  8.0 0.0 copy-start
  8.0 2.2 %copy-done = bf16[32,4,128,128]{3,2,1,0:T(8,128)(2,1)S(1)} copy-done((bf16[32,4,128,128]{3,2,1,0:T(8,128)(2,1)S(1)}, bf16[32,4,128,128]{3,2,1,0:T(8,128)(2,1)}, u32[]{:S(2)}) %copy-start) | copy-done | bytes 4194328
  10.2 0.0 copy-start.2
  10.2 0.0 copy-start.8
  10.2 0.0 copy-start.9
  10.2 5.5 %conv_main.1 = f32[32,3,8,128]{3,2,1,0:T(8,128)} custom-call(bf16[32,4,128,128]{3,2,1,0:T(8,128)(2,1)S(1)} %copy-done, f32[1,128]{1,0:T(1,128)S(1)} %bitcast.5, bf16[256,256]{1,0:T(8,128)(2,1)S(1)} %copy-done.4, bf16[128,81]{1,0:T(8,128)(2,1)S(1)} %copy-done.7, bf16[81,2048]{1,0:T(8,128)(2,1)S(1)} %copy-done.6), custom_call_target="tpu_custom_call" | custom-call | flops 33554432 | bytes 5242880 | tf_op jit(solution)/shard_map/conv_main/pallas_call | solution.py:188
  15.7 1.4 %fusion = f32[32,3,8,128]{3,2,1,0:T(8,128)} fusion(f32[32,3,8,128]{3,2,1,0:T(8,128)} %conv_main.1, f32[2,3,8,128]{3,2,1,0:T(8,128)S(1)} %collective-permute-done), kind=kLoop, calls=%fused_computation.1 | loop fusion | flops 6144 | bytes 73728 | tf_op jit(solution)/shard_map/scatter-add | solution.py:541
  17.1 9.0 %all-to-all-start = ((f32[32,3,8,128]{3,2,1,0:T(8,128)}), f32[32,3,8,128]{3,2,1,0:T(8,128)S(1)}, u32[]{:S(2)}, u32[]{:S(2)}) async-start(f32[32,3,8,128]{3,2,1,0:T(8,128)} %fusion), calls=%async_computation | async-start | bytes 786432 | tf_op jit(solution)/shard_map/all_to_all | solution.py:542
  26.1 0.1 copy.30
  26.2 0.1 copy.25.key_rows_ref
  26.3 0.1 copy.26.key_cols_ref
  26.4 0.1 copy.27.key_vis_ref
  26.5 1.5 %copy.28.head_hbm = bf16[1280,272]{1,0:T(8,128)(2,1)S(1)} copy(bf16[1280,272]{0,1:T(8,128)(2,1)} %param.37) | data formatting | bytes 1392640 | tf_op args[14]
  28.0 8.4 %all-to-all-done.x_ref = f32[32,3,8,128]{3,2,1,0:T(8,128)S(1)} async-done(((f32[32,3,8,128]{3,2,1,0:T(8,128)}), f32[32,3,8,128]{3,2,1,0:T(8,128)S(1)}, u32[]{:S(2)}, u32[]{:S(2)}) %all-to-all-start) | async-done | bytes 393248 | tf_op jit(solution)/shard_map/all_to_all | solution.py:542
  36.4 0.0 copy-start.3
  36.5 1.3 %copy-done.3 = bf16[768,768]{1,0:T(8,128)(2,1)S(1)} copy-done((bf16[768,768]{1,0:T(8,128)(2,1)S(1)}, bf16[768,768]{1,0:T(8,128)(2,1)}, u32[]{:S(2)}) %copy-start.3) | copy-done | bytes 1179672
  37.7 16.9 %pose.1 = f32[32,3,8,128]{3,2,1,0:T(8,128)S(1)} custom-call(s32[1]{0:T(128)} %bitcast.own_ref, f32[3]{0:T(128)S(1)} %copy-done.11, f32[32,3,8,128]{3,2,1,0:T(8,128)S(1)} %all-to-all-done.x_ref, s32[32,3]{1,0:T(8,128)S(1)} %bitcast.3, s32[1,32]{1,0:T(1,128)S(1)} %copy-done.12, s32[32,17]{1,0:T(8,128)S(1)} %copy.25.key_rows_ref, ...), custom_call_target="tpu_custom_call" | custom-call | flops 2022400000 | bytes 17825792 | tf_op jit(solution)/shard_map/pose/pallas_call | solution.py:380
  54.6 13.6 %all_to_all.10.grad_ref = f32[32,3,8,128]{3,2,1,0:T(8,128)S(1)} all-to-all(f32[32,3,8,128]{3,2,1,0:T(8,128)S(1)} %pose.1), channel_id=1, replica_groups=mesh['tile'=32,'tm'=4] {'tile'}, dimensions={0} | all-to-all | bytes 786432 | tf_op jit(solution)/shard_map/all_to_all | solution.py:559
  68.3 1.3 %collective-permute-start.1 = (f32[2,3,8,128]{3,2,1,0:T(8,128)S(1)}, f32[2,3,8,128]{3,2,1,0:T(8,128)S(1)}, u32[]{:S(2)}, u32[]{:S(2)}) collective-permute-start(f32[2,3,8,128]{3,2,1,0:T(8,128)S(1)} %slice.35), channel_id=1, source_target_pairs={{1,0},{2,1},{3,2},{5,4},{6,5},{7,6},{9,8},{10,9},{11,10},{13,12},{... | collective-permute-start | bytes 73736 | tf_op jit(solution)/shard_map/ppermute | solution.py:560
  69.6 3.3 %collective-permute-done.1.next_ref = f32[2,3,8,128]{3,2,1,0:T(8,128)S(1)} collective-permute-done((f32[2,3,8,128]{3,2,1,0:T(8,128)S(1)}, f32[2,3,8,128]{3,2,1,0:T(8,128)S(1)}, u32[]{:S(2)}, u32[]{:S(2)}) %collective-permute-start.1) | collective-permute-done | bytes 24608 | tf_op jit(solution)/shard_map/ppermute | solution.py:560
  72.9 11.3 %conv_back.1 = bf16[32,4,128,128]{3,2,1,0:T(8,128)(2,1)} custom-call(bf16[32,4,128,128]{3,2,1,0:T(8,128)(2,1)S(1)} %copy-done.1, f32[32,3,8,128]{3,2,1,0:T(8,128)S(1)} %all_to_all.10.grad_ref, f32[2,3,8,128]{3,2,1,0:T(8,128)S(1)} %collective-permute-done.1.next_ref, f32[1,128]{1,0:T(1,128)S(1)} %bitcast.6, bf16[256,256]{1,0:T(8,128)(2,1)S(1)} %copy-done.4, ...), custom_call_target="tpu_custom_call" | custom-call | flops 33554432 | bytes 9437184 | tf_op jit(solution)/shard_map/conv_back/pallas_call | solution.py:496
  (32 shorter events, 0.1 us)
Async XLA Ops:
  0.0 7.9 %copy-start.4 = (bf16[256,256]{1,0:T(8,128)(2,1)S(1)}, bf16[256,256]{1,0:T(8,128)(2,1)}, u32[]{:S(2)}) copy-start(bf16[256,256]{1,0:T(8,128)(2,1)} %constant.45.clone.mean_ref) | copy-start | bytes 393220
  0.0 7.9 %copy-start.6 = (bf16[81,2048]{1,0:T(8,128)(2,1)S(1)}, bf16[81,2048]{1,0:T(8,128)(2,1)}, u32[]{:S(2)}) copy-start(bf16[81,2048]{1,0:T(8,128)(2,1)} %constant.46.clone.sel_ref) | copy-start | bytes 995332
  0.0 7.9 %copy-start.10 = (f32[128]{0:T(128)S(1)}, f32[128]{0:T(128)}, u32[]{:S(2)}) copy-start(f32[128]{0:T(128)} %param.24) | copy-start | bytes 1540
  1.5 6.4 %copy-start.7 = (bf16[128,81]{1,0:T(8,128)(2,1)S(1)}, bf16[128,81]{1,0:T(8,128)(2,1)}, u32[]{:S(2)}) copy-start(bf16[128,81]{1,0:T(8,128)(2,1)} %copy.22.conv_ref) | copy-start | bytes 62212
  4.0 11.7 %collective-permute-start = (f32[2,3,8,128]{3,2,1,0:T(8,128)}, f32[2,3,8,128]{3,2,1,0:T(8,128)S(1)}, u32[]{:S(2)}, u32[]{:S(2)}) collective-permute-start(f32[2,3,8,128]{3,2,1,0:T(8,128)} %conv_tail.1), channel_id=1, source_target_pairs={{0,1},{1,2},{2,3},{4,5},{5,6},{6,7},{8,9},{9,10},{10,11},{12,13},{... | collective-permute-start | bytes 73736 | tf_op jit(solution)/shard_map/ppermute | solution.py:540
  8.0 2.2 %copy-start = (bf16[32,4,128,128]{3,2,1,0:T(8,128)(2,1)S(1)}, bf16[32,4,128,128]{3,2,1,0:T(8,128)(2,1)}, u32[]{:S(2)}) copy-start(bf16[32,4,128,128]{3,2,1,0:T(8,128)(2,1)} %feat_ref.5) | copy-start | bytes 12582916
  10.2 16.0 %copy-start.16 = (f32[1280]{0:T(1024)S(1)}, f32[1280]{0:T(1024)}, u32[]{:S(2)}) copy-start(f32[1280]{0:T(1024)} %param.34) | copy-start | bytes 15364
  10.2 16.0 %copy-start.17 = (s32[1,32,3]{1,0,2:T(1,128)S(1)}, s32[1,32,3]{1,0,2:T(1,128)}, u32[]{:S(2)}) copy-start(s32[1,32,3]{1,0,2:T(1,128)} %param.27) | copy-start | bytes 1156
  10.2 16.1 %copy-start.13 = (s32[32,17]{0,1:T(8,128)S(1)}, s32[32,17]{0,1:T(8,128)}, u32[]{:S(2)}) copy-start(s32[32,17]{0,1:T(8,128)} %param.29) | copy-start | bytes 6532
  10.2 16.2 %copy-start.14 = (s32[32,17]{0,1:T(8,128)S(1)}, s32[32,17]{0,1:T(8,128)}, u32[]{:S(2)}) copy-start(s32[32,17]{0,1:T(8,128)} %param.30) | copy-start | bytes 6532
  10.2 16.2 %copy-start.15 = (s32[32,17]{0,1:T(8,128)S(1)}, s32[32,17]{0,1:T(8,128)}, u32[]{:S(2)}) copy-start(s32[32,17]{0,1:T(8,128)} %param.31) | copy-start | bytes 6532
  10.2 26.2 %copy-start.2 = (bf16[768,768]{1,0:T(8,128)(2,1)S(1)}, bf16[768,768]{1,0:T(8,128)(2,1)}, u32[]{:S(2)}) copy-start(bf16[768,768]{1,0:T(8,128)(2,1)} %constant.49.clone.order_t_hbm) | copy-start | bytes 3538948
  10.2 26.2 %copy-start.8 = (bf16[64,1280]{1,0:T(8,128)(2,1)S(1)}, bf16[64,1280]{1,0:T(8,128)(2,1)}, u32[]{:S(2)}) copy-start(bf16[64,1280]{1,0:T(8,128)(2,1)} %position_hbm.1) | copy-start | bytes 491524
  10.2 26.2 %copy-start.9 = (bf16[17,272]{1,0:T(8,128)(2,1)S(1)}, bf16[17,272]{1,0:T(8,128)(2,1)}, u32[]{:S(2)}) copy-start(bf16[17,272]{1,0:T(8,128)(2,1)} %constant.47.clone.key_spread_ref) | copy-start | bytes 27748
  10.2 26.2 %copy-start.11 = (f32[3]{0:T(128)S(1)}, f32[3]{0:T(128)}, u32[]{:S(2)}) copy-start(f32[3]{0:T(128)} %bias_ref.1) | copy-start | bytes 40
  10.2 26.2 %copy-start.12 = (s32[1,32]{1,0:T(1,128)S(1)}, s32[1,32]{1,0:T(1,128)}, u32[]{:S(2)}) copy-start(s32[1,32]{1,0:T(1,128)} %counts_ref.1) | copy-start | bytes 388
  17.1 19.4 %all-to-all-start = ((f32[32,3,8,128]{3,2,1,0:T(8,128)}), f32[32,3,8,128]{3,2,1,0:T(8,128)S(1)}, u32[]{:S(2)}, u32[]{:S(2)}) async-start(f32[32,3,8,128]{3,2,1,0:T(8,128)} %fusion), calls=%async_computation | async-start | bytes 786432 | tf_op jit(solution)/shard_map/all_to_all | solution.py:542
  36.4 1.3 %copy-start.3 = (bf16[768,768]{1,0:T(8,128)(2,1)S(1)}, bf16[768,768]{1,0:T(8,128)(2,1)}, u32[]{:S(2)}) copy-start(bf16[768,768]{1,0:T(8,128)(2,1)} %constant.48.clone.order_hbm) | copy-start | bytes 3538948
  37.7 35.1 %copy-start.1 = (bf16[32,4,128,128]{3,2,1,0:T(8,128)(2,1)S(1)}, bf16[32,4,128,128]{3,2,1,0:T(8,128)(2,1)}, u32[]{:S(2)}) copy-start(bf16[32,4,128,128]{3,2,1,0:T(8,128)(2,1)} %feat_ref.5) | copy-start | bytes 12582916
  37.7 35.1 %copy-start.5 = (bf16[2048,81]{1,0:T(8,128)(2,1)S(1)}, bf16[2048,81]{1,0:T(8,128)(2,1)}, u32[]{:S(2)}) copy-start(bf16[2048,81]{1,0:T(8,128)(2,1)} %constant.50.clone.sel_ref) | copy-start | bytes 995332
  68.3 4.6 %collective-permute-start.1 = (f32[2,3,8,128]{3,2,1,0:T(8,128)S(1)}, f32[2,3,8,128]{3,2,1,0:T(8,128)S(1)}, u32[]{:S(2)}, u32[]{:S(2)}) collective-permute-start(f32[2,3,8,128]{3,2,1,0:T(8,128)S(1)} %slice.35), channel_id=1, source_target_pairs={{1,0},{2,1},{3,2},{5,4},{6,5},{7,6},{9,8},{10,9},{11,10},{13,12},{... | collective-permute-start | bytes 73736 | tf_op jit(solution)/shard_map/ppermute | solution.py:560

commit v2 on v1

v2 whole, which is shorter than its diff:
```python
import jax
import jax.numpy as jnp
import ml_dtypes
import numpy as np
from jax import lax
from jax.experimental import pallas as pl
from jax.experimental.pallas import tpu as pltpu
from jax.sharding import PartitionSpec as P

CH = 128
DP = 1280
HID = 2560
PATCH = 16
KP = 17
HEAD = 272
COLS = 128
ROWS = 4
GROUP = 4
FORWARD_FRAMES = 8
BACK_FRAMES = 10
BACK_ROWS = 4
NORM_EPS = 1e-06
F32 = jnp.float32
BF16 = jnp.bfloat16


def slot_of(c, o, k):
    group = 3 * c + o
    if group < 8:
        return 8 * group + k
    return 8 * (k // 2) + 6 + k % 2


def make_selector():
    table = np.zeros((81, 2, ROWS, 256), np.float32)
    for tau in range(2):
        for r in range(ROWS):
            for f in range(4):
                a = tau + 2 - f
                if not 0 <= a <= 2:
                    continue
                for k in range(6):
                    b = r + 2 - k
                    if not 0 <= b <= 2:
                        continue
                    for c in range(3):
                        for o in range(3):
                            table[3 * (9 * a + 3 * b + c) + o, tau, r, 64 * f + slot_of(c, o, k)] = 1
    return table.reshape(81, 2048)


def make_pixel_order():
    table = np.zeros((768, 768), np.float32)
    for o in range(3):
        for pixel in range(256):
            table[256 * o + pixel, 3 * pixel + o] = 1
    return table


def make_key_spread():
    table = np.zeros((KP, HEAD), np.float32)
    table[np.arange(HEAD) % KP, np.arange(HEAD)] = 1
    return table


SELECTOR = make_selector().astype(ml_dtypes.bfloat16)
SELECTOR_T = np.ascontiguousarray(make_selector().T).astype(ml_dtypes.bfloat16)
PIXEL_ORDER = make_pixel_order().astype(ml_dtypes.bfloat16)
KEY_SPREAD = make_key_spread().astype(ml_dtypes.bfloat16)
MEAN_PAIR = (np.kron(np.eye(2), np.ones((CH, CH))) / CH).astype(ml_dtypes.bfloat16)


def dot(a, b):
    return jnp.dot(a, b, preferred_element_type=F32)


def dot_tn(a, b):
    return lax.dot_general(a, b, (((0,), (0,)), ((), ())), preferred_element_type=F32)


def dot_nt(a, b):
    return lax.dot_general(a, b, (((1,), (1,)), ((), ())), preferred_element_type=F32)


def roll(x, shift, axis):
    shift %= x.shape[axis]
    return pltpu.roll(x, shift, axis) if shift else x


def channel_means(values, mean_pair):
    rounded = [value.astype(BF16) for value in values]
    pairs = [jnp.concatenate(rounded[i : i + 2], axis=1) for i in range(0, len(values), 2)]
    means = dot(jnp.concatenate(pairs, axis=0), mean_pair)
    out = []
    for i in range(len(pairs)):
        rows = slice(COLS * i, COLS * i + COLS)
        out += [means[rows, :CH], means[rows, CH:]]
    return out


def lanes_of(shape):
    return lax.broadcasted_iota(jnp.int32, shape, len(shape) - 1)


def sublanes_of(shape):
    return lax.broadcasted_iota(jnp.int32, shape, len(shape) - 2)


def from_left(x):
    return jnp.where(lanes_of(x.shape) >= 1, roll(x, 1, x.ndim - 1), 0.0)


def from_right(x):
    return jnp.where(lanes_of(x.shape) < COLS - 1, roll(x, -1, x.ndim - 1), 0.0)


def activated_rows(feat_ref, frame, half_gain, mean_pair):
    xs = [feat_ref[frame, r].astype(F32) for r in range(ROWS)]
    acts = []
    for x, mean in zip(xs, channel_means([x * x for x in xs], mean_pair)):
        half = x * lax.rsqrt(mean + NORM_EPS) * half_gain
        acts.append((half + half * jnp.tanh(half)).astype(BF16))
    return acts


def frame_sums(taps, out_ref, frame):
    groups = [taps[8 * g : 8 * g + 8] for g in range(8)]
    row = sublanes_of((8, COLS))
    groups.append(
        jnp.where(
            row < 2,
            roll(groups[0], 2, 0),
            jnp.where(row < 4, roll(groups[1], 4, 0), roll(groups[2], 6, 0)),
        )
    )
    for o in range(3):
        out_ref[frame, o] = from_left(groups[o]) + groups[3 + o] + from_right(groups[6 + o])


def pair_sums(feat_ref, frame, half_gain, mean_pair, weight):
    acts = []
    for tau in range(2):
        acts += activated_rows(feat_ref, frame + tau, half_gain, mean_pair)
    return dot(jnp.concatenate(acts, axis=1), weight)


def tail_kernel(
    feat_hbm, gain_ref, mean_ref, conv_ref, sel_ref, sel_t_ref,
    out_ref, feat_ref, weight_ref, weight_t_ref, sems,
):
    frames = feat_hbm.shape[0]
    last = pltpu.make_async_copy(feat_hbm.at[frames - 2 :], feat_ref.at[frames - 2 :], sems.at[0])
    rest = pltpu.make_async_copy(feat_hbm.at[: frames - 2], feat_ref.at[: frames - 2], sems.at[1])
    last.start()
    rest.start()
    conv = conv_ref[...]
    for i in range(8):
        at = slice(CH * i, CH * i + CH)
        wide = slice(256 * i, 256 * i + 256)
        weight_ref[at, :] = dot_tn(conv, sel_ref[:, wide]).astype(BF16)
        weight_t_ref[:, at] = dot(sel_t_ref[wide, :], conv).astype(BF16)
    last.wait()
    sums = pair_sums(feat_ref, frames - 2, 0.5 * gain_ref[...], mean_ref[...], weight_ref[:, 128:])
    taps = sums.T
    for f in range(2):
        frame_sums(taps[64 * f : 64 * f + 64], out_ref, f)
    rest.wait()


def conv_kernel(
    feat_ref, gain_ref, mean_ref, weight_ref, up_hbm, down_hbm, out_ref, up_ref, down_ref, carry, sems
):
    copies = [
        pltpu.make_async_copy(up_hbm, up_ref, sems.at[0]),
        pltpu.make_async_copy(down_hbm, down_ref, sems.at[1]),
    ]
    for copy in copies:
        copy.start()
    carry[...] = jnp.zeros_like(carry)
    half_gain = 0.5 * gain_ref[...]
    mean_pair = mean_ref[...]

    @pl.loop(0, feat_ref.shape[0] // FORWARD_FRAMES)
    def _(step):
        for pair in range(FORWARD_FRAMES // 2):
            frame = step * FORWARD_FRAMES + 2 * pair
            sums = pair_sums(feat_ref, frame, half_gain, mean_pair, weight_ref[...])
            taps = (sums[:, :128] + carry[...]).T
            carry[...] = sums[:, 128:]
            for f in range(2):
                frame_sums(taps[64 * f : 64 * f + 64], out_ref, frame + f)

    for copy in copies:
        copy.wait()


VMEM = pl.BlockSpec(memory_space=pltpu.VMEM)
ANYWHERE = pl.BlockSpec(memory_space=pl.ANY)


def megabytes(count):
    return pltpu.CompilerParams(vmem_limit_bytes=count * 1024 * 1024)


def conv_tail(features, gain, conv_weight):
    return pl.pallas_call(
        tail_kernel,
        in_specs=[ANYWHERE] + [VMEM] * 5,
        out_specs=[VMEM] * 4,
        out_shape=[
            jax.ShapeDtypeStruct((2, 3, 8, COLS), F32),
            pltpu.VMEM(features.shape, BF16),
            pltpu.VMEM((1024, 256), BF16),
            pltpu.VMEM((256, 1024), BF16),
        ],
        scratch_shapes=[pltpu.SemaphoreType.DMA((2,))],
        compiler_params=megabytes(8),
        name="conv_tail",
    )(
        features,
        gain,
        jnp.asarray(MEAN_PAIR),
        conv_weight,
        jnp.asarray(SELECTOR),
        jnp.asarray(SELECTOR_T),
    )


def conv_main(features, gain, weight, up, down):
    return pl.pallas_call(
        conv_kernel,
        in_specs=[VMEM] * 4 + [ANYWHERE] * 2,
        out_specs=[VMEM, ANYWHERE, ANYWHERE],
        out_shape=[
            jax.ShapeDtypeStruct((features.shape[0], 3, 8, COLS), F32),
            pltpu.VMEM(up.shape, BF16),
            pltpu.VMEM(down.shape, BF16),
        ],
        scratch_shapes=[pltpu.VMEM((COLS, 128), F32), pltpu.SemaphoreType.DMA((2,))],
        compiler_params=megabytes(12),
        cost_estimate=pl.CostEstimate(
            flops=2 * 16384 * 1024, bytes_accessed=20 * 1024 * 1024, transcendentals=2 * 2097152
        ),
        name="conv_main",
    )(features, gain, jnp.asarray(MEAN_PAIR), weight, up, down)


def lay_rows(groups):
    row = sublanes_of(groups[0].shape)
    both = jnp.where(row < 4, groups[0], roll(groups[1], 4, 1))
    return jnp.concatenate([both, groups[2]], axis=1)


def rim_kernel(sums_ref, prior_ref, up_ref, down_ref):
    for o in range(3):
        for k, out_ref in ((0, up_ref), (5, down_ref)):
            out_ref[o] = sums_ref[:, o, k, :]
            out_ref[o, 0:2] = sums_ref[0:2, o, k, :] + prior_ref[:, o, k, :]


def rims(sums, prior):
    shape = jax.ShapeDtypeStruct((3, sums.shape[0], COLS), F32)
    return pl.pallas_call(
        rim_kernel,
        in_specs=[VMEM] * 2,
        out_specs=[VMEM] * 2,
        out_shape=[shape] * 2,
        compiler_params=megabytes(4),
        name="rims",
    )(sums, prior)


def colour_kernel(own_ref, bias_ref, sums_ref, prior_ref, above_ref, below_ref, *rest):
    out_refs, total = rest[:GROUP], rest[GROUP]
    total[...] = sums_ref[...]
    total[0:2] = sums_ref[0:2] + prior_ref[...]
    row = sublanes_of((8, 8, COLS))
    me = lax.rem(own_ref[0], GROUP)
    for turn in range(GROUP):
        frames = pl.ds(pl.multiple_of(lax.rem(me + turn, GROUP) * 8, 8), 8)
        groups = []
        for o in range(3):
            value = total[frames, o]
            value += jnp.where(row == 1, above_ref[o, frames, :][:, None, :], 0.0)
            value += jnp.where(row == 4, below_ref[o, frames, :][:, None, :], 0.0)
            groups.append(roll(value, -1, 1) + bias_ref[o])
        out_refs[turn][...] = lay_rows(groups).astype(BF16)


def colours(own, bias, sums, prior, above, below):
    smem = pl.BlockSpec(memory_space=pltpu.SMEM)
    shape = jax.ShapeDtypeStruct((8, 16, COLS), BF16)
    return pl.pallas_call(
        colour_kernel,
        in_specs=[smem] * 2 + [VMEM] * 4,
        out_specs=[VMEM] * GROUP,
        out_shape=[shape] * GROUP,
        scratch_shapes=[pltpu.VMEM(sums.shape, F32)],
        compiler_params=megabytes(4),
        name="colours",
    )(own, bias, sums, prior, above, below)


def swap_turns(parts):
    count = lax.axis_size("tile")
    out = [parts[0]]
    for turn in range(1, GROUP):
        pairs = [(i, i - i % GROUP + (i + turn) % GROUP) for i in range(count)]
        out.append(lax.ppermute(parts[turn], "tile", pairs))
    return out


def to_neighbours(up, down):
    count = lax.axis_size("tile")
    above = lax.ppermute(down, "tile", [(i, i + 1) for i in range(count - 1)])
    below = lax.ppermute(up, "tile", [(i + 1, i) for i in range(count - 1)])
    return above, below


def swap_blocks(x):
    row, group = sublanes_of(x.shape), lanes_of(x.shape) // 16
    for bit in (4, 2, 1):
        low = (row & bit) == 0
        same = low == ((group & bit) == 0)
        moved = jnp.where(
            low,
            roll(roll(x, -bit, 1), 16 * bit, 2),
            roll(roll(x, bit, 1), -16 * bit, 2),
        )
        x = jnp.where(same, x, moved)
    return x


def gather_patches(me, x_refs, strips):
    for turn in range(GROUP):
        strips[lax.rem(me + GROUP - turn, GROUP)] = x_refs[turn][...].astype(F32)
    first = sublanes_of((8, 8, COLS)) < 4
    pieces = [[], [], []]
    for half in range(2):
        even, odd = strips[2 * half], strips[2 * half + 1]
        pieces[0].append(jnp.where(first, even[:, :8], roll(odd[:, :8], 4, 1)))
        pieces[1].append(jnp.where(first, roll(even[:, :8], 4, 1), odd[:, :8]))
        pieces[2].append(jnp.where(first, even[:, 8:], roll(odd[:, 8:], 4, 1)))
    ordered = [swap_blocks(piece).reshape(64, 128) for group in pieces for piece in group]
    return jnp.concatenate(ordered, axis=1).astype(BF16)


def scatter_patches(me, grad, strips, out_refs):
    rows = [swap_blocks(grad[:, 128 * i : 128 * i + 128].reshape(8, 8, 128)) for i in range(6)]
    for half in range(2):
        groups = [rows[2 * o + half] for o in range(3)]
        strips[2 * half] = lay_rows(groups)
        strips[2 * half + 1] = lay_rows([roll(group, 4, 1) for group in groups])
    for turn in range(GROUP):
        out_refs[turn][...] = strips[lax.rem(me + turn, GROUP)].astype(BF16)


def normal_cdf(x):
    return 0.5 * (1.0 + lax.erf(x * 0.7071067811865476))


def pose_kernel(
    own_ref,
    x0_ref,
    x1_ref,
    x2_ref,
    x3_ref,
    frames_ref,
    counts_ref,
    key_rows_ref,
    key_cols_ref,
    key_vis_ref,
    key_spread_ref,
    gain_ref,
    up,
    down,
    order_hbm,
    patch_hbm,
    head_hbm,
    position_hbm,
    out0_ref,
    out1_ref,
    out2_ref,
    out3_ref,
    order,
    patch,
    head,
    position,
    strips,
    key_table,
    hidden_pre,
    hidden,
    pre_grad,
    sems,
):
    pairs = [(order_hbm, order), (patch_hbm, patch), (position_hbm, position), (head_hbm, head)]
    copies = [pltpu.make_async_copy(src, dst, sems.at[i]) for i, (src, dst) in enumerate(pairs)]
    for copy in copies:
        copy.start()
    token_row = own_ref[0] // GROUP
    me = lax.rem(own_ref[0], GROUP)
    first_frame = pl.multiple_of(me * 8, 8)

    frame = sublanes_of((8, 32)) + first_frame
    hit = jnp.zeros((8, 32), F32)
    for slot in range(3):
        used = frames_ref[slot] == frame
        hit = jnp.maximum(hit, jnp.where(used & (counts_ref[...] > slot), 1.0, 0.0))
    weight = jnp.max(hit, axis=1, keepdims=True)
    spread = key_spread_ref[...]

    def own_keys(ref):
        key_table[...] = dot_tn(ref[...].astype(F32).astype(BF16), spread)
        return key_table[pl.ds(first_frame, 8), :]

    def by_token(value):
        return jnp.broadcast_to(value[:, None, :], (8, 8, HEAD)).reshape(64, HEAD)

    token_column = sublanes_of((64, HEAD)) % 8
    column = lanes_of((64, HEAD))
    pixel_row = token_row * 4 + column // (4 * KP)
    pixel_col = token_column * 4 + (column // KP) % 4
    row_gap = pixel_row.astype(F32) - by_token(own_keys(key_rows_ref))
    col_gap = pixel_col.astype(F32) - by_token(own_keys(key_cols_ref))
    target = jnp.exp((row_gap * row_gap + col_gap * col_gap) * -0.125)
    mask = by_token(own_keys(key_vis_ref) * weight)

    raw = gather_patches(me, (x0_ref, x1_ref, x2_ref, x3_ref), strips)
    copies[0].wait()
    patches = dot(raw, order[...]).astype(BF16)
    copies[1].wait()
    copies[2].wait()
    pair_rows = pl.ds(pl.multiple_of(token_row // 2 * 16, 16), 16)
    two = position[pair_rows, :].astype(F32)
    places = jnp.where(lax.rem(token_row, 2) == 0, two[:8], two[8:])
    places = jnp.broadcast_to(places[None], (8, 8, DP)).reshape(64, DP)
    embedded = dot(patches, patch[...]) + places
    centred = embedded - jnp.mean(embedded, axis=-1, keepdims=True)
    inverse = lax.rsqrt(jnp.mean(centred * centred, axis=-1, keepdims=True) + NORM_EPS)
    unit_rows = centred * inverse
    gain = gain_ref[...]
    normed_tokens = (unit_rows * gain).astype(BF16)

    for i in range(HID // 256):
        at = slice(256 * i, 256 * i + 256)
        value = dot(normed_tokens, up[:, at])
        hidden_pre[:, at] = value
        hidden[:, at] = (value * normal_cdf(value)).astype(BF16)

    block = dot(hidden[...], down[...])
    block_round = (embedded + block).astype(BF16)
    copies[3].wait()
    heatmap = dot_nt(block_round, head[...])
    heat_grad = ((heatmap - target) * mask).astype(BF16)
    out_grad = dot(heat_grad, head[...])
    out_round = out_grad.astype(BF16)

    for i in range(HID // 256):
        at = slice(256 * i, 256 * i + 256)
        grad = dot_nt(out_round, down[at, :])
        pre = hidden_pre[:, at]
        slope = normal_cdf(pre) + pre * jnp.exp(-0.5 * pre * pre) * 0.3989422804014327
        pre_grad[:, at] = (grad * slope).astype(BF16)

    normed_grad = dot_nt(pre_grad[...], up[...])
    unit_grad = normed_grad * gain
    embed_grad = out_grad + inverse * (
        unit_grad
        - jnp.mean(unit_grad, axis=-1, keepdims=True)
        - unit_rows * jnp.mean(unit_grad * unit_rows, axis=-1, keepdims=True)
    )
    colour_grad = dot_nt(embed_grad.astype(BF16), patch[...]).astype(BF16)
    outs = (out0_ref, out1_ref, out2_ref, out3_ref)
    scatter_patches(me, dot_nt(colour_grad, order[...]), strips, outs)


def pose(own, parts, frames, counts, key_rows, key_cols, key_vis, gain, up, down, patch, head, position):
    smem = pl.BlockSpec(memory_space=pltpu.SMEM)
    return pl.pallas_call(
        pose_kernel,
        in_specs=[smem] + [VMEM] * 13 + [ANYWHERE] * 4,
        out_specs=[VMEM] * GROUP,
        out_shape=[jax.ShapeDtypeStruct((8, 16, COLS), BF16)] * GROUP,
        scratch_shapes=[
            pltpu.VMEM((768, 768), BF16),
            pltpu.VMEM((768, DP), BF16),
            pltpu.VMEM((HEAD, DP), BF16),
            pltpu.VMEM((64, DP), BF16),
            pltpu.VMEM((GROUP, 8, 16, COLS), F32),
            pltpu.VMEM((32, HEAD), F32),
            pltpu.VMEM((64, HID), F32),
            pltpu.VMEM((64, HID), BF16),
            pltpu.VMEM((64, HID), BF16),
            pltpu.SemaphoreType.DMA((4,)),
        ],
        compiler_params=megabytes(20),
        cost_estimate=pl.CostEstimate(
            flops=2 * 64 * 15800000, bytes_accessed=17 * 1024 * 1024, transcendentals=64 * HID * 3
        ),
        name="pose",
    )(
        own,
        *parts,
        frames,
        counts,
        key_rows,
        key_cols,
        key_vis,
        jnp.asarray(KEY_SPREAD),
        gain,
        up,
        down,
        jnp.asarray(PIXEL_ORDER),
        patch,
        head,
        position,
    )


def strip_kernel(own_ref, x0_ref, x1_ref, x2_ref, x3_ref, out_ref, first_ref, last_ref):
    me = lax.rem(own_ref[0], GROUP)
    first = sublanes_of((8, 8, COLS)) < 4
    for turn, ref in enumerate((x0_ref, x1_ref, x2_ref, x3_ref)):
        frames = pl.ds(pl.multiple_of(lax.rem(me + GROUP - turn, GROUP) * 8, 8), 8)
        value = ref[...].astype(F32)
        groups = [value[:, :8], roll(value[:, :8], 4, 1), value[:, 8:]]
        for o in range(3):
            out_ref[frames, o] = roll(jnp.where(first, groups[o], 0.0), 1, 1)
    for o in range(3):
        first_ref[o] = out_ref[:, o, 1, :]
        last_ref[o] = out_ref[:, o, 4, :]


def strip_grads(own, parts):
    rim = jax.ShapeDtypeStruct((3, 32, COLS), F32)
    return pl.pallas_call(
        strip_kernel,
        in_specs=[pl.BlockSpec(memory_space=pltpu.SMEM)] + [VMEM] * GROUP,
        out_specs=[VMEM] * 3,
        out_shape=[jax.ShapeDtypeStruct((32, 3, 8, COLS), F32), rim, rim],
        compiler_params=megabytes(4),
        name="strip_grads",
    )(own, *parts)


def whole_kernel(x_ref, above_ref, below_ref, out_ref, first_ref):
    row = sublanes_of((32, 8, COLS))
    for o in range(3):
        value = jnp.where(row == 0, above_ref[o][:, None, :], x_ref[:, o])
        value = jnp.where(row == 5, below_ref[o][:, None, :], value)
        out_ref[:, o] = value
        first_ref[:, o] = value[:2]


def whole_grads(x, above, below):
    return pl.pallas_call(
        whole_kernel,
        in_specs=[VMEM] * 3,
        out_specs=[VMEM] * 2,
        out_shape=[
            jax.ShapeDtypeStruct(x.shape, F32),
            jax.ShapeDtypeStruct((2, 3, 8, COLS), F32),
        ],
        compiler_params=megabytes(4),
        name="whole_grads",
    )(x, above, below)


def frame_taps(groups):
    row = sublanes_of((8, COLS))
    taps = [from_right(g) for g in groups] + list(groups) + [from_left(g) for g in groups]
    last = taps.pop()
    for i in range(3):
        taps[i] = jnp.where(row >= 6, roll(last, 6 - 2 * i, 0), taps[i])
    return taps


def pair_taps(ref, frame):
    rows = []
    for f in range(2):
        rows += frame_taps([ref[frame + f, o] for o in range(3)])
    return jnp.concatenate(rows, axis=0).T


def back_pair(feat_ref, frame, taps, weight, half_gain, mean_pair, store):
    grads = dot(taps, weight)
    places = [(tau, r) for tau in range(2) for r in range(ROWS)]
    for part in range(0, len(places), BACK_ROWS):
        group = places[part : part + BACK_ROWS]
        xs = [feat_ref[frame + tau, r].astype(F32) for tau, r in group]
        means = channel_means([x * x for x in xs], mean_pair)
        kept = []
        for x, mean, (tau, r) in zip(xs, means, group):
            rescale = lax.rsqrt(mean + NORM_EPS)
            normed = x * rescale
            half_pre = normed * half_gain
            tanh = jnp.tanh(half_pre)
            slope = (1.0 + tanh) * (1.0 + half_pre * (1.0 - tanh)) * half_gain
            at = CH * (ROWS * tau + r)
            kept.append((rescale, normed, grads[:, at : at + CH] * slope))
        along = channel_means([scaled * normed for _, normed, scaled in kept], mean_pair)
        for (rescale, normed, scaled), mean, (tau, r) in zip(kept, along, group):
            store(tau, r, (rescale * (scaled - normed * mean)).astype(BF16))


def back_kernel(
    feat_ref, grad_ref, gain_ref, mean_ref, weight_ref, out_hbm, buffer, carry, sems
):
    half_gain = 0.5 * gain_ref[...]
    mean_pair = mean_ref[...]
    carry[...] = pair_taps(grad_ref, 0)
    steps = (feat_ref.shape[0] - 2) // BACK_FRAMES

    def copy_of(step, slot):
        rows = pl.ds(step * BACK_FRAMES, BACK_FRAMES)
        return pltpu.make_async_copy(buffer.at[slot], out_hbm.at[rows], sems.at[slot])

    @pl.loop(0, steps)
    def _(step):
        slot = lax.rem(step, 2)

        @pl.when(step >= 2)
        def _():
            copy_of(step - 2, slot).wait()

        for pair in range(BACK_FRAMES // 2):
            frame = step * BACK_FRAMES + 2 * pair
            now = carry[...]
            later = pair_taps(grad_ref, frame + 2)
            carry[...] = later
            taps = jnp.concatenate([now, later], axis=1).astype(BF16)

            def store(tau, r, value):
                buffer[slot, 2 * pair + tau, r] = value

            back_pair(feat_ref, frame, taps, weight_ref[...], half_gain, mean_pair, store)
        copy_of(step, slot).start()

    for step in range(max(steps - 2, 0), steps):
        copy_of(step, step % 2).wait()


def last_kernel(
    feat_ref, grad_ref, next_ref, gain_ref, mean_ref, weight_ref, prior_hbm, out_hbm, buffer, sem
):
    del prior_hbm
    frame = feat_ref.shape[0] - 2
    taps = jnp.concatenate([pair_taps(grad_ref, frame), pair_taps(next_ref, 0)], axis=1).astype(BF16)

    def store(tau, r, value):
        buffer[tau, r] = value

    back_pair(feat_ref, frame, taps, weight_ref[...], 0.5 * gain_ref[...], mean_ref[...], store)
    copy = pltpu.make_async_copy(buffer, out_hbm.at[frame:], sem)
    copy.start()
    copy.wait()


def conv_backward(features, grads, later, gain, weight):
    mean_pair = jnp.asarray(MEAN_PAIR)
    out_shape = jax.ShapeDtypeStruct(features.shape, BF16)
    part = pl.pallas_call(
        back_kernel,
        in_specs=[VMEM] * 5,
        out_specs=ANYWHERE,
        out_shape=out_shape,
        scratch_shapes=[
            pltpu.VMEM((2, BACK_FRAMES, ROWS, COLS, CH), BF16),
            pltpu.VMEM((COLS, 128), F32),
            pltpu.SemaphoreType.DMA((2,)),
        ],
        compiler_params=megabytes(16),
        cost_estimate=pl.CostEstimate(
            flops=2 * 16384 * 1024, bytes_accessed=9 * 1024 * 1024, transcendentals=2 * 2097152
        ),
        name="conv_back",
    )(features, grads, gain, mean_pair, weight)
    return pl.pallas_call(
        last_kernel,
        in_specs=[VMEM] * 6 + [ANYWHERE],
        out_specs=ANYWHERE,
        out_shape=out_shape,
        input_output_aliases={6: 0},
        scratch_shapes=[pltpu.VMEM((2, ROWS, COLS, CH), BF16), pltpu.SemaphoreType.DMA],
        compiler_params=megabytes(12),
        name="conv_last",
    )(features, grads, later, gain, mean_pair, weight, part)


def per_device(
    features,
    norm_gain,
    conv_weight,
    colour_bias,
    observed_frames,
    observed_counts,
    key_rows,
    key_columns,
    key_visible,
    position_table,
    patch_weight,
    layer_gain,
    up_weight,
    down_weight,
    head_weight,
):
    tm_count = lax.axis_size("tm")
    own = lax.axis_index("tile").reshape(1)
    gain = norm_gain.reshape(1, CH)
    features, layer_gain, own = lax.optimization_barrier(
        (features, layer_gain.reshape(1, DP), own)
    )
    features = pltpu.with_memory_space_constraint(features, pltpu.HBM)
    up_weight = pltpu.with_memory_space_constraint(up_weight, pltpu.HBM)
    down_weight = pltpu.with_memory_space_constraint(down_weight, pltpu.HBM)
    tail, features, weight, weight_t = conv_tail(features, gain, conv_weight.T)
    prior = lax.ppermute(tail, "tm", [(i, i + 1) for i in range(tm_count - 1)])
    sums, up, down = conv_main(features, gain, weight, up_weight, down_weight)
    above, below = to_neighbours(*rims(sums, prior))
    parts = swap_turns(colours(own, colour_bias, sums, prior, above, below))
    parts = pose(
        own,
        parts,
        observed_frames.transpose(2, 0, 1),
        observed_counts,
        key_rows.T,
        key_columns.T,
        key_visible.T,
        layer_gain,
        up,
        down,
        patch_weight,
        head_weight.T,
        position_table,
    )
    grads, first, last = strip_grads(own, swap_turns(parts))
    above, below = to_neighbours(first, last)
    grads, first = whole_grads(grads, above, below)
    later = lax.ppermute(first, "tm", [(i + 1, i) for i in range(tm_count - 1)])
    return conv_backward(features, grads, later, gain, weight_t)


def solution(mesh):
    in_specs = (
        P("tm", "tile", None, None),
        P(),
        P(),
        P(),
        P("tm", None, None),
        P("tm", None),
        P("tm", None),
        P("tm", None),
        P("tm", None),
        P(),
        P(),
        P(),
        P(),
        P(),
        P(),
    )
    return jax.shard_map(
        per_device,
        mesh=mesh,
        in_specs=in_specs,
        out_specs=P("tm", "tile", None, None),
        check_vma=False,
    )
```

time: 84.6 us -> 69.9 us (0.83)
  the two profiles are of different devices: /device:TPU:1 before, /device:TPU:99 now
where the time goes in v2:
time: 69.9 us; the launch traced here: 69.4 us
  Pallas kernels  29.5 us (42%)
  waiting for transfers between devices  17.4 us (25%)
  starting transfers between devices  16.9 us (24%)
  local copies, waits for them, and re-layouts  5.11 us (7%)
    pallas_call x1, Pallas kernels, pose(): pl.pallas_call(pose_kernel, in_specs=[smem] + [VMEM] * 13 + [ANYWHERE] *...  11.3 us
    ppermute x2, waiting for transfers between devices, to_neighbours(): below = lax.ppermute(up, 'tile', [(i + 1, i) for i in range(count - 1)])  10.5 us
    pallas_call x1, Pallas kernels, conv_backward(): pl.pallas_call(back_kernel, in_specs=[VMEM] * 5, out_specs=ANYWHERE, out_...  8.34 us
    ppermute x6, waiting for transfers between devices, swap_turns(): out.append(lax.ppermute(parts[turn], 'tile', pairs))  6.91 us
    pallas_call x1, Pallas kernels, conv_main(): pl.pallas_call(conv_kernel, in_specs=[VMEM] * 4 + [ANYWHERE] * 2, out_spe...  4.91 us
    ppermute x2, starting transfers between devices, to_neighbours(): above = lax.ppermute(down, 'tile', [(i, i + 1) for i in range(count - 1)])  4.64 us
    ppermute x2, starting transfers between devices, to_neighbours(): below = lax.ppermute(up, 'tile', [(i + 1, i) for i in range(count - 1)])  4.47 us
    unnamed x36, local copies, waits for them, and re-layouts  4.39 us
  transfers between devices with their start and end apart: 12, of which 7 were waited for; matrix products, arithmetic and copies ran while one was open for 0% of the time, Pallas kernels for 19%

profile of v2, /device:TPU:99, one launch (start us, length us, event | category | flops | bytes accessed | tf_op | source)
XLA Modules:
  0.0 69.4 jit_solution(2073780527052313790)
XLA Ops:
  0.0 0.7 %reshape.9.gain_ref = f32[1,1280]{1,0:T(1,128)S(1)} reshape(f32[1280]{0:T(1024)} %param.31) | data formatting | bytes 10240 | tf_op jit(solution)/shard_map/reshape | solution.py:711
  0.7 0.9 %copy-done = bf16[256,256]{1,0:T(8,128)(2,1)S(1)} copy-done((bf16[256,256]{1,0:T(8,128)(2,1)S(1)}, bf16[256,256]{1,0:T(8,128)(2,1)}, u32[]{:S(2)}) %copy-start) | copy-done | bytes 131096
  1.6 1.0 %copy-done.5 = bf16[2048,81]{1,0:T(8,128)(2,1)S(1)} copy-done((bf16[2048,81]{1,0:T(8,128)(2,1)S(1)}, bf16[2048,81]{1,0:T(8,128)(2,1)}, u32[]{:S(2)}) %copy-start.5) | copy-done | bytes 331800
  2.7 1.0 %copy-done.6 = bf16[81,2048]{1,0:T(8,128)(2,1)S(1)} copy-done((bf16[81,2048]{1,0:T(8,128)(2,1)S(1)}, bf16[81,2048]{1,0:T(8,128)(2,1)}, u32[]{:S(2)}) %copy-start.6) | copy-done | bytes 331800
  3.7 0.7 %copy-done.8 = bf16[128,81]{0,1:T(8,128)(2,1)S(1)} copy-done((bf16[128,81]{0,1:T(8,128)(2,1)S(1)}, bf16[128,81]{0,1:T(8,128)(2,1)}, u32[]{:S(2)}) %copy-start.8) | copy-done | bytes 20760
  5.0 2.5 %conv_tail.1 = (f32[2,3,8,128]{3,2,1,0:T(8,128)S(1)}, bf16[32,4,128,128]{3,2,1,0:T(8,128)(2,1)S(1)}, bf16[1024,256]{1,0:T(8,128)(2,1)S(1)}, bf16[256,1024]{1,0:T(8,128)(2,1)S(1)}) custom-call(bf16[32,4,128,128]{3,2,1,0:T(8,128)(2,1)} %feat_hbm, f32[1,128]{1,0:T(1,128)S(1)} %bitcast.13, bf16[256,256]{1,0:T(8,128)(2,1)S(1)} %copy-done, ...), custom_call_target="tpu_custom_call" | custom-call | tf_op jit(solution)/shard_map/conv_tail/pallas_call | solution.py:206
  7.5 3.1 %collective-permute-start = (f32[2,3,8,128]{3,2,1,0:T(8,128)S(1)}, f32[2,3,8,128]{3,2,1,0:T(8,128)S(1)}, u32[]{:S(2)}, u32[]{:S(2)}) collective-permute-start(f32[2,3,8,128]{3,2,1,0:T(8,128)S(1)} %get-tuple-element.35), channel_id=1, source_target_pairs={{0,1},{1,2},{2,3},{4,5},{5,6},{6,7},{8,9},{9,10},{10,11},{12,13},{... | collective-permute-start | bytes 73736 | tf_op jit(solution)/shard_map/ppermute | solution.py:717
  10.8 4.9 %conv_main.1 = (f32[32,3,8,128]{3,2,1,0:T(8,128)S(1)}, bf16[1280,2560]{1,0:T(8,128)(2,1)S(1)}, bf16[2560,1280]{1,0:T(8,128)(2,1)S(1)}) custom-call(bf16[32,4,128,128]{3,2,1,0:T(8,128)(2,1)S(1)} %get-tuple-element.31.feat_ref, f32[1,128]{1,0:T(1,128)S(1)} %bitcast.14, bf16[256,256]{1,0:T(8,128)(2,1)S(1)} %copy-done.1, ...), custom_call_target="tpu_custom_call" | custom-call | flops 33554432 | bytes 20971520 | tf_op jit(solution)/shard_map/conv_main/pallas_call | solution.py:230
  15.8 2.7 %collective-permute-start.1 = (f32[3,32,128]{2,1,0:T(8,128)S(1)}, f32[3,32,128]{2,1,0:T(8,128)S(1)}, u32[]{:S(2)}, u32[]{:S(2)}) collective-permute-start(f32[3,32,128]{2,1,0:T(8,128)S(1)} %get-tuple-element.36), channel_id=1, source_target_pairs={{0,4},{4,8},{8,12},{12,16},{16,20},{20,24},{24,28},{28,32},{32,36}... | collective-permute-start | bytes 147464 | tf_op jit(solution)/shard_map/ppermute | solution.py:315
  18.5 2.1 %collective-permute-start.2 = (f32[3,32,128]{2,1,0:T(8,128)S(1)}, f32[3,32,128]{2,1,0:T(8,128)S(1)}, u32[]{:S(2)}, u32[]{:S(2)}) collective-permute-start(f32[3,32,128]{2,1,0:T(8,128)S(1)} %get-tuple-element.37), channel_id=1, source_target_pairs={{4,0},{8,4},{12,8},{16,12},{20,16},{24,20},{28,24},{32,28},{36,32}... | collective-permute-start | bytes 147464 | tf_op jit(solution)/shard_map/ppermute | solution.py:316
  20.6 5.4 %collective-permute-done.2.below_ref = f32[3,32,128]{2,1,0:T(8,128)S(1)} collective-permute-done((f32[3,32,128]{2,1,0:T(8,128)S(1)}, f32[3,32,128]{2,1,0:T(8,128)S(1)}, u32[]{:S(2)}, u32[]{:S(2)}) %collective-permute-start.2) | collective-permute-done | bytes 49184 | tf_op jit(solution)/shard_map/ppermute | solution.py:316
  26.0 0.7 %colours.1 = (bf16[8,16,128]{2,1,0:T(8,128)(2,1)S(1)}, bf16[8,16,128]{2,1,0:T(8,128)(2,1)S(1)}, bf16[8,16,128]{2,1,0:T(8,128)(2,1)S(1)}, bf16[8,16,128]{2,1,0:T(8,128)(2,1)S(1)}) custom-call(s32[1]{0:T(128)} %bitcast.own_ref, f32[3]{0:T(128)S(1)} %copy-done.17, f32[32,3,8,128]{3,2,1,0:T(8,128)S(1)} %get-tuple-element.34.sums_ref, ...), custom_call_target="tpu_custom_call" | custom-call | tf_op jit(solution)/shard_map/colours/pallas_call | solution.py:293
  28.0 1.6 %collective-permute-done.4.x2_ref = bf16[8,16,128]{2,1,0:T(8,128)(2,1)S(1)} collective-permute-done((bf16[8,16,128]{2,1,0:T(8,128)(2,1)S(1)}, bf16[8,16,128]{2,1,0:T(8,128)(2,1)S(1)}, u32[]{:S(2)}, u32[]{:S(2)}) %collective-permute-start.4) | collective-permute-done | bytes 32800 | tf_op jit(solution)/shard_map/ppermute | solution.py:309
  29.7 1.2 %collective-permute-done.5.x3_ref = bf16[8,16,128]{2,1,0:T(8,128)(2,1)S(1)} collective-permute-done((bf16[8,16,128]{2,1,0:T(8,128)(2,1)S(1)}, bf16[8,16,128]{2,1,0:T(8,128)(2,1)S(1)}, u32[]{:S(2)}, u32[]{:S(2)}) %collective-permute-start.5) | collective-permute-done | bytes 32800 | tf_op jit(solution)/shard_map/ppermute | solution.py:309
  31.0 11.3 %pose.1 = (bf16[8,16,128]{2,1,0:T(8,128)(2,1)S(1)}, bf16[8,16,128]{2,1,0:T(8,128)(2,1)S(1)}, bf16[8,16,128]{2,1,0:T(8,128)(2,1)S(1)}, bf16[8,16,128]{2,1,0:T(8,128)(2,1)S(1)}) custom-call(s32[1]{0:T(128)} %bitcast.own_ref, bf16[8,16,128]{2,1,0:T(8,128)(2,1)S(1)} %get-tuple-element.38.x0_ref, bf16[8,16,128]{2,1,0:T(8,128)(2,1)S(1)} %collective-permute-done.3.x1_ref, ...), custom_call_target="tpu_custom_call" | custom-call | flops 2022400000 | bytes 17825792 | tf_op jit(solution)/shard_map/pose/pallas_call | solution.py:479
  42.4 1.7 %collective-permute-start.7 = (bf16[8,16,128]{2,1,0:T(8,128)(2,1)S(1)}, bf16[8,16,128]{2,1,0:T(8,128)(2,1)S(1)}, u32[]{:S(2)}, u32[]{:S(2)}) collective-permute-start(bf16[8,16,128]{2,1,0:T(8,128)(2,1)S(1)} %get-tuple-element.47), channel_id=1, source_target_pairs={{0,8},{4,12},{8,0},{12,4},{16,24},{20,28},{24,16},{28,20},{32,40},... | collective-permute-start | bytes 98312 | tf_op jit(solution)/shard_map/ppermute | solution.py:309
  44.1 1.6 %collective-permute-done.7.x2_ref = bf16[8,16,128]{2,1,0:T(8,128)(2,1)S(1)} collective-permute-done((bf16[8,16,128]{2,1,0:T(8,128)(2,1)S(1)}, bf16[8,16,128]{2,1,0:T(8,128)(2,1)S(1)}, u32[]{:S(2)}, u32[]{:S(2)}) %collective-permute-start.7) | collective-permute-done | bytes 32800 | tf_op jit(solution)/shard_map/ppermute | solution.py:309
  45.7 1.7 %collective-permute-done.8.x3_ref = bf16[8,16,128]{2,1,0:T(8,128)(2,1)S(1)} collective-permute-done((bf16[8,16,128]{2,1,0:T(8,128)(2,1)S(1)}, bf16[8,16,128]{2,1,0:T(8,128)(2,1)S(1)}, u32[]{:S(2)}, u32[]{:S(2)}) %collective-permute-start.8) | collective-permute-done | bytes 32800 | tf_op jit(solution)/shard_map/ppermute | solution.py:309
  47.5 2.0 %collective-permute-start.9 = (f32[3,32,128]{2,1,0:T(8,128)S(1)}, f32[3,32,128]{2,1,0:T(8,128)S(1)}, u32[]{:S(2)}, u32[]{:S(2)}) collective-permute-start(f32[3,32,128]{2,1,0:T(8,128)S(1)} %get-tuple-element.50), channel_id=1, source_target_pairs={{0,4},{4,8},{8,12},{12,16},{16,20},{20,24},{24,28},{28,32},{32,36}... | collective-permute-start | bytes 147464 | tf_op jit(solution)/shard_map/ppermute | solution.py:315
  49.5 2.4 %collective-permute-start.10 = (f32[3,32,128]{2,1,0:T(8,128)S(1)}, f32[3,32,128]{2,1,0:T(8,128)S(1)}, u32[]{:S(2)}, u32[]{:S(2)}) collective-permute-start(f32[3,32,128]{2,1,0:T(8,128)S(1)} %get-tuple-element.51), channel_id=1, source_target_pairs={{4,0},{8,4},{12,8},{16,12},{20,16},{24,20},{28,24},{32,28},{36,32}... | collective-permute-start | bytes 147464 | tf_op jit(solution)/shard_map/ppermute | solution.py:316
  51.8 5.1 %collective-permute-done.10.below_ref = f32[3,32,128]{2,1,0:T(8,128)S(1)} collective-permute-done((f32[3,32,128]{2,1,0:T(8,128)S(1)}, f32[3,32,128]{2,1,0:T(8,128)S(1)}, u32[]{:S(2)}, u32[]{:S(2)}) %collective-permute-start.10) | collective-permute-done | bytes 49184 | tf_op jit(solution)/shard_map/ppermute | solution.py:316
  57.1 2.3 %collective-permute-start.11 = (f32[2,3,8,128]{3,2,1,0:T(8,128)S(1)}, f32[2,3,8,128]{3,2,1,0:T(8,128)S(1)}, u32[]{:S(2)}, u32[]{:S(2)}) collective-permute-start(f32[2,3,8,128]{3,2,1,0:T(8,128)S(1)} %get-tuple-element.53), channel_id=1, source_target_pairs={{1,0},{2,1},{3,2},{5,4},{6,5},{7,6},{9,8},{10,9},{11,10},{13,12},{... | collective-permute-start | bytes 73736 | tf_op jit(solution)/shard_map/ppermute | solution.py:739
  59.4 8.3 %conv_back.1.prior_hbm = bf16[32,4,128,128]{3,2,1,0:T(8,128)(2,1)} custom-call(bf16[32,4,128,128]{3,2,1,0:T(8,128)(2,1)S(1)} %get-tuple-element.31.feat_ref, f32[32,3,8,128]{3,2,1,0:T(8,128)S(1)} %get-tuple-element.52.grad_ref, f32[1,128]{1,0:T(1,128)S(1)} %bitcast.15, bf16[256,256]{1,0:T(8,128)(2,1)S(1)} %copy-done.1, ...), custom_call_target="tpu_custom_call" | custom-call | flops 33554432 | bytes 9437184 | tf_op jit(solution)/shard_map/conv_back/pallas_call | solution.py:662
  67.8 1.4 %conv_last.1 = bf16[32,4,128,128]{3,2,1,0:T(8,128)(2,1)} custom-call(bf16[32,4,128,128]{3,2,1,0:T(8,128)(2,1)S(1)} %get-tuple-element.31.feat_ref, f32[32,3,8,128]{3,2,1,0:T(8,128)S(1)} %get-tuple-element.52.grad_ref, f32[2,3,8,128]{3,2,1,0:T(8,128)S(1)} %collective-permute-done.11.next_ref, f32[1,128]{1,0:T(1,128)S(1)} %bitcast.16, ...), custom_call_target="tpu_custom_call", output_to_operand_aliasing={{}: (6, {})} | custom-call | tf_op jit(solution)/shard_map/conv_last/pallas_call | solution.py:678
  (46 shorter events, 2.3 us)
Async XLA Ops:
  0.0 10.7 %copy-start.14 = (f32[128]{0:T(128)S(1)}, f32[128]{0:T(128)}, u32[]{:S(2)}) copy-start(f32[128]{0:T(128)} %param.21) | copy-start | bytes 1540
  7.5 8.2 %collective-permute-start = (f32[2,3,8,128]{3,2,1,0:T(8,128)S(1)}, f32[2,3,8,128]{3,2,1,0:T(8,128)S(1)}, u32[]{:S(2)}, u32[]{:S(2)}) collective-permute-start(f32[2,3,8,128]{3,2,1,0:T(8,128)S(1)} %get-tuple-element.35), channel_id=1, source_target_pairs={{0,1},{1,2},{2,3},{4,5},{5,6},{6,7},{8,9},{9,10},{10,11},{12,13},{... | collective-permute-start | bytes 73736 | tf_op jit(solution)/shard_map/ppermute | solution.py:717
  10.7 15.3 %copy-start.17 = (f32[3]{0:T(128)S(1)}, f32[3]{0:T(128)}, u32[]{:S(2)}) copy-start(f32[3]{0:T(128)} %bias_ref.1) | copy-start | bytes 40
  10.7 20.2 %copy-start.2 = (bf16[768,1280]{1,0:T(8,128)(2,1)S(1)}, bf16[768,1280]{1,0:T(8,128)(2,1)}, u32[]{:S(2)}) copy-start(bf16[768,1280]{1,0:T(8,128)(2,1)} %patch_hbm.1) | copy-start | bytes 5898244
  10.7 20.2 %copy-start.3 = (bf16[768,768]{1,0:T(8,128)(2,1)S(1)}, bf16[768,768]{1,0:T(8,128)(2,1)}, u32[]{:S(2)}) copy-start(bf16[768,768]{1,0:T(8,128)(2,1)} %constant.20.clone.order_hbm) | copy-start | bytes 3538948
  10.7 20.2 %copy-start.4 = (bf16[1280,272]{0,1:T(8,128)(2,1)S(1)}, bf16[1280,272]{0,1:T(8,128)(2,1)}, u32[]{:S(2)}) copy-start(bf16[1280,272]{0,1:T(8,128)(2,1)} %param.34) | copy-start | bytes 2088964
  10.7 20.2 %copy-start.7 = (bf16[64,1280]{1,0:T(8,128)(2,1)S(1)}, bf16[64,1280]{1,0:T(8,128)(2,1)}, u32[]{:S(2)}) copy-start(bf16[64,1280]{1,0:T(8,128)(2,1)} %position_hbm.1) | copy-start | bytes 491524
  10.7 20.2 %copy-start.9 = (bf16[17,272]{1,0:T(8,128)(2,1)S(1)}, bf16[17,272]{1,0:T(8,128)(2,1)}, u32[]{:S(2)}) copy-start(bf16[17,272]{1,0:T(8,128)(2,1)} %constant.19.clone.key_spread_ref) | copy-start | bytes 27748
  10.8 20.2 %copy-start.10 = (s32[32,17]{0,1:T(8,128)S(1)}, s32[32,17]{0,1:T(8,128)}, u32[]{:S(2)}) copy-start(s32[32,17]{0,1:T(8,128)} %param.26) | copy-start | bytes 6532
  10.8 20.2 %copy-start.11 = (s32[32,17]{0,1:T(8,128)S(1)}, s32[32,17]{0,1:T(8,128)}, u32[]{:S(2)}) copy-start(s32[32,17]{0,1:T(8,128)} %param.27) | copy-start | bytes 6532
  10.8 20.2 %copy-start.12 = (s32[32,17]{0,1:T(8,128)S(1)}, s32[32,17]{0,1:T(8,128)}, u32[]{:S(2)}) copy-start(s32[32,17]{0,1:T(8,128)} %param.28) | copy-start | bytes 6532
  10.8 20.2 %copy-start.15 = (s32[1,32,3]{1,0,2:T(1,128)S(1)}, s32[1,32,3]{1,0,2:T(1,128)}, u32[]{:S(2)}) copy-start(s32[1,32,3]{1,0,2:T(1,128)} %param.24) | copy-start | bytes 1156
  10.8 20.2 %copy-start.16 = (s32[1,32]{1,0:T(1,128)S(1)}, s32[1,32]{1,0:T(1,128)}, u32[]{:S(2)}) copy-start(s32[1,32]{1,0:T(1,128)} %counts_ref.1) | copy-start | bytes 388
  15.8 4.8 %collective-permute-start.1 = (f32[3,32,128]{2,1,0:T(8,128)S(1)}, f32[3,32,128]{2,1,0:T(8,128)S(1)}, u32[]{:S(2)}, u32[]{:S(2)}) collective-permute-start(f32[3,32,128]{2,1,0:T(8,128)S(1)} %get-tuple-element.36), channel_id=1, source_target_pairs={{0,4},{4,8},{8,12},{12,16},{16,20},{20,24},{24,28},{28,32},{32,36}... | collective-permute-start | bytes 147464 | tf_op jit(solution)/shard_map/ppermute | solution.py:315
  18.5 7.5 %collective-permute-start.2 = (f32[3,32,128]{2,1,0:T(8,128)S(1)}, f32[3,32,128]{2,1,0:T(8,128)S(1)}, u32[]{:S(2)}, u32[]{:S(2)}) collective-permute-start(f32[3,32,128]{2,1,0:T(8,128)S(1)} %get-tuple-element.37), channel_id=1, source_target_pairs={{4,0},{8,4},{12,8},{16,12},{20,16},{24,20},{28,24},{32,28},{36,32}... | collective-permute-start | bytes 147464 | tf_op jit(solution)/shard_map/ppermute | solution.py:316
  26.8 1.3 %collective-permute-start.3 = (bf16[8,16,128]{2,1,0:T(8,128)(2,1)S(1)}, bf16[8,16,128]{2,1,0:T(8,128)(2,1)S(1)}, u32[]{:S(2)}, u32[]{:S(2)}) collective-permute-start(bf16[8,16,128]{2,1,0:T(8,128)(2,1)S(1)} %get-tuple-element.39), channel_id=1, source_target_pairs={{0,4},{4,8},{8,12},{12,0},{16,20},{20,24},{24,28},{28,16},{32,36},... | collective-permute-start | bytes 98312 | tf_op jit(solution)/shard_map/ppermute | solution.py:309
  26.8 2.8 %collective-permute-start.4 = (bf16[8,16,128]{2,1,0:T(8,128)(2,1)S(1)}, bf16[8,16,128]{2,1,0:T(8,128)(2,1)S(1)}, u32[]{:S(2)}, u32[]{:S(2)}) collective-permute-start(bf16[8,16,128]{2,1,0:T(8,128)(2,1)S(1)} %get-tuple-element.40), channel_id=1, source_target_pairs={{0,8},{4,12},{8,0},{12,4},{16,24},{20,28},{24,16},{28,20},{32,40},... | collective-permute-start | bytes 98312 | tf_op jit(solution)/shard_map/ppermute | solution.py:309
  26.9 4.0 %collective-permute-start.5 = (bf16[8,16,128]{2,1,0:T(8,128)(2,1)S(1)}, bf16[8,16,128]{2,1,0:T(8,128)(2,1)S(1)}, u32[]{:S(2)}, u32[]{:S(2)}) collective-permute-start(bf16[8,16,128]{2,1,0:T(8,128)(2,1)S(1)} %get-tuple-element.41), channel_id=1, source_target_pairs={{0,12},{4,0},{8,4},{12,8},{16,28},{20,16},{24,20},{28,24},{32,44},... | collective-permute-start | bytes 98312 | tf_op jit(solution)/shard_map/ppermute | solution.py:309
  42.3 1.8 %collective-permute-start.6 = (bf16[8,16,128]{2,1,0:T(8,128)(2,1)S(1)}, bf16[8,16,128]{2,1,0:T(8,128)(2,1)S(1)}, u32[]{:S(2)}, u32[]{:S(2)}) collective-permute-start(bf16[8,16,128]{2,1,0:T(8,128)(2,1)S(1)} %get-tuple-element.46), channel_id=1, source_target_pairs={{0,4},{4,8},{8,12},{12,0},{16,20},{20,24},{24,28},{28,16},{32,36},... | collective-permute-start | bytes 98312 | tf_op jit(solution)/shard_map/ppermute | solution.py:309
  42.4 3.3 %collective-permute-start.7 = (bf16[8,16,128]{2,1,0:T(8,128)(2,1)S(1)}, bf16[8,16,128]{2,1,0:T(8,128)(2,1)S(1)}, u32[]{:S(2)}, u32[]{:S(2)}) collective-permute-start(bf16[8,16,128]{2,1,0:T(8,128)(2,1)S(1)} %get-tuple-element.47), channel_id=1, source_target_pairs={{0,8},{4,12},{8,0},{12,4},{16,24},{20,28},{24,16},{28,20},{32,40},... | collective-permute-start | bytes 98312 | tf_op jit(solution)/shard_map/ppermute | solution.py:309
  44.1 3.3 %collective-permute-start.8 = (bf16[8,16,128]{2,1,0:T(8,128)(2,1)S(1)}, bf16[8,16,128]{2,1,0:T(8,128)(2,1)S(1)}, u32[]{:S(2)}, u32[]{:S(2)}) collective-permute-start(bf16[8,16,128]{2,1,0:T(8,128)(2,1)S(1)} %get-tuple-element.48), channel_id=1, source_target_pairs={{0,12},{4,0},{8,4},{12,8},{16,28},{20,16},{24,20},{28,24},{32,44},... | collective-permute-start | bytes 98312 | tf_op jit(solution)/shard_map/ppermute | solution.py:309
  47.5 4.3 %collective-permute-start.9 = (f32[3,32,128]{2,1,0:T(8,128)S(1)}, f32[3,32,128]{2,1,0:T(8,128)S(1)}, u32[]{:S(2)}, u32[]{:S(2)}) collective-permute-start(f32[3,32,128]{2,1,0:T(8,128)S(1)} %get-tuple-element.50), channel_id=1, source_target_pairs={{0,4},{4,8},{8,12},{12,16},{16,20},{20,24},{24,28},{28,32},{32,36}... | collective-permute-start | bytes 147464 | tf_op jit(solution)/shard_map/ppermute | solution.py:315
  49.5 7.5 %collective-permute-start.10 = (f32[3,32,128]{2,1,0:T(8,128)S(1)}, f32[3,32,128]{2,1,0:T(8,128)S(1)}, u32[]{:S(2)}, u32[]{:S(2)}) collective-permute-start(f32[3,32,128]{2,1,0:T(8,128)S(1)} %get-tuple-element.51), channel_id=1, source_target_pairs={{4,0},{8,4},{12,8},{16,12},{20,16},{24,20},{28,24},{32,28},{36,32}... | collective-permute-start | bytes 147464 | tf_op jit(solution)/shard_map/ppermute | solution.py:316
  57.1 10.7 %collective-permute-start.11 = (f32[2,3,8,128]{3,2,1,0:T(8,128)S(1)}, f32[2,3,8,128]{3,2,1,0:T(8,128)S(1)}, u32[]{:S(2)}, u32[]{:S(2)}) collective-permute-start(f32[2,3,8,128]{3,2,1,0:T(8,128)S(1)} %get-tuple-element.53), channel_id=1, source_target_pairs={{1,0},{2,1},{3,2},{5,4},{6,5},{7,6},{9,8},{10,9},{11,10},{13,12},{... | collective-permute-start | bytes 73736 | tf_op jit(solution)/shard_map/ppermute | solution.py:739
  (6 other events, 9.9 us)

commit v3 on v2

--- a/solution.py
+++ b/solution.py
@@ -145,14 +145,31 @@
 
 
 def tail_kernel(
-    feat_hbm, gain_ref, mean_ref, conv_ref, sel_ref, sel_t_ref,
-    out_ref, feat_ref, weight_ref, weight_t_ref, sems,
+    feat_hbm, gain_hbm, mean_hbm, conv_hbm, sel_hbm, sel_t_hbm,
+    out_ref, feat_ref, weight_ref, weight_t_ref, mean_ref, gain_ref,
+    conv_ref, sel_ref, sel_t_ref, sems,
 ):
     frames = feat_hbm.shape[0]
     last = pltpu.make_async_copy(feat_hbm.at[frames - 2 :], feat_ref.at[frames - 2 :], sems.at[0])
     rest = pltpu.make_async_copy(feat_hbm.at[: frames - 2], feat_ref.at[: frames - 2], sems.at[1])
+    small = [
+        pltpu.make_async_copy(src, dst, sems.at[2 + i])
+        for i, (src, dst) in enumerate(
+            (
+                (conv_hbm, conv_ref),
+                (sel_hbm, sel_ref),
+                (sel_t_hbm, sel_t_ref),
+                (gain_hbm, gain_ref),
+                (mean_hbm, mean_ref),
+            )
+        )
+    ]
+    for copy in small:
+        copy.start()
     last.start()
     rest.start()
+    for copy in small:
+        copy.wait()
     conv = conv_ref[...]
     for i in range(8):
         at = slice(CH * i, CH * i + CH)
@@ -195,6 +212,7 @@
 
 
 VMEM = pl.BlockSpec(memory_space=pltpu.VMEM)
+SMEM = pl.BlockSpec(memory_space=pltpu.SMEM)
 ANYWHERE = pl.BlockSpec(memory_space=pl.ANY)
 
 
@@ -202,31 +220,33 @@
     return pltpu.CompilerParams(vmem_limit_bytes=count * 1024 * 1024)
 
 
-def conv_tail(features, gain, conv_weight):
+def conv_tail(features, *small):
     return pl.pallas_call(
         tail_kernel,
-        in_specs=[ANYWHERE] + [VMEM] * 5,
-        out_specs=[VMEM] * 4,
+        in_specs=[ANYWHERE] * 6,
+        out_specs=[VMEM] * 6,
         out_shape=[
             jax.ShapeDtypeStruct((2, 3, 8, COLS), F32),
             pltpu.VMEM(features.shape, BF16),
             pltpu.VMEM((1024, 256), BF16),
             pltpu.VMEM((256, 1024), BF16),
+            pltpu.VMEM((256, 256), BF16),
+            pltpu.VMEM((1, CH), F32),
         ],
-        scratch_shapes=[pltpu.SemaphoreType.DMA((2,))],
+        scratch_shapes=[
+            pltpu.VMEM((81, CH), BF16),
+            pltpu.VMEM((81, 2048), BF16),
+            pltpu.VMEM((2048, 81), BF16),
+            pltpu.SemaphoreType.DMA((7,)),
+        ],
         compiler_params=megabytes(8),
         name="conv_tail",
     )(
-        features,
-        gain,
-        jnp.asarray(MEAN_PAIR),
-        conv_weight,
-        jnp.asarray(SELECTOR),
-        jnp.asarray(SELECTOR_T),
-    )
-
-
-def conv_main(features, gain, weight, up, down):
+        features, *small
+    )
+
+
+def conv_main(features, gain, mean_pair, weight, up, down):
     return pl.pallas_call(
         conv_kernel,
         in_specs=[VMEM] * 4 + [ANYWHERE] * 2,
@@ -242,7 +262,7 @@
             flops=2 * 16384 * 1024, bytes_accessed=20 * 1024 * 1024, transcendentals=2 * 2097152
         ),
         name="conv_main",
-    )(features, gain, jnp.asarray(MEAN_PAIR), weight, up, down)
+    )(features, gain, mean_pair, weight, up, down)
 
 
 def lay_rows(groups):
@@ -251,29 +271,35 @@
     return jnp.concatenate([both, groups[2]], axis=1)
 
 
-def rim_kernel(sums_ref, prior_ref, up_ref, down_ref):
+def unless(is_edge, value):
+    return jnp.where(is_edge, jnp.zeros_like(value), value)
+
+
+def rim_kernel(place_ref, sums_ref, prior_ref, up_ref, down_ref):
+    first_block = place_ref[1] == 0
     for o in range(3):
         for k, out_ref in ((0, up_ref), (5, down_ref)):
             out_ref[o] = sums_ref[:, o, k, :]
-            out_ref[o, 0:2] = sums_ref[0:2, o, k, :] + prior_ref[:, o, k, :]
-
-
-def rims(sums, prior):
+            out_ref[o, 0:2] = sums_ref[0:2, o, k, :] + unless(first_block, prior_ref[:, o, k, :])
+
+
+def rims(place, sums, prior):
     shape = jax.ShapeDtypeStruct((3, sums.shape[0], COLS), F32)
     return pl.pallas_call(
         rim_kernel,
-        in_specs=[VMEM] * 2,
+        in_specs=[SMEM] + [VMEM] * 2,
         out_specs=[VMEM] * 2,
         out_shape=[shape] * 2,
         compiler_params=megabytes(4),
         name="rims",
-    )(sums, prior)
+    )(place, sums, prior)
 
 
 def colour_kernel(own_ref, bias_ref, sums_ref, prior_ref, above_ref, below_ref, *rest):
     out_refs, total = rest[:GROUP], rest[GROUP]
     total[...] = sums_ref[...]
-    total[0:2] = sums_ref[0:2] + prior_ref[...]
+    total[0:2] = sums_ref[0:2] + unless(own_ref[1] == 0, prior_ref[...])
+    top, bottom = own_ref[0] == 0, own_ref[0] == own_ref[2] - 1
     row = sublanes_of((8, 8, COLS))
     me = lax.rem(own_ref[0], GROUP)
     for turn in range(GROUP):
@@ -281,18 +307,17 @@
         groups = []
         for o in range(3):
             value = total[frames, o]
-            value += jnp.where(row == 1, above_ref[o, frames, :][:, None, :], 0.0)
-            value += jnp.where(row == 4, below_ref[o, frames, :][:, None, :], 0.0)
+            value += jnp.where(row == 1, unless(top, above_ref[o, frames, :])[:, None, :], 0.0)
+            value += jnp.where(row == 4, unless(bottom, below_ref[o, frames, :])[:, None, :], 0.0)
             groups.append(roll(value, -1, 1) + bias_ref[o])
         out_refs[turn][...] = lay_rows(groups).astype(BF16)
 
 
 def colours(own, bias, sums, prior, above, below):
-    smem = pl.BlockSpec(memory_space=pltpu.SMEM)
     shape = jax.ShapeDtypeStruct((8, 16, COLS), BF16)
     return pl.pallas_call(
         colour_kernel,
-        in_specs=[smem] * 2 + [VMEM] * 4,
+        in_specs=[SMEM] * 2 + [VMEM] * 4,
         out_specs=[VMEM] * GROUP,
         out_shape=[shape] * GROUP,
         scratch_shapes=[pltpu.VMEM(sums.shape, F32)],
@@ -312,8 +337,8 @@
 
 def to_neighbours(up, down):
     count = lax.axis_size("tile")
-    above = lax.ppermute(down, "tile", [(i, i + 1) for i in range(count - 1)])
-    below = lax.ppermute(up, "tile", [(i + 1, i) for i in range(count - 1)])
+    above = lax.ppermute(down, "tile", [(i, (i + 1) % count) for i in range(count)])
+    below = lax.ppermute(up, "tile", [((i + 1) % count, i) for i in range(count)])
     return above, below
 
 
@@ -438,7 +463,7 @@
     centred = embedded - jnp.mean(embedded, axis=-1, keepdims=True)
     inverse = lax.rsqrt(jnp.mean(centred * centred, axis=-1, keepdims=True) + NORM_EPS)
     unit_rows = centred * inverse
-    gain = gain_ref[...]
+    gain = jnp.concatenate([gain_ref[i : i + 1] for i in range(DP // 128)], axis=1)
     normed_tokens = (unit_rows * gain).astype(BF16)
 
     for i in range(HID // 256):
@@ -475,10 +500,9 @@
 
 
 def pose(own, parts, frames, counts, key_rows, key_cols, key_vis, gain, up, down, patch, head, position):
-    smem = pl.BlockSpec(memory_space=pltpu.SMEM)
     return pl.pallas_call(
         pose_kernel,
-        in_specs=[smem] + [VMEM] * 13 + [ANYWHERE] * 4,
+        in_specs=[SMEM] + [VMEM] * 13 + [ANYWHERE] * 4,
         out_specs=[VMEM] * GROUP,
         out_shape=[jax.ShapeDtypeStruct((8, 16, COLS), BF16)] * GROUP,
         scratch_shapes=[
@@ -535,7 +559,7 @@
     rim = jax.ShapeDtypeStruct((3, 32, COLS), F32)
     return pl.pallas_call(
         strip_kernel,
-        in_specs=[pl.BlockSpec(memory_space=pltpu.SMEM)] + [VMEM] * GROUP,
+        in_specs=[SMEM] + [VMEM] * GROUP,
         out_specs=[VMEM] * 3,
         out_shape=[jax.ShapeDtypeStruct((32, 3, 8, COLS), F32), rim, rim],
         compiler_params=megabytes(4),
@@ -543,19 +567,20 @@
     )(own, *parts)
 
 
-def whole_kernel(x_ref, above_ref, below_ref, out_ref, first_ref):
+def whole_kernel(place_ref, x_ref, above_ref, below_ref, out_ref, first_ref):
     row = sublanes_of((32, 8, COLS))
+    top, bottom = place_ref[0] == 0, place_ref[0] == place_ref[2] - 1
     for o in range(3):
-        value = jnp.where(row == 0, above_ref[o][:, None, :], x_ref[:, o])
-        value = jnp.where(row == 5, below_ref[o][:, None, :], value)
+        value = jnp.where(row == 0, unless(top, above_ref[o])[:, None, :], x_ref[:, o])
+        value = jnp.where(row == 5, unless(bottom, below_ref[o])[:, None, :], value)
         out_ref[:, o] = value
         first_ref[:, o] = value[:2]
 
 
-def whole_grads(x, above, below):
+def whole_grads(place, x, above, below):
     return pl.pallas_call(
         whole_kernel,
-        in_specs=[VMEM] * 3,
+        in_specs=[SMEM] + [VMEM] * 3,
         out_specs=[VMEM] * 2,
         out_shape=[
             jax.ShapeDtypeStruct(x.shape, F32),
@@ -563,7 +588,7 @@
         ],
         compiler_params=megabytes(4),
         name="whole_grads",
-    )(x, above, below)
+    )(place, x, above, below)
 
 
 def frame_taps(groups):
@@ -641,11 +666,13 @@
 
 
 def last_kernel(
-    feat_ref, grad_ref, next_ref, gain_ref, mean_ref, weight_ref, prior_hbm, out_hbm, buffer, sem
+    place_ref, feat_ref, grad_ref, next_ref, gain_ref, mean_ref, weight_ref, prior_hbm, out_hbm, buffer, sem
 ):
     del prior_hbm
     frame = feat_ref.shape[0] - 2
-    taps = jnp.concatenate([pair_taps(grad_ref, frame), pair_taps(next_ref, 0)], axis=1).astype(BF16)
+    last_block = place_ref[1] == place_ref[3] - 1
+    later = unless(last_block, pair_taps(next_ref, 0))
+    taps = jnp.concatenate([pair_taps(grad_ref, frame), later], axis=1).astype(BF16)
 
     def store(tau, r, value):
         buffer[tau, r] = value
@@ -656,8 +683,7 @@
     copy.wait()
 
 
-def conv_backward(features, grads, later, gain, weight):
-    mean_pair = jnp.asarray(MEAN_PAIR)
+def conv_backward(place, features, grads, later, gain, mean_pair, weight):
     out_shape = jax.ShapeDtypeStruct(features.shape, BF16)
     part = pl.pallas_call(
         back_kernel,
@@ -677,14 +703,14 @@
     )(features, grads, gain, mean_pair, weight)
     return pl.pallas_call(
         last_kernel,
-        in_specs=[VMEM] * 6 + [ANYWHERE],
+        in_specs=[SMEM] + [VMEM] * 6 + [ANYWHERE],
         out_specs=ANYWHERE,
         out_shape=out_shape,
-        input_output_aliases={6: 0},
+        input_output_aliases={7: 0},
         scratch_shapes=[pltpu.VMEM((2, ROWS, COLS, CH), BF16), pltpu.SemaphoreType.DMA],
         compiler_params=megabytes(12),
         name="conv_last",
-    )(features, grads, later, gain, mean_pair, weight, part)
+    )(place, features, grads, later, gain, mean_pair, weight, part)
 
 
 def per_device(
@@ -705,18 +731,31 @@
     head_weight,
 ):
     tm_count = lax.axis_size("tm")
-    own = lax.axis_index("tile").reshape(1)
+    own = jnp.stack(
+        [
+            lax.axis_index("tile"),
+            lax.axis_index("tm"),
+            jnp.int32(lax.axis_size("tile")),
+            jnp.int32(tm_count),
+        ]
+    )
     gain = norm_gain.reshape(1, CH)
     features, layer_gain, own = lax.optimization_barrier(
-        (features, layer_gain.reshape(1, DP), own)
+        (features, layer_gain.reshape(DP // 128, 128), own)
     )
     features = pltpu.with_memory_space_constraint(features, pltpu.HBM)
     up_weight = pltpu.with_memory_space_constraint(up_weight, pltpu.HBM)
     down_weight = pltpu.with_memory_space_constraint(down_weight, pltpu.HBM)
-    tail, features, weight, weight_t = conv_tail(features, gain, conv_weight.T)
-    prior = lax.ppermute(tail, "tm", [(i, i + 1) for i in range(tm_count - 1)])
-    sums, up, down = conv_main(features, gain, weight, up_weight, down_weight)
-    above, below = to_neighbours(*rims(sums, prior))
+    gain = pltpu.with_memory_space_constraint(gain, pltpu.HBM)
+    consts = [jnp.asarray(x) for x in (MEAN_PAIR, SELECTOR, SELECTOR_T)]
+    mean_pair, sel, sel_t = [pltpu.with_memory_space_constraint(x, pltpu.HBM) for x in consts]
+    conv_weight = pltpu.with_memory_space_constraint(conv_weight.T, pltpu.HBM)
+    tail, features, weight, weight_t, mean_pair, gain = conv_tail(
+        features, gain, mean_pair, conv_weight, sel, sel_t
+    )
+    prior = lax.ppermute(tail, "tm", [(i, (i + 1) % tm_count) for i in range(tm_count)])
+    sums, up, down = conv_main(features, gain, mean_pair, weight, up_weight, down_weight)
+    above, below = to_neighbours(*rims(own, sums, prior))
     parts = swap_turns(colours(own, colour_bias, sums, prior, above, below))
     parts = pose(
         own,
@@ -735,9 +774,9 @@
     )
     grads, first, last = strip_grads(own, swap_turns(parts))
     above, below = to_neighbours(first, last)
-    grads, first = whole_grads(grads, above, below)
-    later = lax.ppermute(first, "tm", [(i + 1, i) for i in range(tm_count - 1)])
-    return conv_backward(features, grads, later, gain, weight_t)
+    grads, first = whole_grads(own, grads, above, below)
+    later = lax.ppermute(first, "tm", [((i + 1) % tm_count, i) for i in range(tm_count)])
+    return conv_backward(own, features, grads, later, gain, mean_pair, weight_t)
 
 
 def solution(mesh):

time: 69.9 us -> 60.3 us (0.86)
  the two profiles are of different devices: /device:TPU:99 before, /device:TPU:0 now
where the time goes in v3:
time: 60.3 us; the launch traced here: 60.2 us
  Pallas kernels  32.3 us (54%)
  starting transfers between devices  19.2 us (32%)
  waiting for transfers between devices  8.24 us (14%)
    pallas_call x1, Pallas kernels, pose(): pl.pallas_call(pose_kernel, in_specs=[SMEM] + [VMEM] * 13 + [ANYWHERE] *...  11.8 us
    ppermute x2, starting transfers between devices, to_neighbours(): lax.ppermute(up, 'tile', [((i + 1) % count, i) for i in range(count)])  10.9 us
    pallas_call x1, Pallas kernels, conv_backward(): pl.pallas_call(back_kernel, in_specs=[VMEM] * 5, out_specs=ANYWHERE, out_...  8.32 us
    pallas_call x1, Pallas kernels, conv_main(): pl.pallas_call(conv_kernel, in_specs=[VMEM] * 4 + [ANYWHERE] * 2, out_spe...  4.91 us
    ppermute x6, waiting for transfers between devices, swap_turns(): out.append(lax.ppermute(parts[turn], 'tile', pairs))  4.74 us
    ppermute x6, starting transfers between devices, swap_turns(): out.append(lax.ppermute(parts[turn], 'tile', pairs))  4.5 us
    ppermute x2, waiting for transfers between devices, to_neighbours(): lax.ppermute(down, 'tile', [(i, (i + 1) % count) for i in range(count)])  3.2 us
    pallas_call x1, Pallas kernels, conv_tail(): pl.pallas_call(tail_kernel, in_specs=[ANYWHERE] * 6, out_specs=[VMEM] * 6...  2.61 us
  transfers between devices with their start and end apart: 12, of which 8 were waited for; matrix products, arithmetic and copies ran while one was open for 0% of the time, Pallas kernels for 22%

profile of v3, /device:TPU:0, one launch (start us, length us, event | category | flops | bytes accessed | tf_op | source)
XLA Modules:
  0.0 60.2 jit_solution(7432457252602454347)
XLA Ops:
  0.1 2.6 %conv_tail.1 = (f32[2,3,8,128]{3,2,1,0:T(8,128)S(1)}, bf16[32,4,128,128]{3,2,1,0:T(8,128)(2,1)S(1)}, bf16[1024,256]{1,0:T(8,128)(2,1)S(1)}, bf16[256,1024]{1,0:T...) custom-call(bf16[32,4,128,128]{3,2,1,0:T(8,128)(2,1)} %feat_hbm, f32[1,128]{1,0:T(1,128)} %bitcast.17, ...), custom_call_target="tpu_custom_call" | custom-call | tf_op jit(solution)/shard_map/conv_tail/pallas_call | solution.py:224
  2.7 1.6 %collective-permute-start = (f32[2,3,8,128]{3,2,1,0:T(8,128)S(1)}, f32[2,3,8,128]{3,2,1,0:T(8,128)S(1)}, u32[]{:S(2)}, u32[]{:S(2)}) collective-permute-start(f32[2,3,8,128]{3,2,1,0:T(8,128)S(1)} %get-tuple-element.39), channel_id=1, source_target_pairs={{0,1},{1,2},{2,3},{3,0},{4,5},{5,6},{6,7},{7,4},{8,9},{9,10},{10,1... | collective-permute-start | bytes 73736 | tf_op jit(solution)/shard_map/ppermute | solution.py:756
  4.4 4.9 %conv_main.1 = (f32[32,3,8,128]{3,2,1,0:T(8,128)S(1)}, bf16[1280,2560]{1,0:T(8,128)(2,1)S(1)}, bf16[2560,1280]{1,0:T(8,128)(2,1)S(1)}) custom-call(bf16[32,4,128,128]{3,2,1,0:T(8,128)(2,1)S(1)} %get-tuple-element.34.feat_ref, f32[1,128]{1,0:T(1,128)S(1)} %get-tuple-element.35.gain_ref, bf16[256,256]{1,0:T(8,128)(2,1)S(1)} %get-tuple-element.36.mean_ref, ...), custom_call_target="tpu_custom_call" | custom-call | flops 33554432 | bytes 20971520 | tf_op jit(solution)/shard_map/conv_main/pallas_call | solution.py:250
  9.4 0.6 %rims.1 = (f32[3,32,128]{2,1,0:T(8,128)S(1)}, f32[3,32,128]{2,1,0:T(8,128)S(1)}) custom-call(s32[4]{0:T(128)S(1)} %pad_add_fusion.place_ref.own_ref, f32[32,3,8,128]{3,2,1,0:T(8,128)S(1)} %get-tuple-element.38.sums_ref, f32[2,3,8,128]{3,2,1,0:T(8,128)S(1)} %collective-permute-done.prior_ref), custom_call_target="tpu_custom_call" | custom-call | tf_op jit(solution)/shard_map/rims/pallas_call | solution.py:288
  10.1 5.7 %collective-permute-start.2 = (f32[3,32,128]{2,1,0:T(8,128)S(1)}, f32[3,32,128]{2,1,0:T(8,128)S(1)}, u32[]{:S(2)}, u32[]{:S(2)}) collective-permute-start(f32[3,32,128]{2,1,0:T(8,128)S(1)} %get-tuple-element.41), channel_id=1, source_target_pairs={{4,0},{8,4},{12,8},{16,12},{20,16},{24,20},{28,24},{32,28},{36,32}... | collective-permute-start | bytes 147464 | tf_op jit(solution)/shard_map/ppermute | solution.py:341
  15.8 1.7 %collective-permute-done.1.above_ref = f32[3,32,128]{2,1,0:T(8,128)S(1)} collective-permute-done((f32[3,32,128]{2,1,0:T(8,128)S(1)}, f32[3,32,128]{2,1,0:T(8,128)S(1)}, u32[]{:S(2)}, u32[]{:S(2)}) %collective-permute-start.1) | collective-permute-done | bytes 49184 | tf_op jit(solution)/shard_map/ppermute | solution.py:340
  17.5 0.7 %colours.1 = (bf16[8,16,128]{2,1,0:T(8,128)(2,1)S(1)}, bf16[8,16,128]{2,1,0:T(8,128)(2,1)S(1)}, bf16[8,16,128]{2,1,0:T(8,128)(2,1)S(1)}, bf16[8,16,128]{2,1,0:T(8,128)(2,1)S(1)}) custom-call(s32[4]{0:T(128)S(1)} %pad_add_fusion.place_ref.own_ref, f32[3]{0:T(128)S(1)} %copy-done.11, f32[32,3,8,128]{3,2,1,0:T(8,128)S(1)} %get-tuple-element.38.sums_ref, ...), custom_call_target="tpu_custom_call" | custom-call | tf_op jit(solution)/shard_map/colours/pallas_call | solution.py:318
  18.4 1.7 %collective-permute-start.5 = (bf16[8,16,128]{2,1,0:T(8,128)(2,1)S(1)}, bf16[8,16,128]{2,1,0:T(8,128)(2,1)S(1)}, u32[]{:S(2)}, u32[]{:S(2)}) collective-permute-start(bf16[8,16,128]{2,1,0:T(8,128)(2,1)S(1)} %get-tuple-element.45), channel_id=1, source_target_pairs={{0,12},{4,0},{8,4},{12,8},{16,28},{20,16},{24,20},{28,24},{32,44},... | collective-permute-start | bytes 98312 | tf_op jit(solution)/shard_map/ppermute | solution.py:334
  20.1 1.6 %collective-permute-done.3.x1_ref = bf16[8,16,128]{2,1,0:T(8,128)(2,1)S(1)} collective-permute-done((bf16[8,16,128]{2,1,0:T(8,128)(2,1)S(1)}, bf16[8,16,128]{2,1,0:T(8,128)(2,1)S(1)}, u32[]{:S(2)}, u32[]{:S(2)}) %collective-permute-start.3) | collective-permute-done | bytes 32800 | tf_op jit(solution)/shard_map/ppermute | solution.py:334
  21.7 0.7 %collective-permute-done.4.x2_ref = bf16[8,16,128]{2,1,0:T(8,128)(2,1)S(1)} collective-permute-done((bf16[8,16,128]{2,1,0:T(8,128)(2,1)S(1)}, bf16[8,16,128]{2,1,0:T(8,128)(2,1)S(1)}, u32[]{:S(2)}, u32[]{:S(2)}) %collective-permute-start.4) | collective-permute-done | bytes 32800 | tf_op jit(solution)/shard_map/ppermute | solution.py:334
  22.5 11.8 %pose.1 = (bf16[8,16,128]{2,1,0:T(8,128)(2,1)S(1)}, bf16[8,16,128]{2,1,0:T(8,128)(2,1)S(1)}, bf16[8,16,128]{2,1,0:T(8,128)(2,1)S(1)}, bf16[8,16,128]{2,1,0:T(8,128)(2,1)S(1)}) custom-call(s32[4]{0:T(128)S(1)} %pad_add_fusion.place_ref.own_ref, bf16[8,16,128]{2,1,0:T(8,128)(2,1)S(1)} %get-tuple-element.42.x0_ref, ...), custom_call_target="tpu_custom_call" | custom-call | flops 2022400000 | bytes 17825792 | tf_op jit(solution)/shard_map/pose/pallas_call | solution.py:503
  34.3 1.2 %collective-permute-start.6 = (bf16[8,16,128]{2,1,0:T(8,128)(2,1)S(1)}, bf16[8,16,128]{2,1,0:T(8,128)(2,1)S(1)}, u32[]{:S(2)}, u32[]{:S(2)}) collective-permute-start(bf16[8,16,128]{2,1,0:T(8,128)(2,1)S(1)} %get-tuple-element.50), channel_id=1, source_target_pairs={{0,4},{4,8},{8,12},{12,0},{16,20},{20,24},{24,28},{28,16},{32,36},... | collective-permute-start | bytes 98312 | tf_op jit(solution)/shard_map/ppermute | solution.py:334
  35.5 0.3 collective-permute-start.7
  35.8 1.1 %collective-permute-start.8 = (bf16[8,16,128]{2,1,0:T(8,128)(2,1)S(1)}, bf16[8,16,128]{2,1,0:T(8,128)(2,1)S(1)}, u32[]{:S(2)}, u32[]{:S(2)}) collective-permute-start(bf16[8,16,128]{2,1,0:T(8,128)(2,1)S(1)} %get-tuple-element.52), channel_id=1, source_target_pairs={{0,12},{4,0},{8,4},{12,8},{16,28},{20,16},{24,20},{28,24},{32,44},... | collective-permute-start | bytes 98312 | tf_op jit(solution)/shard_map/ppermute | solution.py:334
  37.0 0.7 %collective-permute-done.6.x1_ref = bf16[8,16,128]{2,1,0:T(8,128)(2,1)S(1)} collective-permute-done((bf16[8,16,128]{2,1,0:T(8,128)(2,1)S(1)}, bf16[8,16,128]{2,1,0:T(8,128)(2,1)S(1)}, u32[]{:S(2)}, u32[]{:S(2)}) %collective-permute-start.6) | collective-permute-done | bytes 32800 | tf_op jit(solution)/shard_map/ppermute | solution.py:334
  37.7 1.7 %collective-permute-done.7.x2_ref = bf16[8,16,128]{2,1,0:T(8,128)(2,1)S(1)} collective-permute-done((bf16[8,16,128]{2,1,0:T(8,128)(2,1)S(1)}, bf16[8,16,128]{2,1,0:T(8,128)(2,1)S(1)}, u32[]{:S(2)}, u32[]{:S(2)}) %collective-permute-start.7) | collective-permute-done | bytes 32800 | tf_op jit(solution)/shard_map/ppermute | solution.py:334
  39.5 0.6 %strip_grads.1 = (f32[32,3,8,128]{3,2,1,0:T(8,128)S(1)}, f32[3,32,128]{2,1,0:T(8,128)S(1)}, f32[3,32,128]{2,1,0:T(8,128)S(1)}) custom-call(s32[4]{0:T(128)S(1)} %pad_add_fusion.place_ref.own_ref, bf16[8,16,128]{2,1,0:T(8,128)(2,1)S(1)} %get-tuple-element.49.x0_ref, bf16[8,16,128]{2,1,0:T(8,128)(2,1)S(1)} %collective-permute-done.6.x1_ref, ...), custom_call_target="tpu_custom_call" | custom-call | tf_op jit(solution)/shard_map/strip_grads/pallas_call | solution.py:560
  40.3 5.2 %collective-permute-start.10 = (f32[3,32,128]{2,1,0:T(8,128)S(1)}, f32[3,32,128]{2,1,0:T(8,128)S(1)}, u32[]{:S(2)}, u32[]{:S(2)}) collective-permute-start(f32[3,32,128]{2,1,0:T(8,128)S(1)} %get-tuple-element.55), channel_id=1, source_target_pairs={{4,0},{8,4},{12,8},{16,12},{20,16},{24,20},{28,24},{32,28},{36,32}... | collective-permute-start | bytes 147464 | tf_op jit(solution)/shard_map/ppermute | solution.py:341
  45.5 1.5 %collective-permute-done.9.above_ref = f32[3,32,128]{2,1,0:T(8,128)S(1)} collective-permute-done((f32[3,32,128]{2,1,0:T(8,128)S(1)}, f32[3,32,128]{2,1,0:T(8,128)S(1)}, u32[]{:S(2)}, u32[]{:S(2)}) %collective-permute-start.9) | collective-permute-done | bytes 49184 | tf_op jit(solution)/shard_map/ppermute | solution.py:340
  47.0 0.2 collective-permute-done.10.below_ref
  47.3 0.6 %whole_grads.1 = (f32[32,3,8,128]{3,2,1,0:T(8,128)S(1)}, f32[2,3,8,128]{3,2,1,0:T(8,128)S(1)}) custom-call(s32[4]{0:T(128)S(1)} %pad_add_fusion.place_ref.own_ref, f32[32,3,8,128]{3,2,1,0:T(8,128)S(1)} %get-tuple-element.53.x_ref, f32[3,32,128]{2,1,0:T(8,128)S(1)} %collective-permute-done.9.above_ref, f32[3,32,128]{2,1,0:T(8,128)S(1)} %collective-permute-done.10.below_ref), custom_call_target="tpu_custom_call" | custom-call | tf_op jit(solution)/shard_map/whole_grads/pallas_call | solution.py:581
  47.9 1.8 %collective-permute-start.11 = (f32[2,3,8,128]{3,2,1,0:T(8,128)S(1)}, f32[2,3,8,128]{3,2,1,0:T(8,128)S(1)}, u32[]{:S(2)}, u32[]{:S(2)}) collective-permute-start(f32[2,3,8,128]{3,2,1,0:T(8,128)S(1)} %get-tuple-element.57), channel_id=1, source_target_pairs={{1,0},{2,1},{3,2},{0,3},{5,4},{6,5},{7,6},{4,7},{9,8},{10,9},{11,1... | collective-permute-start | bytes 73736 | tf_op jit(solution)/shard_map/ppermute | solution.py:778
  49.7 8.3 %conv_back.1.prior_hbm = bf16[32,4,128,128]{3,2,1,0:T(8,128)(2,1)} custom-call(bf16[32,4,128,128]{3,2,1,0:T(8,128)(2,1)S(1)} %get-tuple-element.34.feat_ref, f32[32,3,8,128]{3,2,1,0:T(8,128)S(1)} %get-tuple-element.56.grad_ref, f32[1,128]{1,0:T(1,128)S(1)} %get-tuple-element.35.gain_ref, bf16[256,256]{1,0:T(8,128)(2,1)S(1)} %get-tuple-element.36.mean_ref, ...), custom_call_target="tpu_custom_call" | custom-call | flops 33554432 | bytes 9437184 | tf_op jit(solution)/shard_map/conv_back/pallas_call | solution.py:688
  58.1 2.0 %conv_last.1 = bf16[32,4,128,128]{3,2,1,0:T(8,128)(2,1)} custom-call(s32[4]{0:T(128)S(1)} %pad_add_fusion.place_ref.own_ref, bf16[32,4,128,128]{3,2,1,0:T(8,128)(2,1)S(1)} %get-tuple-element.34.feat_ref, f32[32,3,8,128]{3,2,1,0:T(8,128)S(1)} %get-tuple-element.56.grad_ref, ...), custom_call_target="tpu_custom_call", output_to_operand_aliasing={{}: (7, {})} | custom-call | tf_op jit(solution)/shard_map/conv_last/pallas_call | solution.py:704
  (34 shorter events, 0.7 us)
Async XLA Ops:
  2.7 6.7 %collective-permute-start = (f32[2,3,8,128]{3,2,1,0:T(8,128)S(1)}, f32[2,3,8,128]{3,2,1,0:T(8,128)S(1)}, u32[]{:S(2)}, u32[]{:S(2)}) collective-permute-start(f32[2,3,8,128]{3,2,1,0:T(8,128)S(1)} %get-tuple-element.39), channel_id=1, source_target_pairs={{0,1},{1,2},{2,3},{3,0},{4,5},{5,6},{6,7},{7,4},{8,9},{9,10},{10,1... | collective-permute-start | bytes 73736 | tf_op jit(solution)/shard_map/ppermute | solution.py:756
  4.3 13.2 %copy-start.11 = (f32[3]{0:T(128)S(1)}, f32[3]{0:T(128)}, u32[]{:S(2)}) copy-start(f32[3]{0:T(128)} %bias_ref.1) | copy-start | bytes 40
  4.3 18.1 %copy-start = (bf16[768,1280]{1,0:T(8,128)(2,1)S(1)}, bf16[768,1280]{1,0:T(8,128)(2,1)}, u32[]{:S(2)}) copy-start(bf16[768,1280]{1,0:T(8,128)(2,1)} %patch_hbm.1) | copy-start | bytes 5898244
  4.3 18.1 %copy-start.1 = (bf16[768,768]{1,0:T(8,128)(2,1)S(1)}, bf16[768,768]{1,0:T(8,128)(2,1)}, u32[]{:S(2)}) copy-start(bf16[768,768]{1,0:T(8,128)(2,1)} %constant.27.clone.order_hbm) | copy-start | bytes 3538948
  4.3 18.1 %copy-start.2 = (bf16[1280,272]{0,1:T(8,128)(2,1)S(1)}, bf16[1280,272]{0,1:T(8,128)(2,1)}, u32[]{:S(2)}) copy-start(bf16[1280,272]{0,1:T(8,128)(2,1)} %param.34) | copy-start | bytes 2088964
  4.3 18.1 %copy-start.3 = (bf16[64,1280]{1,0:T(8,128)(2,1)S(1)}, bf16[64,1280]{1,0:T(8,128)(2,1)}, u32[]{:S(2)}) copy-start(bf16[64,1280]{1,0:T(8,128)(2,1)} %position_hbm.1) | copy-start | bytes 491524
  4.4 18.1 %copy-start.4 = (bf16[17,272]{1,0:T(8,128)(2,1)S(1)}, bf16[17,272]{1,0:T(8,128)(2,1)}, u32[]{:S(2)}) copy-start(bf16[17,272]{1,0:T(8,128)(2,1)} %constant.26.clone.key_spread_ref) | copy-start | bytes 27748
  4.4 18.1 %copy-start.5 = (s32[32,17]{0,1:T(8,128)S(1)}, s32[32,17]{0,1:T(8,128)}, u32[]{:S(2)}) copy-start(s32[32,17]{0,1:T(8,128)} %param.26) | copy-start | bytes 6532
  4.4 18.1 %copy-start.6 = (s32[32,17]{0,1:T(8,128)S(1)}, s32[32,17]{0,1:T(8,128)}, u32[]{:S(2)}) copy-start(s32[32,17]{0,1:T(8,128)} %param.27) | copy-start | bytes 6532
  4.4 18.1 %copy-start.7 = (s32[32,17]{0,1:T(8,128)S(1)}, s32[32,17]{0,1:T(8,128)}, u32[]{:S(2)}) copy-start(s32[32,17]{0,1:T(8,128)} %param.28) | copy-start | bytes 6532
  4.4 18.0 %copy-start.8 = (f32[1280]{0:T(1024)S(1)}, f32[1280]{0:T(1024)}, u32[]{:S(2)}) copy-start(f32[1280]{0:T(1024)} %param.31) | copy-start | bytes 15364
  4.4 18.0 %copy-start.9 = (s32[1,32,3]{1,0,2:T(1,128)S(1)}, s32[1,32,3]{1,0,2:T(1,128)}, u32[]{:S(2)}) copy-start(s32[1,32,3]{1,0,2:T(1,128)} %param.24) | copy-start | bytes 1156
  4.4 18.0 %copy-start.10 = (s32[1,32]{1,0:T(1,128)S(1)}, s32[1,32]{1,0:T(1,128)}, u32[]{:S(2)}) copy-start(s32[1,32]{1,0:T(1,128)} %counts_ref.1) | copy-start | bytes 388
  10.0 7.5 %collective-permute-start.1 = (f32[3,32,128]{2,1,0:T(8,128)S(1)}, f32[3,32,128]{2,1,0:T(8,128)S(1)}, u32[]{:S(2)}, u32[]{:S(2)}) collective-permute-start(f32[3,32,128]{2,1,0:T(8,128)S(1)} %get-tuple-element.40), channel_id=1, source_target_pairs={{0,4},{4,8},{8,12},{12,16},{16,20},{20,24},{24,28},{28,32},{32,36}... | collective-permute-start | bytes 147464 | tf_op jit(solution)/shard_map/ppermute | solution.py:340
  10.1 7.5 %collective-permute-start.2 = (f32[3,32,128]{2,1,0:T(8,128)S(1)}, f32[3,32,128]{2,1,0:T(8,128)S(1)}, u32[]{:S(2)}, u32[]{:S(2)}) collective-permute-start(f32[3,32,128]{2,1,0:T(8,128)S(1)} %get-tuple-element.41), channel_id=1, source_target_pairs={{4,0},{8,4},{12,8},{16,12},{20,16},{24,20},{28,24},{32,28},{36,32}... | collective-permute-start | bytes 147464 | tf_op jit(solution)/shard_map/ppermute | solution.py:341
  18.3 3.4 %collective-permute-start.3 = (bf16[8,16,128]{2,1,0:T(8,128)(2,1)S(1)}, bf16[8,16,128]{2,1,0:T(8,128)(2,1)S(1)}, u32[]{:S(2)}, u32[]{:S(2)}) collective-permute-start(bf16[8,16,128]{2,1,0:T(8,128)(2,1)S(1)} %get-tuple-element.43), channel_id=1, source_target_pairs={{0,4},{4,8},{8,12},{12,0},{16,20},{20,24},{24,28},{28,16},{32,36},... | collective-permute-start | bytes 98312 | tf_op jit(solution)/shard_map/ppermute | solution.py:334
  18.4 4.0 %collective-permute-start.4 = (bf16[8,16,128]{2,1,0:T(8,128)(2,1)S(1)}, bf16[8,16,128]{2,1,0:T(8,128)(2,1)S(1)}, u32[]{:S(2)}, u32[]{:S(2)}) collective-permute-start(bf16[8,16,128]{2,1,0:T(8,128)(2,1)S(1)} %get-tuple-element.44), channel_id=1, source_target_pairs={{0,8},{4,12},{8,0},{12,4},{16,24},{20,28},{24,16},{28,20},{32,40},... | collective-permute-start | bytes 98312 | tf_op jit(solution)/shard_map/ppermute | solution.py:334
  18.4 3.9 %collective-permute-start.5 = (bf16[8,16,128]{2,1,0:T(8,128)(2,1)S(1)}, bf16[8,16,128]{2,1,0:T(8,128)(2,1)S(1)}, u32[]{:S(2)}, u32[]{:S(2)}) collective-permute-start(bf16[8,16,128]{2,1,0:T(8,128)(2,1)S(1)} %get-tuple-element.45), channel_id=1, source_target_pairs={{0,12},{4,0},{8,4},{12,8},{16,28},{20,16},{24,20},{28,24},{32,44},... | collective-permute-start | bytes 98312 | tf_op jit(solution)/shard_map/ppermute | solution.py:334
  34.3 3.4 %collective-permute-start.6 = (bf16[8,16,128]{2,1,0:T(8,128)(2,1)S(1)}, bf16[8,16,128]{2,1,0:T(8,128)(2,1)S(1)}, u32[]{:S(2)}, u32[]{:S(2)}) collective-permute-start(bf16[8,16,128]{2,1,0:T(8,128)(2,1)S(1)} %get-tuple-element.50), channel_id=1, source_target_pairs={{0,4},{4,8},{8,12},{12,0},{16,20},{20,24},{24,28},{28,16},{32,36},... | collective-permute-start | bytes 98312 | tf_op jit(solution)/shard_map/ppermute | solution.py:334
  35.5 3.9 %collective-permute-start.7 = (bf16[8,16,128]{2,1,0:T(8,128)(2,1)S(1)}, bf16[8,16,128]{2,1,0:T(8,128)(2,1)S(1)}, u32[]{:S(2)}, u32[]{:S(2)}) collective-permute-start(bf16[8,16,128]{2,1,0:T(8,128)(2,1)S(1)} %get-tuple-element.51), channel_id=1, source_target_pairs={{0,8},{4,12},{8,0},{12,4},{16,24},{20,28},{24,16},{28,20},{32,40},... | collective-permute-start | bytes 98312 | tf_op jit(solution)/shard_map/ppermute | solution.py:334
  35.8 3.6 %collective-permute-start.8 = (bf16[8,16,128]{2,1,0:T(8,128)(2,1)S(1)}, bf16[8,16,128]{2,1,0:T(8,128)(2,1)S(1)}, u32[]{:S(2)}, u32[]{:S(2)}) collective-permute-start(bf16[8,16,128]{2,1,0:T(8,128)(2,1)S(1)} %get-tuple-element.52), channel_id=1, source_target_pairs={{0,12},{4,0},{8,4},{12,8},{16,28},{20,16},{24,20},{28,24},{32,44},... | collective-permute-start | bytes 98312 | tf_op jit(solution)/shard_map/ppermute | solution.py:334
  40.1 6.9 %collective-permute-start.9 = (f32[3,32,128]{2,1,0:T(8,128)S(1)}, f32[3,32,128]{2,1,0:T(8,128)S(1)}, u32[]{:S(2)}, u32[]{:S(2)}) collective-permute-start(f32[3,32,128]{2,1,0:T(8,128)S(1)} %get-tuple-element.54), channel_id=1, source_target_pairs={{0,4},{4,8},{8,12},{12,16},{16,20},{20,24},{24,28},{28,32},{32,36}... | collective-permute-start | bytes 147464 | tf_op jit(solution)/shard_map/ppermute | solution.py:340
  40.3 6.9 %collective-permute-start.10 = (f32[3,32,128]{2,1,0:T(8,128)S(1)}, f32[3,32,128]{2,1,0:T(8,128)S(1)}, u32[]{:S(2)}, u32[]{:S(2)}) collective-permute-start(f32[3,32,128]{2,1,0:T(8,128)S(1)} %get-tuple-element.55), channel_id=1, source_target_pairs={{4,0},{8,4},{12,8},{16,12},{20,16},{24,20},{28,24},{32,28},{36,32}... | collective-permute-start | bytes 147464 | tf_op jit(solution)/shard_map/ppermute | solution.py:341
  47.9 10.1 %collective-permute-start.11 = (f32[2,3,8,128]{3,2,1,0:T(8,128)S(1)}, f32[2,3,8,128]{3,2,1,0:T(8,128)S(1)}, u32[]{:S(2)}, u32[]{:S(2)}) collective-permute-start(f32[2,3,8,128]{3,2,1,0:T(8,128)S(1)} %get-tuple-element.57), channel_id=1, source_target_pairs={{1,0},{2,1},{3,2},{0,3},{5,4},{6,5},{7,6},{4,7},{9,8},{10,9},{11,1... | collective-permute-start | bytes 73736 | tf_op jit(solution)/shard_map/ppermute | solution.py:778

commit v4 on v3

--- a/solution.py
+++ b/solution.py
@@ -1,3 +1,5 @@
+import functools
+
 import jax
 import jax.numpy as jnp
 import ml_dtypes
@@ -17,7 +19,7 @@
 ROWS = 4
 GROUP = 4
 FORWARD_FRAMES = 8
-BACK_FRAMES = 10
+BACK_FRAMES = 8
 BACK_ROWS = 4
 NORM_EPS = 1e-06
 F32 = jnp.float32
@@ -275,12 +277,19 @@
     return jnp.where(is_edge, jnp.zeros_like(value), value)
 
 
-def rim_kernel(place_ref, sums_ref, prior_ref, up_ref, down_ref):
+def is_even(place_ref):
+    return lax.rem(place_ref[0], 2) == 0
+
+
+def rim_kernel(place_ref, sums_ref, prior_ref, inside_ref, across_ref, up, down):
     first_block = place_ref[1] == 0
     for o in range(3):
-        for k, out_ref in ((0, up_ref), (5, down_ref)):
+        for k, out_ref in ((0, up), (5, down)):
             out_ref[o] = sums_ref[:, o, k, :]
             out_ref[o, 0:2] = sums_ref[0:2, o, k, :] + unless(first_block, prior_ref[:, o, k, :])
+    even = is_even(place_ref)
+    inside_ref[...] = jnp.where(even, down[...], up[...])
+    across_ref[...] = jnp.where(even, up[...], down[...])
 
 
 def rims(place, sums, prior):
@@ -290,30 +299,35 @@
         in_specs=[SMEM] + [VMEM] * 2,
         out_specs=[VMEM] * 2,
         out_shape=[shape] * 2,
+        scratch_shapes=[pltpu.VMEM(shape.shape, F32)] * 2,
         compiler_params=megabytes(4),
         name="rims",
     )(place, sums, prior)
 
 
-def colour_kernel(own_ref, bias_ref, sums_ref, prior_ref, above_ref, below_ref, *rest):
+def colour_kernel(own_ref, bias_ref, sums_ref, prior_ref, inside_ref, across_ref, *rest):
     out_refs, total = rest[:GROUP], rest[GROUP]
     total[...] = sums_ref[...]
     total[0:2] = sums_ref[0:2] + unless(own_ref[1] == 0, prior_ref[...])
     top, bottom = own_ref[0] == 0, own_ref[0] == own_ref[2] - 1
     row = sublanes_of((8, 8, COLS))
     me = lax.rem(own_ref[0], GROUP)
+    even = is_even(own_ref)
     for turn in range(GROUP):
         frames = pl.ds(pl.multiple_of(lax.rem(me + turn, GROUP) * 8, 8), 8)
         groups = []
         for o in range(3):
             value = total[frames, o]
-            value += jnp.where(row == 1, unless(top, above_ref[o, frames, :])[:, None, :], 0.0)
-            value += jnp.where(row == 4, unless(bottom, below_ref[o, frames, :])[:, None, :], 0.0)
+            inside, across = inside_ref[o, frames, :], across_ref[o, frames, :]
+            above = unless(top, jnp.where(even, across, inside))
+            below = unless(bottom, jnp.where(even, inside, across))
+            value += jnp.where(row == 1, above[:, None, :], 0.0)
+            value += jnp.where(row == 4, below[:, None, :], 0.0)
             groups.append(roll(value, -1, 1) + bias_ref[o])
         out_refs[turn][...] = lay_rows(groups).astype(BF16)
 
 
-def colours(own, bias, sums, prior, above, below):
+def colours(own, bias, sums, prior, inside, across):
     shape = jax.ShapeDtypeStruct((8, 16, COLS), BF16)
     return pl.pallas_call(
         colour_kernel,
@@ -323,7 +337,7 @@
         scratch_shapes=[pltpu.VMEM(sums.shape, F32)],
         compiler_params=megabytes(4),
         name="colours",
-    )(own, bias, sums, prior, above, below)
+    )(own, bias, sums, prior, inside, across)
 
 
 def swap_turns(parts):
@@ -335,11 +349,11 @@
     return out
 
 
-def to_neighbours(up, down):
+def swap_rims(inside, across):
     count = lax.axis_size("tile")
-    above = lax.ppermute(down, "tile", [(i, (i + 1) % count) for i in range(count)])
-    below = lax.ppermute(up, "tile", [((i + 1) % count, i) for i in range(count)])
-    return above, below
+    pairs = [(i, i + 1 - 2 * (i % 2)) for i in range(count)]
+    others = [(i, min(max(i - 1 + 2 * (i % 2), 0), count - 1)) for i in range(count)]
+    return lax.ppermute(inside, "tile", pairs), lax.ppermute(across, "tile", others)
 
 
 def swap_blocks(x):
@@ -541,7 +555,7 @@
     )
 
 
-def strip_kernel(own_ref, x0_ref, x1_ref, x2_ref, x3_ref, out_ref, first_ref, last_ref):
+def strip_kernel(own_ref, x0_ref, x1_ref, x2_ref, x3_ref, out_ref, inside_ref, across_ref):
     me = lax.rem(own_ref[0], GROUP)
     first = sublanes_of((8, 8, COLS)) < 4
     for turn, ref in enumerate((x0_ref, x1_ref, x2_ref, x3_ref)):
@@ -550,9 +564,11 @@
         groups = [value[:, :8], roll(value[:, :8], 4, 1), value[:, 8:]]
         for o in range(3):
             out_ref[frames, o] = roll(jnp.where(first, groups[o], 0.0), 1, 1)
+    even = is_even(own_ref)
     for o in range(3):
-        first_ref[o] = out_ref[:, o, 1, :]
-        last_ref[o] = out_ref[:, o, 4, :]
+        upper, lower = out_ref[:, o, 1, :], out_ref[:, o, 4, :]
+        inside_ref[o] = jnp.where(even, lower, upper)
+        across_ref[o] = jnp.where(even, upper, lower)
 
 
 def strip_grads(own, parts):
@@ -567,17 +583,20 @@
     )(own, *parts)
 
 
-def whole_kernel(place_ref, x_ref, above_ref, below_ref, out_ref, first_ref):
+def whole_kernel(place_ref, x_ref, inside_ref, across_ref, out_ref, first_ref):
     row = sublanes_of((32, 8, COLS))
     top, bottom = place_ref[0] == 0, place_ref[0] == place_ref[2] - 1
+    even = is_even(place_ref)
     for o in range(3):
-        value = jnp.where(row == 0, unless(top, above_ref[o])[:, None, :], x_ref[:, o])
-        value = jnp.where(row == 5, unless(bottom, below_ref[o])[:, None, :], value)
+        above = unless(top, jnp.where(even, across_ref[o], inside_ref[o]))
+        below = unless(bottom, jnp.where(even, inside_ref[o], across_ref[o]))
+        value = jnp.where(row == 0, above[:, None, :], x_ref[:, o])
+        value = jnp.where(row == 5, below[:, None, :], value)
         out_ref[:, o] = value
         first_ref[:, o] = value[:2]
 
 
-def whole_grads(place, x, above, below):
+def whole_grads(place, x, inside, across):
     return pl.pallas_call(
         whole_kernel,
         in_specs=[SMEM] + [VMEM] * 3,
@@ -588,7 +607,7 @@
         ],
         compiler_params=megabytes(4),
         name="whole_grads",
-    )(place, x, above, below)
+    )(place, x, inside, across)
 
 
 def frame_taps(groups):
@@ -607,69 +626,95 @@
     return jnp.concatenate(rows, axis=0).T
 
 
-def back_pair(feat_ref, frame, taps, weight, half_gain, mean_pair, store):
-    grads = dot(taps, weight)
+def prepare_kernel(start, feat_ref, gain_ref, mean_ref, slope_ref, normed_ref):
+    half_gain = 0.5 * gain_ref[...]
+    mean_pair = mean_ref[...]
     places = [(tau, r) for tau in range(2) for r in range(ROWS)]
-    for part in range(0, len(places), BACK_ROWS):
-        group = places[part : part + BACK_ROWS]
-        xs = [feat_ref[frame + tau, r].astype(F32) for tau, r in group]
+
+    @pl.loop(0, slope_ref.shape[0] // 2)
+    def _(pair):
+        xs = [feat_ref[start + 2 * pair + tau, r].astype(F32) for tau, r in places]
         means = channel_means([x * x for x in xs], mean_pair)
-        kept = []
-        for x, mean, (tau, r) in zip(xs, means, group):
+        for x, mean, (tau, r) in zip(xs, means, places):
             rescale = lax.rsqrt(mean + NORM_EPS)
             normed = x * rescale
             half_pre = normed * half_gain
             tanh = jnp.tanh(half_pre)
             slope = (1.0 + tanh) * (1.0 + half_pre * (1.0 - tanh)) * half_gain
-            at = CH * (ROWS * tau + r)
-            kept.append((rescale, normed, grads[:, at : at + CH] * slope))
-        along = channel_means([scaled * normed for _, normed, scaled in kept], mean_pair)
-        for (rescale, normed, scaled), mean, (tau, r) in zip(kept, along, group):
-            store(tau, r, (rescale * (scaled - normed * mean)).astype(BF16))
-
-
-def back_kernel(
-    feat_ref, grad_ref, gain_ref, mean_ref, weight_ref, out_hbm, buffer, carry, sems
-):
-    half_gain = 0.5 * gain_ref[...]
+            slope_ref[2 * pair + tau, r] = (slope * rescale).astype(BF16)
+            normed_ref[2 * pair + tau, r] = normed.astype(BF16)
+
+
+def prepare(start, count, features, gain, mean_pair):
+    kept = pltpu.VMEM((count, ROWS, COLS, CH), BF16)
+    return pl.pallas_call(
+        functools.partial(prepare_kernel, start),
+        in_specs=[VMEM] * 3,
+        out_specs=[VMEM] * 2,
+        out_shape=[kept] * 2,
+        compiler_params=megabytes(8),
+        cost_estimate=pl.CostEstimate(
+            flops=10**9, bytes_accessed=10**5 * count, transcendentals=65536 * count
+        ),
+        name="prepare_%d" % start,
+    )(features, gain, mean_pair)
+
+
+def back_pair(kept, frame, taps, weight, mean_pair, store):
+    slope_ref, normed_ref = kept
+    grads = dot(taps, weight)
+    places = [(tau, r) for tau in range(2) for r in range(ROWS)]
+    for part in range(0, len(places), BACK_ROWS):
+        group = places[part : part + BACK_ROWS]
+        pairs = []
+        for i, (tau, r) in enumerate(group):
+            at = CH * (part + i)
+            scaled = grads[:, at : at + CH] * slope_ref[frame + tau, r].astype(F32)
+            pairs.append((scaled, normed_ref[frame + tau, r].astype(F32)))
+        along = channel_means([scaled * normed for scaled, normed in pairs], mean_pair)
+        for (scaled, normed), mean, (tau, r) in zip(pairs, along, group):
+            store(tau, r, (scaled - normed * mean).astype(BF16))
+
+
+def back_kernel(*refs):
+    kept = refs[:-7]
+    grad_ref, mean_ref, weight_ref, out_hbm, buffer, carry, sems = refs[-7:]
     mean_pair = mean_ref[...]
     carry[...] = pair_taps(grad_ref, 0)
-    steps = (feat_ref.shape[0] - 2) // BACK_FRAMES
-
-    def copy_of(step, slot):
-        rows = pl.ds(step * BACK_FRAMES, BACK_FRAMES)
-        return pltpu.make_async_copy(buffer.at[slot], out_hbm.at[rows], sems.at[slot])
-
-    @pl.loop(0, steps)
-    def _(step):
-        slot = lax.rem(step, 2)
-
-        @pl.when(step >= 2)
-        def _():
-            copy_of(step - 2, slot).wait()
-
-        for pair in range(BACK_FRAMES // 2):
-            frame = step * BACK_FRAMES + 2 * pair
+    last_pair = grad_ref.shape[0] - 2
+    copies = []
+    for step in range(len(kept) // 2):
+        base = step * BACK_FRAMES
+        count = min(BACK_FRAMES, last_pair - base)
+        slot = step % 2
+        if step >= 2:
+            copies[step - 2].wait()
+        for pair in range(count // 2):
             now = carry[...]
-            later = pair_taps(grad_ref, frame + 2)
+            later = pair_taps(grad_ref, base + 2 * pair + 2)
             carry[...] = later
             taps = jnp.concatenate([now, later], axis=1).astype(BF16)
 
             def store(tau, r, value):
                 buffer[slot, 2 * pair + tau, r] = value
 
-            back_pair(feat_ref, frame, taps, weight_ref[...], half_gain, mean_pair, store)
-        copy_of(step, slot).start()
-
-    for step in range(max(steps - 2, 0), steps):
-        copy_of(step, step % 2).wait()
+            back_pair(kept[2 * step : 2 * step + 2], 2 * pair, taps, weight_ref[...], mean_pair, store)
+        copies.append(
+            pltpu.make_async_copy(
+                buffer.at[slot, :count], out_hbm.at[base : base + count], sems.at[slot]
+            )
+        )
+        copies[-1].start()
+    for copy in copies[-2:]:
+        copy.wait()
 
 
 def last_kernel(
-    place_ref, feat_ref, grad_ref, next_ref, gain_ref, mean_ref, weight_ref, prior_hbm, out_hbm, buffer, sem
+    place_ref, slope_ref, normed_ref, grad_ref, next_ref, mean_ref, weight_ref, prior_hbm,
+    out_hbm, buffer, sem,
 ):
     del prior_hbm
-    frame = feat_ref.shape[0] - 2
+    frame = grad_ref.shape[0] - 2
     last_block = place_ref[1] == place_ref[3] - 1
     later = unless(last_block, pair_taps(next_ref, 0))
     taps = jnp.concatenate([pair_taps(grad_ref, frame), later], axis=1).astype(BF16)
@@ -677,17 +722,18 @@
     def store(tau, r, value):
         buffer[tau, r] = value
 
-    back_pair(feat_ref, frame, taps, weight_ref[...], 0.5 * gain_ref[...], mean_ref[...], store)
+    kept = (slope_ref, normed_ref)
+    back_pair(kept, BACK_FRAMES - 2, taps, weight_ref[...], mean_ref[...], store)
     copy = pltpu.make_async_copy(buffer, out_hbm.at[frame:], sem)
     copy.start()
     copy.wait()
 
 
-def conv_backward(place, features, grads, later, gain, mean_pair, weight):
-    out_shape = jax.ShapeDtypeStruct(features.shape, BF16)
+def conv_backward(place, kept, grads, later, mean_pair, weight):
+    out_shape = jax.ShapeDtypeStruct((grads.shape[0], ROWS, COLS, CH), BF16)
     part = pl.pallas_call(
         back_kernel,
-        in_specs=[VMEM] * 5,
+        in_specs=[VMEM] * (len(kept) * 2 + 3),
         out_specs=ANYWHERE,
         out_shape=out_shape,
         scratch_shapes=[
@@ -700,7 +746,7 @@
             flops=2 * 16384 * 1024, bytes_accessed=9 * 1024 * 1024, transcendentals=2 * 2097152
         ),
         name="conv_back",
-    )(features, grads, gain, mean_pair, weight)
+    )(*[x for pair in kept for x in pair], grads, mean_pair, weight)
     return pl.pallas_call(
         last_kernel,
         in_specs=[SMEM] + [VMEM] * 6 + [ANYWHERE],
@@ -710,7 +756,7 @@
         scratch_shapes=[pltpu.VMEM((2, ROWS, COLS, CH), BF16), pltpu.SemaphoreType.DMA],
         compiler_params=megabytes(12),
         name="conv_last",
-    )(place, features, grads, later, gain, mean_pair, weight, part)
+    )(place, *kept[-1], grads, later, mean_pair, weight, part)
 
 
 def per_device(
@@ -755,8 +801,15 @@
     )
     prior = lax.ppermute(tail, "tm", [(i, (i + 1) % tm_count) for i in range(tm_count)])
     sums, up, down = conv_main(features, gain, mean_pair, weight, up_weight, down_weight)
-    above, below = to_neighbours(*rims(own, sums, prior))
-    parts = swap_turns(colours(own, colour_bias, sums, prior, above, below))
+    def prepare_beside(chunk, *moving):
+        kept.append(prepare(chunk * BACK_FRAMES, BACK_FRAMES, features, gain, mean_pair))
+        *moving, kept[-1] = lax.optimization_barrier((*moving, kept[-1]))
+        return moving
+
+    kept = []
+    rim_sums = prepare_beside(0, *swap_rims(*rims(own, sums, prior)))
+    parts = swap_turns(colours(own, colour_bias, sums, prior, *rim_sums))
+    parts = prepare_beside(1, *parts)
     parts = pose(
         own,
         parts,
@@ -772,11 +825,11 @@
         head_weight.T,
         position_table,
     )
-    grads, first, last = strip_grads(own, swap_turns(parts))
-    above, below = to_neighbours(first, last)
-    grads, first = whole_grads(own, grads, above, below)
+    grads, inside, across = strip_grads(own, prepare_beside(2, *swap_turns(parts)))
+    rim_grads = prepare_beside(3, *swap_rims(inside, across))
+    grads, first = whole_grads(own, grads, *rim_grads)
     later = lax.ppermute(first, "tm", [((i + 1) % tm_count, i) for i in range(tm_count)])
-    return conv_backward(own, features, grads, later, gain, mean_pair, weight_t)
+    return conv_backward(own, kept, grads, later, mean_pair, weight_t)
 
 
 def solution(mesh):

time: 60.3 us -> 58.3 us (0.967)
  the two profiles are of different devices: /device:TPU:0 before, /device:TPU:25 now
where the time goes in v4:
time: 58.3 us; the launch traced here: 58.2 us
  Pallas kernels  35.4 us (61%)
  starting transfers between devices  18.7 us (32%)
  waiting for transfers between devices  3.53 us (6%)
    pallas_call x1, Pallas kernels, pose(): pl.pallas_call(pose_kernel, in_specs=[SMEM] + [VMEM] * 13 + [ANYWHERE] *...  11.8 us
    pallas_call x4, Pallas kernels, prepare(): pl.pallas_call(functools.partial(prepare_kernel, start), in_specs=[VMEM]...  6.61 us
    ppermute x2, starting transfers between devices, swap_rims(): lax.ppermute(across, 'tile', others)  5.97 us
    pallas_call x1, Pallas kernels, conv_backward(): pl.pallas_call(back_kernel, in_specs=[VMEM] * (len(kept) * 2 + 3), out_sp...  5.1 us
    ppermute x2, starting transfers between devices, swap_rims(): lax.ppermute(inside, 'tile', pairs)  4.98 us
    ppermute x6, starting transfers between devices, swap_turns(): out.append(lax.ppermute(parts[turn], 'tile', pairs))  4.91 us
    pallas_call x1, Pallas kernels, conv_main(): pl.pallas_call(conv_kernel, in_specs=[VMEM] * 4 + [ANYWHERE] * 2, out_spe...  4.76 us
    ppermute x6, waiting for transfers between devices, swap_turns(): out.append(lax.ppermute(parts[turn], 'tile', pairs))  3.27 us
  transfers between devices with their start and end apart: 12, of which 5 were waited for; matrix products, arithmetic and copies ran while one was open for 0% of the time, Pallas kernels for 28%

profile of v4, /device:TPU:25, one launch (start us, length us, event | category | flops | bytes accessed | tf_op | source)
XLA Modules:
  0.0 58.2 jit_solution(6366727131503451834)
XLA Ops:
  0.1 2.6 %conv_tail.1 = (f32[2,3,8,128]{3,2,1,0:T(8,128)S(1)}, bf16[32,4,128,128]{3,2,1,0:T(8,128)(2,1)S(1)}, bf16[1024,256]{1,0:T(8,128)(2,1)S(1)}, bf16[256,1024]{1,0:T...) custom-call(bf16[32,4,128,128]{3,2,1,0:T(8,128)(2,1)} %feat_hbm, f32[1,128]{1,0:T(1,128)} %bitcast.17, ...), custom_call_target="tpu_custom_call" | custom-call | tf_op jit(solution)/shard_map/conv_tail/pallas_call | solution.py:226
  2.7 1.3 %collective-permute-start = (f32[2,3,8,128]{3,2,1,0:T(8,128)S(1)}, f32[2,3,8,128]{3,2,1,0:T(8,128)S(1)}, u32[]{:S(2)}, u32[]{:S(2)}) collective-permute-start(f32[2,3,8,128]{3,2,1,0:T(8,128)S(1)} %get-tuple-element.67), channel_id=1, source_target_pairs={{0,1},{1,2},{2,3},{3,0},{4,5},{5,6},{6,7},{7,4},{8,9},{9,10},{10,1... | collective-permute-start | bytes 73736 | tf_op jit(solution)/shard_map/ppermute | solution.py:802
  4.0 4.8 %conv_main.1 = (f32[32,3,8,128]{3,2,1,0:T(8,128)S(1)}, bf16[1280,2560]{1,0:T(8,128)(2,1)S(1)}, bf16[2560,1280]{1,0:T(8,128)(2,1)S(1)}) custom-call(bf16[32,4,128,128]{3,2,1,0:T(8,128)(2,1)S(1)} %get-tuple-element.62.feat_ref, f32[1,128]{1,0:T(1,128)S(1)} %get-tuple-element.63.gain_ref, bf16[256,256]{1,0:T(8,128)(2,1)S(1)} %get-tuple-element.64.mean_ref.refs_9_, ...), custom_call_target="tpu_custom_call" | custom-call | flops 33554432 | bytes 20971520 | tf_op jit(solution)/shard_map/conv_main/pallas_call | solution.py:252
  8.8 0.6 %rims.1 = (f32[3,32,128]{2,1,0:T(8,128)S(1)}, f32[3,32,128]{2,1,0:T(8,128)S(1)}) custom-call(s32[4]{0:T(128)S(1)} %pad_add_fusion.place_ref.own_ref, f32[32,3,8,128]{3,2,1,0:T(8,128)S(1)} %get-tuple-element.66.sums_ref, f32[2,3,8,128]{3,2,1,0:T(8,128)S(1)} %collective-permute-done.prior_ref), custom_call_target="tpu_custom_call" | custom-call | tf_op jit(solution)/shard_map/rims/pallas_call | solution.py:297
  9.4 1.0 %collective-permute-start.1 = (f32[3,32,128]{2,1,0:T(8,128)S(1)}, f32[3,32,128]{2,1,0:T(8,128)S(1)}, u32[]{:S(2)}, u32[]{:S(2)}) collective-permute-start(f32[3,32,128]{2,1,0:T(8,128)S(1)} %get-tuple-element.68), channel_id=1, source_target_pairs={{0,4},{4,0},{8,12},{12,8},{16,20},{20,16},{24,28},{28,24},{32,36},... | collective-permute-start | bytes 147464 | tf_op jit(solution)/shard_map/ppermute | solution.py:356
  10.5 3.7 %collective-permute-start.2 = (f32[3,32,128]{2,1,0:T(8,128)S(1)}, f32[3,32,128]{2,1,0:T(8,128)S(1)}, u32[]{:S(2)}, u32[]{:S(2)}) collective-permute-start(f32[3,32,128]{2,1,0:T(8,128)S(1)} %get-tuple-element.69), channel_id=1, source_target_pairs={{0,0},{4,8},{8,4},{12,16},{16,12},{20,24},{24,20},{28,32},{32,28},... | collective-permute-start | bytes 147464 | tf_op jit(solution)/shard_map/ppermute | solution.py:356
  14.3 1.7 %prepare_0.1 = (bf16[8,4,128,128]{3,2,1,0:T(8,128)(2,1)S(1)}, bf16[8,4,128,128]{3,2,1,0:T(8,128)(2,1)S(1)}) custom-call(bf16[32,4,128,128]{3,2,1,0:T(8,128)(2,1)S(1)} %get-tuple-element.62.feat_ref, f32[1,128]{1,0:T(1,128)S(1)} %get-tuple-element.63.gain_ref, bf16[256,256]{1,0:T(8,128)(2,1)S(1)} %get-tuple-element.64.mean_ref.refs_9_), custom_call_target="tpu_custom_call" | custom-call | flops 1000000000 | bytes 800000 | tf_op jit(solution)/shard_map/prepare_0/pallas_call | solution.py:650
  16.2 0.7 %colours.1 = (bf16[8,16,128]{2,1,0:T(8,128)(2,1)S(1)}, bf16[8,16,128]{2,1,0:T(8,128)(2,1)S(1)}, bf16[8,16,128]{2,1,0:T(8,128)(2,1)S(1)}, bf16[8,16,128]{2,1,0:T(8,128)(2,1)S(1)}) custom-call(s32[4]{0:T(128)S(1)} %pad_add_fusion.place_ref.own_ref, f32[3]{0:T(128)S(1)} %copy-done.11, f32[32,3,8,128]{3,2,1,0:T(8,128)S(1)} %get-tuple-element.66.sums_ref, ...), custom_call_target="tpu_custom_call" | custom-call | tf_op jit(solution)/shard_map/colours/pallas_call | solution.py:332
  16.9 1.6 %collective-permute-start.3 = (bf16[8,16,128]{2,1,0:T(8,128)(2,1)S(1)}, bf16[8,16,128]{2,1,0:T(8,128)(2,1)S(1)}, u32[]{:S(2)}, u32[]{:S(2)}) collective-permute-start(bf16[8,16,128]{2,1,0:T(8,128)(2,1)S(1)} %get-tuple-element.75), channel_id=1, source_target_pairs={{0,4},{4,8},{8,12},{12,0},{16,20},{20,24},{24,28},{28,16},{32,36},... | collective-permute-start | bytes 98312 | tf_op jit(solution)/shard_map/ppermute | solution.py:348
  18.6 2.4 %collective-permute-start.4 = (bf16[8,16,128]{2,1,0:T(8,128)(2,1)S(1)}, bf16[8,16,128]{2,1,0:T(8,128)(2,1)S(1)}, u32[]{:S(2)}, u32[]{:S(2)}) collective-permute-start(bf16[8,16,128]{2,1,0:T(8,128)(2,1)S(1)} %get-tuple-element.76), channel_id=1, source_target_pairs={{0,8},{4,12},{8,0},{12,4},{16,24},{20,28},{24,16},{28,20},{32,40},... | collective-permute-start | bytes 98312 | tf_op jit(solution)/shard_map/ppermute | solution.py:348
  20.9 1.7 %prepare_8.1 = (bf16[8,4,128,128]{3,2,1,0:T(8,128)(2,1)S(1)}, bf16[8,4,128,128]{3,2,1,0:T(8,128)(2,1)S(1)}) custom-call(bf16[32,4,128,128]{3,2,1,0:T(8,128)(2,1)S(1)} %get-tuple-element.62.feat_ref, f32[1,128]{1,0:T(1,128)S(1)} %get-tuple-element.63.gain_ref, bf16[256,256]{1,0:T(8,128)(2,1)S(1)} %get-tuple-element.64.mean_ref.refs_9_), custom_call_target="tpu_custom_call" | custom-call | flops 1000000000 | bytes 800000 | tf_op jit(solution)/shard_map/prepare_8/pallas_call | solution.py:650
  23.0 1.3 %collective-permute-done.5.x3_ref = bf16[8,16,128]{2,1,0:T(8,128)(2,1)S(1)} collective-permute-done((bf16[8,16,128]{2,1,0:T(8,128)(2,1)S(1)}, bf16[8,16,128]{2,1,0:T(8,128)(2,1)S(1)}, u32[]{:S(2)}, u32[]{:S(2)}) %collective-permute-start.5) | collective-permute-done | bytes 32800 | tf_op jit(solution)/shard_map/ppermute | solution.py:348
  24.4 11.8 %pose.1 = (bf16[8,16,128]{2,1,0:T(8,128)(2,1)S(1)}, bf16[8,16,128]{2,1,0:T(8,128)(2,1)S(1)}, bf16[8,16,128]{2,1,0:T(8,128)(2,1)S(1)}, bf16[8,16,128]{2,1,0:T(8,128)(2,1)S(1)}) custom-call(s32[4]{0:T(128)S(1)} %pad_add_fusion.place_ref.own_ref, bf16[8,16,128]{2,1,0:T(8,128)(2,1)S(1)} %get-tuple-element.80.x0_ref, ...), custom_call_target="tpu_custom_call" | custom-call | flops 2022400000 | bytes 17825792 | tf_op jit(solution)/shard_map/pose/pallas_call | solution.py:517
  36.4 0.6 %collective-permute-start.7 = (bf16[8,16,128]{2,1,0:T(8,128)(2,1)S(1)}, bf16[8,16,128]{2,1,0:T(8,128)(2,1)S(1)}, u32[]{:S(2)}, u32[]{:S(2)}) collective-permute-start(bf16[8,16,128]{2,1,0:T(8,128)(2,1)S(1)} %get-tuple-element.89), channel_id=1, source_target_pairs={{0,8},{4,12},{8,0},{12,4},{16,24},{20,28},{24,16},{28,20},{32,40},... | collective-permute-start | bytes 98312 | tf_op jit(solution)/shard_map/ppermute | solution.py:348
  37.1 1.7 %prepare_16.1 = (bf16[8,4,128,128]{3,2,1,0:T(8,128)(2,1)S(1)}, bf16[8,4,128,128]{3,2,1,0:T(8,128)(2,1)S(1)}) custom-call(bf16[32,4,128,128]{3,2,1,0:T(8,128)(2,1)S(1)} %get-tuple-element.62.feat_ref, f32[1,128]{1,0:T(1,128)S(1)} %get-tuple-element.63.gain_ref, bf16[256,256]{1,0:T(8,128)(2,1)S(1)} %get-tuple-element.64.mean_ref.refs_9_), custom_call_target="tpu_custom_call" | custom-call | flops 1000000000 | bytes 800000 | tf_op jit(solution)/shard_map/prepare_16/pallas_call | solution.py:650
  39.2 1.2 %collective-permute-done.8.x3_ref = bf16[8,16,128]{2,1,0:T(8,128)(2,1)S(1)} collective-permute-done((bf16[8,16,128]{2,1,0:T(8,128)(2,1)S(1)}, bf16[8,16,128]{2,1,0:T(8,128)(2,1)S(1)}, u32[]{:S(2)}, u32[]{:S(2)}) %collective-permute-start.8) | collective-permute-done | bytes 32800 | tf_op jit(solution)/shard_map/ppermute | solution.py:348
  40.4 0.7 %strip_grads.1 = (f32[32,3,8,128]{3,2,1,0:T(8,128)S(1)}, f32[3,32,128]{2,1,0:T(8,128)S(1)}, f32[3,32,128]{2,1,0:T(8,128)S(1)}) custom-call(s32[4]{0:T(128)S(1)} %pad_add_fusion.place_ref.own_ref, bf16[8,16,128]{2,1,0:T(8,128)(2,1)S(1)} %get-tuple-element.93.x0_ref, bf16[8,16,128]{2,1,0:T(8,128)(2,1)S(1)} %collective-permute-done.6.x1_ref, ...), custom_call_target="tpu_custom_call" | custom-call | tf_op jit(solution)/shard_map/strip_grads/pallas_call | solution.py:576
  41.1 2.2 %collective-permute-start.10 = (f32[3,32,128]{2,1,0:T(8,128)S(1)}, f32[3,32,128]{2,1,0:T(8,128)S(1)}, u32[]{:S(2)}, u32[]{:S(2)}) collective-permute-start(f32[3,32,128]{2,1,0:T(8,128)S(1)} %get-tuple-element.98), channel_id=1, source_target_pairs={{0,0},{4,8},{8,4},{12,16},{16,12},{20,24},{24,20},{28,32},{32,28},... | collective-permute-start | bytes 147464 | tf_op jit(solution)/shard_map/ppermute | solution.py:356
  43.3 3.9 %collective-permute-start.9 = (f32[3,32,128]{2,1,0:T(8,128)S(1)}, f32[3,32,128]{2,1,0:T(8,128)S(1)}, u32[]{:S(2)}, u32[]{:S(2)}) collective-permute-start(f32[3,32,128]{2,1,0:T(8,128)S(1)} %get-tuple-element.97), channel_id=1, source_target_pairs={{0,4},{4,0},{8,12},{12,8},{16,20},{20,16},{24,28},{28,24},{32,36},... | collective-permute-start | bytes 147464 | tf_op jit(solution)/shard_map/ppermute | solution.py:356
  47.2 1.7 %prepare_24.1 = (bf16[8,4,128,128]{3,2,1,0:T(8,128)(2,1)S(1)}, bf16[8,4,128,128]{3,2,1,0:T(8,128)(2,1)S(1)}) custom-call(bf16[32,4,128,128]{3,2,1,0:T(8,128)(2,1)S(1)} %get-tuple-element.62.feat_ref, f32[1,128]{1,0:T(1,128)S(1)} %get-tuple-element.63.gain_ref, bf16[256,256]{1,0:T(8,128)(2,1)S(1)} %get-tuple-element.64.mean_ref.refs_9_), custom_call_target="tpu_custom_call" | custom-call | flops 1000000000 | bytes 800000 | tf_op jit(solution)/shard_map/prepare_24/pallas_call | solution.py:650
  48.9 0.7 %whole_grads.1 = (f32[32,3,8,128]{3,2,1,0:T(8,128)S(1)}, f32[2,3,8,128]{3,2,1,0:T(8,128)S(1)}) custom-call(s32[4]{0:T(128)S(1)} %pad_add_fusion.place_ref.own_ref, f32[32,3,8,128]{3,2,1,0:T(8,128)S(1)} %get-tuple-element.103.x_ref, f32[3,32,128]{2,1,0:T(8,128)S(1)} %collective-permute-done.9.inside_ref, f32[3,32,128]{2,1,0:T(8,128)S(1)} %collective-permute-done.10.across_ref), custom_call_target="tpu_custom_call" | custom-call | tf_op jit(solution)/shard_map/whole_grads/pallas_call | solution.py:600
  49.6 1.5 %collective-permute-start.11 = (f32[2,3,8,128]{3,2,1,0:T(8,128)S(1)}, f32[2,3,8,128]{3,2,1,0:T(8,128)S(1)}, u32[]{:S(2)}, u32[]{:S(2)}) collective-permute-start(f32[2,3,8,128]{3,2,1,0:T(8,128)S(1)} %get-tuple-element.107), channel_id=1, source_target_pairs={{1,0},{2,1},{3,2},{0,3},{5,4},{6,5},{7,6},{4,7},{9,8},{10,9},{11,1... | collective-permute-start | bytes 73736 | tf_op jit(solution)/shard_map/ppermute | solution.py:831
  51.1 5.1 %conv_back.1.prior_hbm = bf16[32,4,128,128]{3,2,1,0:T(8,128)(2,1)} custom-call(bf16[8,4,128,128]{3,2,1,0:T(8,128)(2,1)S(1)} %get-tuple-element.109.refs_0_, bf16[8,4,128,128]{3,2,1,0:T(8,128)(2,1)S(1)} %get-tuple-element.110.refs_1_, bf16[8,4,128,128]{3,2,1,0:T(8,128)(2,1)S(1)} %get-tuple-element.111.refs_2_, ...), custom_call_target="tpu_custom_call" | custom-call | flops 33554432 | bytes 9437184 | tf_op jit(solution)/shard_map/conv_back/pallas_call | solution.py:734
  56.2 1.8 %conv_last.1 = bf16[32,4,128,128]{3,2,1,0:T(8,128)(2,1)} custom-call(s32[4]{0:T(128)S(1)} %pad_add_fusion.place_ref.own_ref, bf16[8,4,128,128]{3,2,1,0:T(8,128)(2,1)S(1)} %get-tuple-element.101.refs_6_.slope_ref, bf16[8,4,128,128]{3,2,1,0:T(8,128)(2,1)S(1)} %get-tuple-element.102.refs_7_.normed_ref, ...), custom_call_target="tpu_custom_call", output_to_operand_aliasing={{}: (7, {})} | custom-call | tf_op jit(solution)/shard_map/conv_last/pallas_call | solution.py:750
  (38 shorter events, 1.4 us)
Async XLA Ops:
  2.7 6.1 %collective-permute-start = (f32[2,3,8,128]{3,2,1,0:T(8,128)S(1)}, f32[2,3,8,128]{3,2,1,0:T(8,128)S(1)}, u32[]{:S(2)}, u32[]{:S(2)}) collective-permute-start(f32[2,3,8,128]{3,2,1,0:T(8,128)S(1)} %get-tuple-element.67), channel_id=1, source_target_pairs={{0,1},{1,2},{2,3},{3,0},{4,5},{5,6},{6,7},{7,4},{8,9},{9,10},{10,1... | collective-permute-start | bytes 73736 | tf_op jit(solution)/shard_map/ppermute | solution.py:802
  8.7 7.4 %copy-start.11 = (f32[3]{0:T(128)S(1)}, f32[3]{0:T(128)}, u32[]{:S(2)}) copy-start(f32[3]{0:T(128)} %bias_ref.1) | copy-start | bytes 40
  9.4 6.5 %collective-permute-start.1 = (f32[3,32,128]{2,1,0:T(8,128)S(1)}, f32[3,32,128]{2,1,0:T(8,128)S(1)}, u32[]{:S(2)}, u32[]{:S(2)}) collective-permute-start(f32[3,32,128]{2,1,0:T(8,128)S(1)} %get-tuple-element.68), channel_id=1, source_target_pairs={{0,4},{4,0},{8,12},{12,8},{16,20},{20,16},{24,28},{28,24},{32,36},... | collective-permute-start | bytes 147464 | tf_op jit(solution)/shard_map/ppermute | solution.py:356
  10.4 13.9 %copy-start = (bf16[768,1280]{1,0:T(8,128)(2,1)S(1)}, bf16[768,1280]{1,0:T(8,128)(2,1)}, u32[]{:S(2)}) copy-start(bf16[768,1280]{1,0:T(8,128)(2,1)} %patch_hbm.1) | copy-start | bytes 5898244
  10.4 13.9 %copy-start.1 = (bf16[768,768]{1,0:T(8,128)(2,1)S(1)}, bf16[768,768]{1,0:T(8,128)(2,1)}, u32[]{:S(2)}) copy-start(bf16[768,768]{1,0:T(8,128)(2,1)} %constant.27.clone.order_hbm) | copy-start | bytes 3538948
  10.4 13.9 %copy-start.2 = (bf16[1280,272]{0,1:T(8,128)(2,1)S(1)}, bf16[1280,272]{0,1:T(8,128)(2,1)}, u32[]{:S(2)}) copy-start(bf16[1280,272]{0,1:T(8,128)(2,1)} %param.34) | copy-start | bytes 2088964
  10.4 13.9 %copy-start.3 = (bf16[64,1280]{1,0:T(8,128)(2,1)S(1)}, bf16[64,1280]{1,0:T(8,128)(2,1)}, u32[]{:S(2)}) copy-start(bf16[64,1280]{1,0:T(8,128)(2,1)} %position_hbm.1) | copy-start | bytes 491524
  10.4 13.9 %copy-start.4 = (bf16[17,272]{1,0:T(8,128)(2,1)S(1)}, bf16[17,272]{1,0:T(8,128)(2,1)}, u32[]{:S(2)}) copy-start(bf16[17,272]{1,0:T(8,128)(2,1)} %constant.26.clone.key_spread_ref) | copy-start | bytes 27748
  10.4 13.9 %copy-start.5 = (s32[32,17]{0,1:T(8,128)S(1)}, s32[32,17]{0,1:T(8,128)}, u32[]{:S(2)}) copy-start(s32[32,17]{0,1:T(8,128)} %param.26) | copy-start | bytes 6532
  10.4 13.9 %copy-start.6 = (s32[32,17]{0,1:T(8,128)S(1)}, s32[32,17]{0,1:T(8,128)}, u32[]{:S(2)}) copy-start(s32[32,17]{0,1:T(8,128)} %param.27) | copy-start | bytes 6532
  10.5 13.9 %copy-start.7 = (s32[32,17]{0,1:T(8,128)S(1)}, s32[32,17]{0,1:T(8,128)}, u32[]{:S(2)}) copy-start(s32[32,17]{0,1:T(8,128)} %param.28) | copy-start | bytes 6532
  10.5 13.9 %copy-start.8 = (f32[1280]{0:T(1024)S(1)}, f32[1280]{0:T(1024)}, u32[]{:S(2)}) copy-start(f32[1280]{0:T(1024)} %param.31) | copy-start | bytes 15364
  10.5 13.9 %copy-start.9 = (s32[1,32,3]{1,0,2:T(1,128)S(1)}, s32[1,32,3]{1,0,2:T(1,128)}, u32[]{:S(2)}) copy-start(s32[1,32,3]{1,0,2:T(1,128)} %param.24) | copy-start | bytes 1156
  10.5 13.9 %copy-start.10 = (s32[1,32]{1,0:T(1,128)S(1)}, s32[1,32]{1,0:T(1,128)}, u32[]{:S(2)}) copy-start(s32[1,32]{1,0:T(1,128)} %counts_ref.1) | copy-start | bytes 388
  10.5 5.7 %collective-permute-start.2 = (f32[3,32,128]{2,1,0:T(8,128)S(1)}, f32[3,32,128]{2,1,0:T(8,128)S(1)}, u32[]{:S(2)}, u32[]{:S(2)}) collective-permute-start(f32[3,32,128]{2,1,0:T(8,128)S(1)} %get-tuple-element.69), channel_id=1, source_target_pairs={{0,0},{4,8},{8,4},{12,16},{16,12},{20,24},{24,20},{28,32},{32,28},... | collective-permute-start | bytes 147464 | tf_op jit(solution)/shard_map/ppermute | solution.py:356
  16.9 5.7 %collective-permute-start.3 = (bf16[8,16,128]{2,1,0:T(8,128)(2,1)S(1)}, bf16[8,16,128]{2,1,0:T(8,128)(2,1)S(1)}, u32[]{:S(2)}, u32[]{:S(2)}) collective-permute-start(bf16[8,16,128]{2,1,0:T(8,128)(2,1)S(1)} %get-tuple-element.75), channel_id=1, source_target_pairs={{0,4},{4,8},{8,12},{12,0},{16,20},{20,24},{24,28},{28,16},{32,36},... | collective-permute-start | bytes 98312 | tf_op jit(solution)/shard_map/ppermute | solution.py:348
  18.6 4.4 %collective-permute-start.4 = (bf16[8,16,128]{2,1,0:T(8,128)(2,1)S(1)}, bf16[8,16,128]{2,1,0:T(8,128)(2,1)S(1)}, u32[]{:S(2)}, u32[]{:S(2)}) collective-permute-start(bf16[8,16,128]{2,1,0:T(8,128)(2,1)S(1)} %get-tuple-element.76), channel_id=1, source_target_pairs={{0,8},{4,12},{8,0},{12,4},{16,24},{20,28},{24,16},{28,20},{32,40},... | collective-permute-start | bytes 98312 | tf_op jit(solution)/shard_map/ppermute | solution.py:348
  20.9 3.3 %collective-permute-start.5 = (bf16[8,16,128]{2,1,0:T(8,128)(2,1)S(1)}, bf16[8,16,128]{2,1,0:T(8,128)(2,1)S(1)}, u32[]{:S(2)}, u32[]{:S(2)}) collective-permute-start(bf16[8,16,128]{2,1,0:T(8,128)(2,1)S(1)} %get-tuple-element.77), channel_id=1, source_target_pairs={{0,12},{4,0},{8,4},{12,8},{16,28},{20,16},{24,20},{28,24},{32,44},... | collective-permute-start | bytes 98312 | tf_op jit(solution)/shard_map/ppermute | solution.py:348
  36.2 2.5 %collective-permute-start.6 = (bf16[8,16,128]{2,1,0:T(8,128)(2,1)S(1)}, bf16[8,16,128]{2,1,0:T(8,128)(2,1)S(1)}, u32[]{:S(2)}, u32[]{:S(2)}) collective-permute-start(bf16[8,16,128]{2,1,0:T(8,128)(2,1)S(1)} %get-tuple-element.88), channel_id=1, source_target_pairs={{0,4},{4,8},{8,12},{12,0},{16,20},{20,24},{24,28},{28,16},{32,36},... | collective-permute-start | bytes 98312 | tf_op jit(solution)/shard_map/ppermute | solution.py:348
  36.4 2.8 %collective-permute-start.7 = (bf16[8,16,128]{2,1,0:T(8,128)(2,1)S(1)}, bf16[8,16,128]{2,1,0:T(8,128)(2,1)S(1)}, u32[]{:S(2)}, u32[]{:S(2)}) collective-permute-start(bf16[8,16,128]{2,1,0:T(8,128)(2,1)S(1)} %get-tuple-element.89), channel_id=1, source_target_pairs={{0,8},{4,12},{8,0},{12,4},{16,24},{20,28},{24,16},{28,20},{32,40},... | collective-permute-start | bytes 98312 | tf_op jit(solution)/shard_map/ppermute | solution.py:348
  37.0 3.4 %collective-permute-start.8 = (bf16[8,16,128]{2,1,0:T(8,128)(2,1)S(1)}, bf16[8,16,128]{2,1,0:T(8,128)(2,1)S(1)}, u32[]{:S(2)}, u32[]{:S(2)}) collective-permute-start(bf16[8,16,128]{2,1,0:T(8,128)(2,1)S(1)} %get-tuple-element.90), channel_id=1, source_target_pairs={{0,12},{4,0},{8,4},{12,8},{16,28},{20,16},{24,20},{28,24},{32,44},... | collective-permute-start | bytes 98312 | tf_op jit(solution)/shard_map/ppermute | solution.py:348
  41.1 7.8 %collective-permute-start.10 = (f32[3,32,128]{2,1,0:T(8,128)S(1)}, f32[3,32,128]{2,1,0:T(8,128)S(1)}, u32[]{:S(2)}, u32[]{:S(2)}) collective-permute-start(f32[3,32,128]{2,1,0:T(8,128)S(1)} %get-tuple-element.98), channel_id=1, source_target_pairs={{0,0},{4,8},{8,4},{12,16},{16,12},{20,24},{24,20},{28,32},{32,28},... | collective-permute-start | bytes 147464 | tf_op jit(solution)/shard_map/ppermute | solution.py:356
  43.3 5.6 %collective-permute-start.9 = (f32[3,32,128]{2,1,0:T(8,128)S(1)}, f32[3,32,128]{2,1,0:T(8,128)S(1)}, u32[]{:S(2)}, u32[]{:S(2)}) collective-permute-start(f32[3,32,128]{2,1,0:T(8,128)S(1)} %get-tuple-element.97), channel_id=1, source_target_pairs={{0,4},{4,0},{8,12},{12,8},{16,20},{20,16},{24,28},{28,24},{32,36},... | collective-permute-start | bytes 147464 | tf_op jit(solution)/shard_map/ppermute | solution.py:356
  49.6 6.7 %collective-permute-start.11 = (f32[2,3,8,128]{3,2,1,0:T(8,128)S(1)}, f32[2,3,8,128]{3,2,1,0:T(8,128)S(1)}, u32[]{:S(2)}, u32[]{:S(2)}) collective-permute-start(f32[2,3,8,128]{3,2,1,0:T(8,128)S(1)} %get-tuple-element.107), channel_id=1, source_target_pairs={{1,0},{2,1},{3,2},{0,3},{5,4},{6,5},{7,6},{4,7},{9,8},{10,9},{11,1... | collective-permute-start | bytes 73736 | tf_op jit(solution)/shard_map/ppermute | solution.py:831

commit v5 on v4

--- a/solution.py
+++ b/solution.py
@@ -288,12 +288,12 @@
             out_ref[o] = sums_ref[:, o, k, :]
             out_ref[o, 0:2] = sums_ref[0:2, o, k, :] + unless(first_block, prior_ref[:, o, k, :])
     even = is_even(place_ref)
-    inside_ref[...] = jnp.where(even, down[...], up[...])
-    across_ref[...] = jnp.where(even, up[...], down[...])
+    inside_ref[...] = jnp.where(even, down[...], up[...]).astype(BF16)
+    across_ref[...] = jnp.where(even, up[...], down[...]).astype(BF16)
 
 
 def rims(place, sums, prior):
-    shape = jax.ShapeDtypeStruct((3, sums.shape[0], COLS), F32)
+    shape = jax.ShapeDtypeStruct((3, sums.shape[0], COLS), BF16)
     return pl.pallas_call(
         rim_kernel,
         in_specs=[SMEM] + [VMEM] * 2,
@@ -306,23 +306,23 @@
 
 
 def colour_kernel(own_ref, bias_ref, sums_ref, prior_ref, inside_ref, across_ref, *rest):
-    out_refs, total = rest[:GROUP], rest[GROUP]
+    out_refs, (total, above_rim, below_rim) = rest[:GROUP], rest[GROUP:]
     total[...] = sums_ref[...]
     total[0:2] = sums_ref[0:2] + unless(own_ref[1] == 0, prior_ref[...])
     top, bottom = own_ref[0] == 0, own_ref[0] == own_ref[2] - 1
     row = sublanes_of((8, 8, COLS))
     me = lax.rem(own_ref[0], GROUP)
     even = is_even(own_ref)
+    inside, across = inside_ref[...].astype(F32), across_ref[...].astype(F32)
+    above_rim[...] = unless(top, jnp.where(even, across, inside))
+    below_rim[...] = unless(bottom, jnp.where(even, inside, across))
     for turn in range(GROUP):
         frames = pl.ds(pl.multiple_of(lax.rem(me + turn, GROUP) * 8, 8), 8)
         groups = []
         for o in range(3):
             value = total[frames, o]
-            inside, across = inside_ref[o, frames, :], across_ref[o, frames, :]
-            above = unless(top, jnp.where(even, across, inside))
-            below = unless(bottom, jnp.where(even, inside, across))
-            value += jnp.where(row == 1, above[:, None, :], 0.0)
-            value += jnp.where(row == 4, below[:, None, :], 0.0)
+            value += jnp.where(row == 1, above_rim[o, frames, :][:, None, :], 0.0)
+            value += jnp.where(row == 4, below_rim[o, frames, :][:, None, :], 0.0)
             groups.append(roll(value, -1, 1) + bias_ref[o])
         out_refs[turn][...] = lay_rows(groups).astype(BF16)
 
@@ -334,7 +334,8 @@
         in_specs=[SMEM] * 2 + [VMEM] * 4,
         out_specs=[VMEM] * GROUP,
         out_shape=[shape] * GROUP,
-        scratch_shapes=[pltpu.VMEM(sums.shape, F32)],
+        scratch_shapes=[pltpu.VMEM(sums.shape, F32)]
+        + [pltpu.VMEM((3, sums.shape[0], COLS), F32)] * 2,
         compiler_params=megabytes(4),
         name="colours",
     )(own, bias, sums, prior, inside, across)
@@ -567,12 +568,12 @@
     even = is_even(own_ref)
     for o in range(3):
         upper, lower = out_ref[:, o, 1, :], out_ref[:, o, 4, :]
-        inside_ref[o] = jnp.where(even, lower, upper)
-        across_ref[o] = jnp.where(even, upper, lower)
+        inside_ref[o] = jnp.where(even, lower, upper).astype(BF16)
+        across_ref[o] = jnp.where(even, upper, lower).astype(BF16)
 
 
 def strip_grads(own, parts):
-    rim = jax.ShapeDtypeStruct((3, 32, COLS), F32)
+    rim = jax.ShapeDtypeStruct((3, 32, COLS), BF16)
     return pl.pallas_call(
         strip_kernel,
         in_specs=[SMEM] + [VMEM] * GROUP,
@@ -588,8 +589,9 @@
     top, bottom = place_ref[0] == 0, place_ref[0] == place_ref[2] - 1
     even = is_even(place_ref)
     for o in range(3):
-        above = unless(top, jnp.where(even, across_ref[o], inside_ref[o]))
-        below = unless(bottom, jnp.where(even, inside_ref[o], across_ref[o]))
+        inside, across = inside_ref[o].astype(F32), across_ref[o].astype(F32)
+        above = unless(top, jnp.where(even, across, inside))
+        below = unless(bottom, jnp.where(even, inside, across))
         value = jnp.where(row == 0, above[:, None, :], x_ref[:, o])
         value = jnp.where(row == 5, below[:, None, :], value)
         out_ref[:, o] = value

time: 58.3 us -> 58.1 us (level)
  transfers between devices with their start and end apart: 12 -> 12, of which waited for: 5 -> 4; matrix products, arithmetic and copies ran while one was open for 0% -> 0% of each run, Pallas kernels for 28% -> 28%
where the time goes in v5:
time: 58.1 us; the launch traced here: 58 us
  Pallas kernels  35.4 us (61%)
  starting transfers between devices  18.7 us (32%)
  waiting for transfers between devices  3.28 us (6%)
    pallas_call x1, Pallas kernels, pose(): pl.pallas_call(pose_kernel, in_specs=[SMEM] + [VMEM] * 13 + [ANYWHERE] *...  11.8 us
    pallas_call x4, Pallas kernels, prepare(): pl.pallas_call(functools.partial(prepare_kernel, start), in_specs=[VMEM]...  6.61 us
    ppermute x2, starting transfers between devices, swap_rims(): lax.ppermute(across, 'tile', others)  5.98 us
    pallas_call x1, Pallas kernels, conv_backward(): pl.pallas_call(back_kernel, in_specs=[VMEM] * (len(kept) * 2 + 3), out_sp...  5.1 us
    ppermute x6, starting transfers between devices, swap_turns(): out.append(lax.ppermute(parts[turn], 'tile', pairs))  5.08 us
    ppermute x2, starting transfers between devices, swap_rims(): lax.ppermute(inside, 'tile', pairs)  4.79 us
    pallas_call x1, Pallas kernels, conv_main(): pl.pallas_call(conv_kernel, in_specs=[VMEM] * 4 + [ANYWHERE] * 2, out_spe...  4.76 us
    ppermute x6, waiting for transfers between devices, swap_turns(): out.append(lax.ppermute(parts[turn], 'tile', pairs))  3.26 us
  transfers between devices with their start and end apart: 12, of which 4 were waited for; matrix products, arithmetic and copies ran while one was open for 0% of the time, Pallas kernels for 28%

profile of v5, /device:TPU:25, one launch (start us, length us, event | category | flops | bytes accessed | tf_op | source)
XLA Modules:
  0.0 58.0 jit_solution(3503339845171468472)
XLA Ops:
  0.1 2.6 %conv_tail.1 = (f32[2,3,8,128]{3,2,1,0:T(8,128)S(1)}, bf16[32,4,128,128]{3,2,1,0:T(8,128)(2,1)S(1)}, bf16[1024,256]{1,0:T(8,128)(2,1)S(1)}, bf16[256,1024]{1,0:T...) custom-call(bf16[32,4,128,128]{3,2,1,0:T(8,128)(2,1)} %feat_hbm, f32[1,128]{1,0:T(1,128)} %bitcast.17, ...), custom_call_target="tpu_custom_call" | custom-call | tf_op jit(solution)/shard_map/conv_tail/pallas_call | solution.py:226
  2.7 1.3 %collective-permute-start = (f32[2,3,8,128]{3,2,1,0:T(8,128)S(1)}, f32[2,3,8,128]{3,2,1,0:T(8,128)S(1)}, u32[]{:S(2)}, u32[]{:S(2)}) collective-permute-start(f32[2,3,8,128]{3,2,1,0:T(8,128)S(1)} %get-tuple-element.67), channel_id=1, source_target_pairs={{0,1},{1,2},{2,3},{3,0},{4,5},{5,6},{6,7},{7,4},{8,9},{9,10},{10,1... | collective-permute-start | bytes 73736 | tf_op jit(solution)/shard_map/ppermute | solution.py:804
  4.0 4.8 %conv_main.1 = (f32[32,3,8,128]{3,2,1,0:T(8,128)S(1)}, bf16[1280,2560]{1,0:T(8,128)(2,1)S(1)}, bf16[2560,1280]{1,0:T(8,128)(2,1)S(1)}) custom-call(bf16[32,4,128,128]{3,2,1,0:T(8,128)(2,1)S(1)} %get-tuple-element.62.feat_ref, f32[1,128]{1,0:T(1,128)S(1)} %get-tuple-element.63.gain_ref, bf16[256,256]{1,0:T(8,128)(2,1)S(1)} %get-tuple-element.64.mean_ref.refs_9_, ...), custom_call_target="tpu_custom_call" | custom-call | flops 33554432 | bytes 20971520 | tf_op jit(solution)/shard_map/conv_main/pallas_call | solution.py:252
  8.8 0.6 %rims.1 = (bf16[3,32,128]{2,1,0:T(8,128)(2,1)S(1)}, bf16[3,32,128]{2,1,0:T(8,128)(2,1)S(1)}) custom-call(s32[4]{0:T(128)S(1)} %pad_add_fusion.place_ref.own_ref, f32[32,3,8,128]{3,2,1,0:T(8,128)S(1)} %get-tuple-element.66.sums_ref, f32[2,3,8,128]{3,2,1,0:T(8,128)S(1)} %collective-permute-done.prior_ref), custom_call_target="tpu_custom_call" | custom-call | tf_op jit(solution)/shard_map/rims/pallas_call | solution.py:297
  9.4 1.0 %collective-permute-start.1 = (bf16[3,32,128]{2,1,0:T(8,128)(2,1)S(1)}, bf16[3,32,128]{2,1,0:T(8,128)(2,1)S(1)}, u32[]{:S(2)}, u32[]{:S(2)}) collective-permute-start(bf16[3,32,128]{2,1,0:T(8,128)(2,1)S(1)} %get-tuple-element.68), channel_id=1, source_target_pairs={{0,4},{4,0},{8,12},{12,8},{16,20},{20,16},{24,28},{28,24},{32,36},... | collective-permute-start | bytes 73736 | tf_op jit(solution)/shard_map/ppermute | solution.py:357
  10.5 3.7 %collective-permute-start.2 = (bf16[3,32,128]{2,1,0:T(8,128)(2,1)S(1)}, bf16[3,32,128]{2,1,0:T(8,128)(2,1)S(1)}, u32[]{:S(2)}, u32[]{:S(2)}) collective-permute-start(bf16[3,32,128]{2,1,0:T(8,128)(2,1)S(1)} %get-tuple-element.69), channel_id=1, source_target_pairs={{0,0},{4,8},{8,4},{12,16},{16,12},{20,24},{24,20},{28,32},{32,28},... | collective-permute-start | bytes 73736 | tf_op jit(solution)/shard_map/ppermute | solution.py:357
  14.3 1.7 %prepare_0.1 = (bf16[8,4,128,128]{3,2,1,0:T(8,128)(2,1)S(1)}, bf16[8,4,128,128]{3,2,1,0:T(8,128)(2,1)S(1)}) custom-call(bf16[32,4,128,128]{3,2,1,0:T(8,128)(2,1)S(1)} %get-tuple-element.62.feat_ref, f32[1,128]{1,0:T(1,128)S(1)} %get-tuple-element.63.gain_ref, bf16[256,256]{1,0:T(8,128)(2,1)S(1)} %get-tuple-element.64.mean_ref.refs_9_), custom_call_target="tpu_custom_call" | custom-call | flops 1000000000 | bytes 800000 | tf_op jit(solution)/shard_map/prepare_0/pallas_call | solution.py:652
  16.0 0.7 %colours.1 = (bf16[8,16,128]{2,1,0:T(8,128)(2,1)S(1)}, bf16[8,16,128]{2,1,0:T(8,128)(2,1)S(1)}, bf16[8,16,128]{2,1,0:T(8,128)(2,1)S(1)}, bf16[8,16,128]{2,1,0:T(8,128)(2,1)S(1)}) custom-call(s32[4]{0:T(128)S(1)} %pad_add_fusion.place_ref.own_ref, f32[3]{0:T(128)S(1)} %copy-done.11, f32[32,3,8,128]{3,2,1,0:T(8,128)S(1)} %get-tuple-element.66.sums_ref, ...), custom_call_target="tpu_custom_call" | custom-call | tf_op jit(solution)/shard_map/colours/pallas_call | solution.py:332
  16.7 1.6 %collective-permute-start.3 = (bf16[8,16,128]{2,1,0:T(8,128)(2,1)S(1)}, bf16[8,16,128]{2,1,0:T(8,128)(2,1)S(1)}, u32[]{:S(2)}, u32[]{:S(2)}) collective-permute-start(bf16[8,16,128]{2,1,0:T(8,128)(2,1)S(1)} %get-tuple-element.75), channel_id=1, source_target_pairs={{0,4},{4,8},{8,12},{12,0},{16,20},{20,24},{24,28},{28,16},{32,36},... | collective-permute-start | bytes 98312 | tf_op jit(solution)/shard_map/ppermute | solution.py:349
  18.3 2.6 %collective-permute-start.4 = (bf16[8,16,128]{2,1,0:T(8,128)(2,1)S(1)}, bf16[8,16,128]{2,1,0:T(8,128)(2,1)S(1)}, u32[]{:S(2)}, u32[]{:S(2)}) collective-permute-start(bf16[8,16,128]{2,1,0:T(8,128)(2,1)S(1)} %get-tuple-element.76), channel_id=1, source_target_pairs={{0,8},{4,12},{8,0},{12,4},{16,24},{20,28},{24,16},{28,20},{32,40},... | collective-permute-start | bytes 98312 | tf_op jit(solution)/shard_map/ppermute | solution.py:349
  20.9 1.7 %prepare_8.1 = (bf16[8,4,128,128]{3,2,1,0:T(8,128)(2,1)S(1)}, bf16[8,4,128,128]{3,2,1,0:T(8,128)(2,1)S(1)}) custom-call(bf16[32,4,128,128]{3,2,1,0:T(8,128)(2,1)S(1)} %get-tuple-element.62.feat_ref, f32[1,128]{1,0:T(1,128)S(1)} %get-tuple-element.63.gain_ref, bf16[256,256]{1,0:T(8,128)(2,1)S(1)} %get-tuple-element.64.mean_ref.refs_9_), custom_call_target="tpu_custom_call" | custom-call | flops 1000000000 | bytes 800000 | tf_op jit(solution)/shard_map/prepare_8/pallas_call | solution.py:652
  22.9 1.3 %collective-permute-done.5.x3_ref = bf16[8,16,128]{2,1,0:T(8,128)(2,1)S(1)} collective-permute-done((bf16[8,16,128]{2,1,0:T(8,128)(2,1)S(1)}, bf16[8,16,128]{2,1,0:T(8,128)(2,1)S(1)}, u32[]{:S(2)}, u32[]{:S(2)}) %collective-permute-start.5) | collective-permute-done | bytes 32800 | tf_op jit(solution)/shard_map/ppermute | solution.py:349
  24.3 11.8 %pose.1 = (bf16[8,16,128]{2,1,0:T(8,128)(2,1)S(1)}, bf16[8,16,128]{2,1,0:T(8,128)(2,1)S(1)}, bf16[8,16,128]{2,1,0:T(8,128)(2,1)S(1)}, bf16[8,16,128]{2,1,0:T(8,128)(2,1)S(1)}) custom-call(s32[4]{0:T(128)S(1)} %pad_add_fusion.place_ref.own_ref, bf16[8,16,128]{2,1,0:T(8,128)(2,1)S(1)} %get-tuple-element.80.x0_ref, ...), custom_call_target="tpu_custom_call" | custom-call | flops 2022400000 | bytes 17825792 | tf_op jit(solution)/shard_map/pose/pallas_call | solution.py:518
  36.3 0.6 %collective-permute-start.7 = (bf16[8,16,128]{2,1,0:T(8,128)(2,1)S(1)}, bf16[8,16,128]{2,1,0:T(8,128)(2,1)S(1)}, u32[]{:S(2)}, u32[]{:S(2)}) collective-permute-start(bf16[8,16,128]{2,1,0:T(8,128)(2,1)S(1)} %get-tuple-element.89), channel_id=1, source_target_pairs={{0,8},{4,12},{8,0},{12,4},{16,24},{20,28},{24,16},{28,20},{32,40},... | collective-permute-start | bytes 98312 | tf_op jit(solution)/shard_map/ppermute | solution.py:349
  37.0 1.7 %prepare_16.1 = (bf16[8,4,128,128]{3,2,1,0:T(8,128)(2,1)S(1)}, bf16[8,4,128,128]{3,2,1,0:T(8,128)(2,1)S(1)}) custom-call(bf16[32,4,128,128]{3,2,1,0:T(8,128)(2,1)S(1)} %get-tuple-element.62.feat_ref, f32[1,128]{1,0:T(1,128)S(1)} %get-tuple-element.63.gain_ref, bf16[256,256]{1,0:T(8,128)(2,1)S(1)} %get-tuple-element.64.mean_ref.refs_9_), custom_call_target="tpu_custom_call" | custom-call | flops 1000000000 | bytes 800000 | tf_op jit(solution)/shard_map/prepare_16/pallas_call | solution.py:652
  39.1 1.2 %collective-permute-done.8.x3_ref = bf16[8,16,128]{2,1,0:T(8,128)(2,1)S(1)} collective-permute-done((bf16[8,16,128]{2,1,0:T(8,128)(2,1)S(1)}, bf16[8,16,128]{2,1,0:T(8,128)(2,1)S(1)}, u32[]{:S(2)}, u32[]{:S(2)}) %collective-permute-start.8) | collective-permute-done | bytes 32800 | tf_op jit(solution)/shard_map/ppermute | solution.py:349
  40.3 0.7 %strip_grads.1 = (f32[32,3,8,128]{3,2,1,0:T(8,128)S(1)}, bf16[3,32,128]{2,1,0:T(8,128)(2,1)S(1)}, bf16[3,32,128]{2,1,0:T(8,128)(2,1)S(1)}) custom-call(s32[4]{0:T(128)S(1)} %pad_add_fusion.place_ref.own_ref, bf16[8,16,128]{2,1,0:T(8,128)(2,1)S(1)} %get-tuple-element.93.x0_ref, bf16[8,16,128]{2,1,0:T(8,128)(2,1)S(1)} %collective-permute-done.6.x1_ref, ...), custom_call_target="tpu_custom_call" | custom-call | tf_op jit(solution)/shard_map/strip_grads/pallas_call | solution.py:577
  41.0 2.2 %collective-permute-start.10 = (bf16[3,32,128]{2,1,0:T(8,128)(2,1)S(1)}, bf16[3,32,128]{2,1,0:T(8,128)(2,1)S(1)}, u32[]{:S(2)}, u32[]{:S(2)}) collective-permute-start(bf16[3,32,128]{2,1,0:T(8,128)(2,1)S(1)} %get-tuple-element.98), channel_id=1, source_target_pairs={{0,0},{4,8},{8,4},{12,16},{16,12},{20,24},{24,20},{28,32},{32,28},... | collective-permute-start | bytes 73736 | tf_op jit(solution)/shard_map/ppermute | solution.py:357
  43.3 3.8 %collective-permute-start.9 = (bf16[3,32,128]{2,1,0:T(8,128)(2,1)S(1)}, bf16[3,32,128]{2,1,0:T(8,128)(2,1)S(1)}, u32[]{:S(2)}, u32[]{:S(2)}) collective-permute-start(bf16[3,32,128]{2,1,0:T(8,128)(2,1)S(1)} %get-tuple-element.97), channel_id=1, source_target_pairs={{0,4},{4,0},{8,12},{12,8},{16,20},{20,16},{24,28},{28,24},{32,36},... | collective-permute-start | bytes 73736 | tf_op jit(solution)/shard_map/ppermute | solution.py:357
  47.0 1.6 %prepare_24.1 = (bf16[8,4,128,128]{3,2,1,0:T(8,128)(2,1)S(1)}, bf16[8,4,128,128]{3,2,1,0:T(8,128)(2,1)S(1)}) custom-call(bf16[32,4,128,128]{3,2,1,0:T(8,128)(2,1)S(1)} %get-tuple-element.62.feat_ref, f32[1,128]{1,0:T(1,128)S(1)} %get-tuple-element.63.gain_ref, bf16[256,256]{1,0:T(8,128)(2,1)S(1)} %get-tuple-element.64.mean_ref.refs_9_), custom_call_target="tpu_custom_call" | custom-call | flops 1000000000 | bytes 800000 | tf_op jit(solution)/shard_map/prepare_24/pallas_call | solution.py:652
  48.7 0.7 %whole_grads.1 = (f32[32,3,8,128]{3,2,1,0:T(8,128)S(1)}, f32[2,3,8,128]{3,2,1,0:T(8,128)S(1)}) custom-call(s32[4]{0:T(128)S(1)} %pad_add_fusion.place_ref.own_ref, f32[32,3,8,128]{3,2,1,0:T(8,128)S(1)} %get-tuple-element.103.x_ref, bf16[3,32,128]{2,1,0:T(8,128)(2,1)S(1)} %collective-permute-done.9.inside_ref, ...), custom_call_target="tpu_custom_call" | custom-call | tf_op jit(solution)/shard_map/whole_grads/pallas_call | solution.py:602
  49.4 1.5 %collective-permute-start.11 = (f32[2,3,8,128]{3,2,1,0:T(8,128)S(1)}, f32[2,3,8,128]{3,2,1,0:T(8,128)S(1)}, u32[]{:S(2)}, u32[]{:S(2)}) collective-permute-start(f32[2,3,8,128]{3,2,1,0:T(8,128)S(1)} %get-tuple-element.107), channel_id=1, source_target_pairs={{1,0},{2,1},{3,2},{0,3},{5,4},{6,5},{7,6},{4,7},{9,8},{10,9},{11,1... | collective-permute-start | bytes 73736 | tf_op jit(solution)/shard_map/ppermute | solution.py:833
  50.9 5.1 %conv_back.1.prior_hbm = bf16[32,4,128,128]{3,2,1,0:T(8,128)(2,1)} custom-call(bf16[8,4,128,128]{3,2,1,0:T(8,128)(2,1)S(1)} %get-tuple-element.109.refs_0_, bf16[8,4,128,128]{3,2,1,0:T(8,128)(2,1)S(1)} %get-tuple-element.110.refs_1_, bf16[8,4,128,128]{3,2,1,0:T(8,128)(2,1)S(1)} %get-tuple-element.111.refs_2_, ...), custom_call_target="tpu_custom_call" | custom-call | flops 33554432 | bytes 9437184 | tf_op jit(solution)/shard_map/conv_back/pallas_call | solution.py:736
  56.0 1.8 %conv_last.1 = bf16[32,4,128,128]{3,2,1,0:T(8,128)(2,1)} custom-call(s32[4]{0:T(128)S(1)} %pad_add_fusion.place_ref.own_ref, bf16[8,4,128,128]{3,2,1,0:T(8,128)(2,1)S(1)} %get-tuple-element.101.refs_6_.slope_ref, bf16[8,4,128,128]{3,2,1,0:T(8,128)(2,1)S(1)} %get-tuple-element.102.refs_7_.normed_ref, ...), custom_call_target="tpu_custom_call", output_to_operand_aliasing={{}: (7, {})} | custom-call | tf_op jit(solution)/shard_map/conv_last/pallas_call | solution.py:752
  (38 shorter events, 1.2 us)
Async XLA Ops:
  2.7 6.1 %collective-permute-start = (f32[2,3,8,128]{3,2,1,0:T(8,128)S(1)}, f32[2,3,8,128]{3,2,1,0:T(8,128)S(1)}, u32[]{:S(2)}, u32[]{:S(2)}) collective-permute-start(f32[2,3,8,128]{3,2,1,0:T(8,128)S(1)} %get-tuple-element.67), channel_id=1, source_target_pairs={{0,1},{1,2},{2,3},{3,0},{4,5},{5,6},{6,7},{7,4},{8,9},{9,10},{10,1... | collective-permute-start | bytes 73736 | tf_op jit(solution)/shard_map/ppermute | solution.py:804
  8.7 7.2 %copy-start.11 = (f32[3]{0:T(128)S(1)}, f32[3]{0:T(128)}, u32[]{:S(2)}) copy-start(f32[3]{0:T(128)} %bias_ref.1) | copy-start | bytes 40
  9.4 6.5 %collective-permute-start.1 = (bf16[3,32,128]{2,1,0:T(8,128)(2,1)S(1)}, bf16[3,32,128]{2,1,0:T(8,128)(2,1)S(1)}, u32[]{:S(2)}, u32[]{:S(2)}) collective-permute-start(bf16[3,32,128]{2,1,0:T(8,128)(2,1)S(1)} %get-tuple-element.68), channel_id=1, source_target_pairs={{0,4},{4,0},{8,12},{12,8},{16,20},{20,16},{24,28},{28,24},{32,36},... | collective-permute-start | bytes 73736 | tf_op jit(solution)/shard_map/ppermute | solution.py:357
  10.4 13.8 %copy-start = (bf16[768,1280]{1,0:T(8,128)(2,1)S(1)}, bf16[768,1280]{1,0:T(8,128)(2,1)}, u32[]{:S(2)}) copy-start(bf16[768,1280]{1,0:T(8,128)(2,1)} %patch_hbm.1) | copy-start | bytes 5898244
  10.4 13.8 %copy-start.1 = (bf16[768,768]{1,0:T(8,128)(2,1)S(1)}, bf16[768,768]{1,0:T(8,128)(2,1)}, u32[]{:S(2)}) copy-start(bf16[768,768]{1,0:T(8,128)(2,1)} %constant.27.clone.order_hbm) | copy-start | bytes 3538948
  10.4 13.8 %copy-start.2 = (bf16[1280,272]{0,1:T(8,128)(2,1)S(1)}, bf16[1280,272]{0,1:T(8,128)(2,1)}, u32[]{:S(2)}) copy-start(bf16[1280,272]{0,1:T(8,128)(2,1)} %param.34) | copy-start | bytes 2088964
  10.4 13.8 %copy-start.3 = (bf16[64,1280]{1,0:T(8,128)(2,1)S(1)}, bf16[64,1280]{1,0:T(8,128)(2,1)}, u32[]{:S(2)}) copy-start(bf16[64,1280]{1,0:T(8,128)(2,1)} %position_hbm.1) | copy-start | bytes 491524
  10.4 13.8 %copy-start.4 = (bf16[17,272]{1,0:T(8,128)(2,1)S(1)}, bf16[17,272]{1,0:T(8,128)(2,1)}, u32[]{:S(2)}) copy-start(bf16[17,272]{1,0:T(8,128)(2,1)} %constant.26.clone.key_spread_ref) | copy-start | bytes 27748
  10.4 13.8 %copy-start.5 = (s32[32,17]{0,1:T(8,128)S(1)}, s32[32,17]{0,1:T(8,128)}, u32[]{:S(2)}) copy-start(s32[32,17]{0,1:T(8,128)} %param.26) | copy-start | bytes 6532
  10.4 13.8 %copy-start.6 = (s32[32,17]{0,1:T(8,128)S(1)}, s32[32,17]{0,1:T(8,128)}, u32[]{:S(2)}) copy-start(s32[32,17]{0,1:T(8,128)} %param.27) | copy-start | bytes 6532
  10.5 13.8 %copy-start.7 = (s32[32,17]{0,1:T(8,128)S(1)}, s32[32,17]{0,1:T(8,128)}, u32[]{:S(2)}) copy-start(s32[32,17]{0,1:T(8,128)} %param.28) | copy-start | bytes 6532
  10.5 13.8 %copy-start.8 = (f32[1280]{0:T(1024)S(1)}, f32[1280]{0:T(1024)}, u32[]{:S(2)}) copy-start(f32[1280]{0:T(1024)} %param.31) | copy-start | bytes 15364
  10.5 13.8 %copy-start.9 = (s32[1,32,3]{1,0,2:T(1,128)S(1)}, s32[1,32,3]{1,0,2:T(1,128)}, u32[]{:S(2)}) copy-start(s32[1,32,3]{1,0,2:T(1,128)} %param.24) | copy-start | bytes 1156
  10.5 13.8 %copy-start.10 = (s32[1,32]{1,0:T(1,128)S(1)}, s32[1,32]{1,0:T(1,128)}, u32[]{:S(2)}) copy-start(s32[1,32]{1,0:T(1,128)} %counts_ref.1) | copy-start | bytes 388
  10.5 5.4 %collective-permute-start.2 = (bf16[3,32,128]{2,1,0:T(8,128)(2,1)S(1)}, bf16[3,32,128]{2,1,0:T(8,128)(2,1)S(1)}, u32[]{:S(2)}, u32[]{:S(2)}) collective-permute-start(bf16[3,32,128]{2,1,0:T(8,128)(2,1)S(1)} %get-tuple-element.69), channel_id=1, source_target_pairs={{0,0},{4,8},{8,4},{12,16},{16,12},{20,24},{24,20},{28,32},{32,28},... | collective-permute-start | bytes 73736 | tf_op jit(solution)/shard_map/ppermute | solution.py:357
  16.7 5.8 %collective-permute-start.3 = (bf16[8,16,128]{2,1,0:T(8,128)(2,1)S(1)}, bf16[8,16,128]{2,1,0:T(8,128)(2,1)S(1)}, u32[]{:S(2)}, u32[]{:S(2)}) collective-permute-start(bf16[8,16,128]{2,1,0:T(8,128)(2,1)S(1)} %get-tuple-element.75), channel_id=1, source_target_pairs={{0,4},{4,8},{8,12},{12,0},{16,20},{20,24},{24,28},{28,16},{32,36},... | collective-permute-start | bytes 98312 | tf_op jit(solution)/shard_map/ppermute | solution.py:349
  18.3 4.6 %collective-permute-start.4 = (bf16[8,16,128]{2,1,0:T(8,128)(2,1)S(1)}, bf16[8,16,128]{2,1,0:T(8,128)(2,1)S(1)}, u32[]{:S(2)}, u32[]{:S(2)}) collective-permute-start(bf16[8,16,128]{2,1,0:T(8,128)(2,1)S(1)} %get-tuple-element.76), channel_id=1, source_target_pairs={{0,8},{4,12},{8,0},{12,4},{16,24},{20,28},{24,16},{28,20},{32,40},... | collective-permute-start | bytes 98312 | tf_op jit(solution)/shard_map/ppermute | solution.py:349
  20.9 3.3 %collective-permute-start.5 = (bf16[8,16,128]{2,1,0:T(8,128)(2,1)S(1)}, bf16[8,16,128]{2,1,0:T(8,128)(2,1)S(1)}, u32[]{:S(2)}, u32[]{:S(2)}) collective-permute-start(bf16[8,16,128]{2,1,0:T(8,128)(2,1)S(1)} %get-tuple-element.77), channel_id=1, source_target_pairs={{0,12},{4,0},{8,4},{12,8},{16,28},{20,16},{24,20},{28,24},{32,44},... | collective-permute-start | bytes 98312 | tf_op jit(solution)/shard_map/ppermute | solution.py:349
  36.1 2.6 %collective-permute-start.6 = (bf16[8,16,128]{2,1,0:T(8,128)(2,1)S(1)}, bf16[8,16,128]{2,1,0:T(8,128)(2,1)S(1)}, u32[]{:S(2)}, u32[]{:S(2)}) collective-permute-start(bf16[8,16,128]{2,1,0:T(8,128)(2,1)S(1)} %get-tuple-element.88), channel_id=1, source_target_pairs={{0,4},{4,8},{8,12},{12,0},{16,20},{20,24},{24,28},{28,16},{32,36},... | collective-permute-start | bytes 98312 | tf_op jit(solution)/shard_map/ppermute | solution.py:349
  36.3 2.8 %collective-permute-start.7 = (bf16[8,16,128]{2,1,0:T(8,128)(2,1)S(1)}, bf16[8,16,128]{2,1,0:T(8,128)(2,1)S(1)}, u32[]{:S(2)}, u32[]{:S(2)}) collective-permute-start(bf16[8,16,128]{2,1,0:T(8,128)(2,1)S(1)} %get-tuple-element.89), channel_id=1, source_target_pairs={{0,8},{4,12},{8,0},{12,4},{16,24},{20,28},{24,16},{28,20},{32,40},... | collective-permute-start | bytes 98312 | tf_op jit(solution)/shard_map/ppermute | solution.py:349
  36.9 3.4 %collective-permute-start.8 = (bf16[8,16,128]{2,1,0:T(8,128)(2,1)S(1)}, bf16[8,16,128]{2,1,0:T(8,128)(2,1)S(1)}, u32[]{:S(2)}, u32[]{:S(2)}) collective-permute-start(bf16[8,16,128]{2,1,0:T(8,128)(2,1)S(1)} %get-tuple-element.90), channel_id=1, source_target_pairs={{0,12},{4,0},{8,4},{12,8},{16,28},{20,16},{24,20},{28,24},{32,44},... | collective-permute-start | bytes 98312 | tf_op jit(solution)/shard_map/ppermute | solution.py:349
  41.0 7.7 %collective-permute-start.10 = (bf16[3,32,128]{2,1,0:T(8,128)(2,1)S(1)}, bf16[3,32,128]{2,1,0:T(8,128)(2,1)S(1)}, u32[]{:S(2)}, u32[]{:S(2)}) collective-permute-start(bf16[3,32,128]{2,1,0:T(8,128)(2,1)S(1)} %get-tuple-element.98), channel_id=1, source_target_pairs={{0,0},{4,8},{8,4},{12,16},{16,12},{20,24},{24,20},{28,32},{32,28},... | collective-permute-start | bytes 73736 | tf_op jit(solution)/shard_map/ppermute | solution.py:357
  43.3 5.4 %collective-permute-start.9 = (bf16[3,32,128]{2,1,0:T(8,128)(2,1)S(1)}, bf16[3,32,128]{2,1,0:T(8,128)(2,1)S(1)}, u32[]{:S(2)}, u32[]{:S(2)}) collective-permute-start(bf16[3,32,128]{2,1,0:T(8,128)(2,1)S(1)} %get-tuple-element.97), channel_id=1, source_target_pairs={{0,4},{4,0},{8,12},{12,8},{16,20},{20,16},{24,28},{28,24},{32,36},... | collective-permute-start | bytes 73736 | tf_op jit(solution)/shard_map/ppermute | solution.py:357
  49.4 6.6 %collective-permute-start.11 = (f32[2,3,8,128]{3,2,1,0:T(8,128)S(1)}, f32[2,3,8,128]{3,2,1,0:T(8,128)S(1)}, u32[]{:S(2)}, u32[]{:S(2)}) collective-permute-start(f32[2,3,8,128]{3,2,1,0:T(8,128)S(1)} %get-tuple-element.107), channel_id=1, source_target_pairs={{1,0},{2,1},{3,2},{0,3},{5,4},{6,5},{7,6},{4,7},{9,8},{10,9},{11,1... | collective-permute-start | bytes 73736 | tf_op jit(solution)/shard_map/ppermute | solution.py:833

commit v6 on v5

--- a/solution.py
+++ b/solution.py
@@ -18,7 +18,7 @@
 COLS = 128
 ROWS = 4
 GROUP = 4
-FORWARD_FRAMES = 8
+FORWARD_FRAMES = 16
 BACK_FRAMES = 8
 BACK_ROWS = 4
 NORM_EPS = 1e-06
@@ -68,6 +68,7 @@
 SELECTOR = make_selector().astype(ml_dtypes.bfloat16)
 SELECTOR_T = np.ascontiguousarray(make_selector().T).astype(ml_dtypes.bfloat16)
 PIXEL_ORDER = make_pixel_order().astype(ml_dtypes.bfloat16)
+PIXEL_ORDER_T = np.ascontiguousarray(make_pixel_order().T).astype(ml_dtypes.bfloat16)
 KEY_SPREAD = make_key_spread().astype(ml_dtypes.bfloat16)
 MEAN_PAIR = (np.kron(np.eye(2), np.ones((CH, CH))) / CH).astype(ml_dtypes.bfloat16)
 
@@ -414,29 +415,21 @@
     gain_ref,
     up,
     down,
-    order_hbm,
-    patch_hbm,
-    head_hbm,
-    position_hbm,
+    order,
+    patch,
+    head,
+    position,
+    order_t,
     out0_ref,
     out1_ref,
     out2_ref,
     out3_ref,
-    order,
-    patch,
-    head,
-    position,
     strips,
     key_table,
     hidden_pre,
     hidden,
     pre_grad,
-    sems,
 ):
-    pairs = [(order_hbm, order), (patch_hbm, patch), (position_hbm, position), (head_hbm, head)]
-    copies = [pltpu.make_async_copy(src, dst, sems.at[i]) for i, (src, dst) in enumerate(pairs)]
-    for copy in copies:
-        copy.start()
     token_row = own_ref[0] // GROUP
     me = lax.rem(own_ref[0], GROUP)
     first_frame = pl.multiple_of(me * 8, 8)
@@ -466,10 +459,7 @@
     mask = by_token(own_keys(key_vis_ref) * weight)
 
     raw = gather_patches(me, (x0_ref, x1_ref, x2_ref, x3_ref), strips)
-    copies[0].wait()
     patches = dot(raw, order[...]).astype(BF16)
-    copies[1].wait()
-    copies[2].wait()
     pair_rows = pl.ds(pl.multiple_of(token_row // 2 * 16, 16), 16)
     two = position[pair_rows, :].astype(F32)
     places = jnp.where(lax.rem(token_row, 2) == 0, two[:8], two[8:])
@@ -489,7 +479,6 @@
 
     block = dot(hidden[...], down[...])
     block_round = (embedded + block).astype(BF16)
-    copies[3].wait()
     heatmap = dot_nt(block_round, head[...])
     heat_grad = ((heatmap - target) * mask).astype(BF16)
     out_grad = dot(heat_grad, head[...])
@@ -511,26 +500,21 @@
     )
     colour_grad = dot_nt(embed_grad.astype(BF16), patch[...]).astype(BF16)
     outs = (out0_ref, out1_ref, out2_ref, out3_ref)
-    scatter_patches(me, dot_nt(colour_grad, order[...]), strips, outs)
+    scatter_patches(me, dot(colour_grad, order_t[...]), strips, outs)
 
 
 def pose(own, parts, frames, counts, key_rows, key_cols, key_vis, gain, up, down, patch, head, position):
     return pl.pallas_call(
         pose_kernel,
-        in_specs=[SMEM] + [VMEM] * 13 + [ANYWHERE] * 4,
+        in_specs=[SMEM] + [VMEM] * 18,
         out_specs=[VMEM] * GROUP,
         out_shape=[jax.ShapeDtypeStruct((8, 16, COLS), BF16)] * GROUP,
         scratch_shapes=[
-            pltpu.VMEM((768, 768), BF16),
-            pltpu.VMEM((768, DP), BF16),
-            pltpu.VMEM((HEAD, DP), BF16),
-            pltpu.VMEM((64, DP), BF16),
             pltpu.VMEM((GROUP, 8, 16, COLS), F32),
             pltpu.VMEM((32, HEAD), F32),
             pltpu.VMEM((64, HID), F32),
             pltpu.VMEM((64, HID), BF16),
             pltpu.VMEM((64, HID), BF16),
-            pltpu.SemaphoreType.DMA((4,)),
         ],
         compiler_params=megabytes(20),
         cost_estimate=pl.CostEstimate(
@@ -553,6 +537,7 @@
         patch,
         head,
         position,
+        jnp.asarray(PIXEL_ORDER_T),
     )
 
 
@@ -633,8 +618,7 @@
     mean_pair = mean_ref[...]
     places = [(tau, r) for tau in range(2) for r in range(ROWS)]
 
-    @pl.loop(0, slope_ref.shape[0] // 2)
-    def _(pair):
+    for pair in range(slope_ref.shape[0] // 2):
         xs = [feat_ref[start + 2 * pair + tau, r].astype(F32) for tau, r in places]
         means = channel_means([x * x for x in xs], mean_pair)
         for x, mean, (tau, r) in zip(xs, means, places):

time: 58.1 us -> 56.1 us (0.966)
  Pallas kernels: 35.4 us -> 31.9 us
  waiting for transfers between devices: 3.28 us -> 4.52 us
    pallas_call x1, Pallas kernels: 11.8 us -> 10 us  [pose(): pl.pallas_call(pose_kernel, in_specs=[SMEM] + [VMEM] * 18, out_specs=[VME...]
    pallas_call x4, Pallas kernels: 6.61 us -> 4.92 us  [prepare(): pl.pallas_call(functools.partial(prepare_kernel, start), in_specs=[VMEM]...]
    ppermute x6, waiting for transfers between devices: 3.26 us -> 4.1 us  [swap_turns(): out.append(lax.ppermute(parts[turn], 'tile', pairs))]
  transfers between devices with their start and end apart: 12 -> 12, of which waited for: 4 -> 5; matrix products, arithmetic and copies ran while one was open for 0% -> 0% of each run, Pallas kernels for 28% -> 26%
where the time goes in v6:
time: 56.1 us; the launch traced here: 56 us
  Pallas kernels  31.9 us (57%)
  starting transfers between devices  18.9 us (34%)
  waiting for transfers between devices  4.52 us (8%)
    pallas_call x1, Pallas kernels, pose(): pl.pallas_call(pose_kernel, in_specs=[SMEM] + [VMEM] * 18, out_specs=[VME...  10 us
    ppermute x2, starting transfers between devices, swap_rims(): lax.ppermute(across, 'tile', others)  5.97 us
    pallas_call x1, Pallas kernels, conv_backward(): pl.pallas_call(back_kernel, in_specs=[VMEM] * (len(kept) * 2 + 3), out_sp...  5.1 us
    ppermute x2, starting transfers between devices, swap_rims(): lax.ppermute(inside, 'tile', pairs)  4.99 us
    pallas_call x4, Pallas kernels, prepare(): pl.pallas_call(functools.partial(prepare_kernel, start), in_specs=[VMEM]...  4.92 us
    ppermute x6, starting transfers between devices, swap_turns(): out.append(lax.ppermute(parts[turn], 'tile', pairs))  4.91 us
    pallas_call x1, Pallas kernels, conv_main(): pl.pallas_call(conv_kernel, in_specs=[VMEM] * 4 + [ANYWHERE] * 2, out_spe...  4.76 us
    ppermute x6, waiting for transfers between devices, swap_turns(): out.append(lax.ppermute(parts[turn], 'tile', pairs))  4.1 us
  transfers between devices with their start and end apart: 12, of which 5 were waited for; matrix products, arithmetic and copies ran while one was open for 0% of the time, Pallas kernels for 26%

profile of v6, /device:TPU:25, one launch (start us, length us, event | category | flops | bytes accessed | tf_op | source)
XLA Modules:
  0.0 56.0 jit_solution(11357164758007656263)
XLA Ops:
  0.1 2.6 %conv_tail.1 = (f32[2,3,8,128]{3,2,1,0:T(8,128)S(1)}, bf16[32,4,128,128]{3,2,1,0:T(8,128)(2,1)S(1)}, bf16[1024,256]{1,0:T(8,128)(2,1)S(1)}, bf16[256,1024]{1,0:T...) custom-call(bf16[32,4,128,128]{3,2,1,0:T(8,128)(2,1)} %feat_hbm, f32[1,128]{1,0:T(1,128)} %bitcast.17, ...), custom_call_target="tpu_custom_call" | custom-call | tf_op jit(solution)/shard_map/conv_tail/pallas_call | solution.py:227
  2.7 1.3 %collective-permute-start = (f32[2,3,8,128]{3,2,1,0:T(8,128)S(1)}, f32[2,3,8,128]{3,2,1,0:T(8,128)S(1)}, u32[]{:S(2)}, u32[]{:S(2)}) collective-permute-start(f32[2,3,8,128]{3,2,1,0:T(8,128)S(1)} %get-tuple-element.67), channel_id=1, source_target_pairs={{0,1},{1,2},{2,3},{3,0},{4,5},{5,6},{6,7},{7,4},{8,9},{9,10},{10,1... | collective-permute-start | bytes 73736 | tf_op jit(solution)/shard_map/ppermute | solution.py:788
  4.0 4.8 %conv_main.1 = (f32[32,3,8,128]{3,2,1,0:T(8,128)S(1)}, bf16[1280,2560]{1,0:T(8,128)(2,1)S(1)}, bf16[2560,1280]{1,0:T(8,128)(2,1)S(1)}) custom-call(bf16[32,4,128,128]{3,2,1,0:T(8,128)(2,1)S(1)} %get-tuple-element.62.feat_ref, f32[1,128]{1,0:T(1,128)S(1)} %get-tuple-element.63.gain_ref, bf16[256,256]{1,0:T(8,128)(2,1)S(1)} %get-tuple-element.64.mean_ref.refs_9_, ...), custom_call_target="tpu_custom_call" | custom-call | flops 33554432 | bytes 20971520 | tf_op jit(solution)/shard_map/conv_main/pallas_call | solution.py:253
  9.4 1.0 %collective-permute-start.1 = (bf16[3,32,128]{2,1,0:T(8,128)(2,1)S(1)}, bf16[3,32,128]{2,1,0:T(8,128)(2,1)S(1)}, u32[]{:S(2)}, u32[]{:S(2)}) collective-permute-start(bf16[3,32,128]{2,1,0:T(8,128)(2,1)S(1)} %get-tuple-element.68), channel_id=1, source_target_pairs={{0,4},{4,0},{8,12},{12,8},{16,20},{20,16},{24,28},{28,24},{32,36},... | collective-permute-start | bytes 73736 | tf_op jit(solution)/shard_map/ppermute | solution.py:358
  10.5 3.7 %collective-permute-start.2 = (bf16[3,32,128]{2,1,0:T(8,128)(2,1)S(1)}, bf16[3,32,128]{2,1,0:T(8,128)(2,1)S(1)}, u32[]{:S(2)}, u32[]{:S(2)}) collective-permute-start(bf16[3,32,128]{2,1,0:T(8,128)(2,1)S(1)} %get-tuple-element.69), channel_id=1, source_target_pairs={{0,0},{4,8},{8,4},{12,16},{16,12},{20,24},{24,20},{28,32},{32,28},... | collective-permute-start | bytes 73736 | tf_op jit(solution)/shard_map/ppermute | solution.py:358
  14.3 1.2 %prepare_0.1 = (bf16[8,4,128,128]{3,2,1,0:T(8,128)(2,1)S(1)}, bf16[8,4,128,128]{3,2,1,0:T(8,128)(2,1)S(1)}) custom-call(bf16[32,4,128,128]{3,2,1,0:T(8,128)(2,1)S(1)} %get-tuple-element.62.feat_ref, f32[1,128]{1,0:T(1,128)S(1)} %get-tuple-element.63.gain_ref, bf16[256,256]{1,0:T(8,128)(2,1)S(1)} %get-tuple-element.64.mean_ref.refs_9_), custom_call_target="tpu_custom_call" | custom-call | flops 1000000000 | bytes 800000 | tf_op jit(solution)/shard_map/prepare_0/pallas_call | solution.py:636
  15.9 0.7 %colours.1 = (bf16[8,16,128]{2,1,0:T(8,128)(2,1)S(1)}, bf16[8,16,128]{2,1,0:T(8,128)(2,1)S(1)}, bf16[8,16,128]{2,1,0:T(8,128)(2,1)S(1)}, bf16[8,16,128]{2,1,0:T(8,128)(2,1)S(1)}) custom-call(s32[4]{0:T(128)S(1)} %pad_add_fusion.place_ref.own_ref, f32[3]{0:T(128)S(1)} %copy-done.12, f32[32,3,8,128]{3,2,1,0:T(8,128)S(1)} %get-tuple-element.66.sums_ref, ...), custom_call_target="tpu_custom_call" | custom-call | tf_op jit(solution)/shard_map/colours/pallas_call | solution.py:333
  16.7 1.6 %collective-permute-start.3 = (bf16[8,16,128]{2,1,0:T(8,128)(2,1)S(1)}, bf16[8,16,128]{2,1,0:T(8,128)(2,1)S(1)}, u32[]{:S(2)}, u32[]{:S(2)}) collective-permute-start(bf16[8,16,128]{2,1,0:T(8,128)(2,1)S(1)} %get-tuple-element.75), channel_id=1, source_target_pairs={{0,4},{4,8},{8,12},{12,0},{16,20},{20,24},{24,28},{28,16},{32,36},... | collective-permute-start | bytes 98312 | tf_op jit(solution)/shard_map/ppermute | solution.py:350
  18.3 2.4 %collective-permute-start.4 = (bf16[8,16,128]{2,1,0:T(8,128)(2,1)S(1)}, bf16[8,16,128]{2,1,0:T(8,128)(2,1)S(1)}, u32[]{:S(2)}, u32[]{:S(2)}) collective-permute-start(bf16[8,16,128]{2,1,0:T(8,128)(2,1)S(1)} %get-tuple-element.76), channel_id=1, source_target_pairs={{0,8},{4,12},{8,0},{12,4},{16,24},{20,28},{24,16},{28,20},{32,40},... | collective-permute-start | bytes 98312 | tf_op jit(solution)/shard_map/ppermute | solution.py:350
  20.7 1.2 %prepare_8.1 = (bf16[8,4,128,128]{3,2,1,0:T(8,128)(2,1)S(1)}, bf16[8,4,128,128]{3,2,1,0:T(8,128)(2,1)S(1)}) custom-call(bf16[32,4,128,128]{3,2,1,0:T(8,128)(2,1)S(1)} %get-tuple-element.62.feat_ref, f32[1,128]{1,0:T(1,128)S(1)} %get-tuple-element.63.gain_ref, bf16[256,256]{1,0:T(8,128)(2,1)S(1)} %get-tuple-element.64.mean_ref.refs_9_), custom_call_target="tpu_custom_call" | custom-call | flops 1000000000 | bytes 800000 | tf_op jit(solution)/shard_map/prepare_8/pallas_call | solution.py:636
  22.0 0.8 %collective-permute-done.4.x2_ref = bf16[8,16,128]{2,1,0:T(8,128)(2,1)S(1)} collective-permute-done((bf16[8,16,128]{2,1,0:T(8,128)(2,1)S(1)}, bf16[8,16,128]{2,1,0:T(8,128)(2,1)S(1)}, u32[]{:S(2)}, u32[]{:S(2)}) %collective-permute-start.4) | collective-permute-done | bytes 32800 | tf_op jit(solution)/shard_map/ppermute | solution.py:350
  22.7 1.3 %collective-permute-done.5.x3_ref = bf16[8,16,128]{2,1,0:T(8,128)(2,1)S(1)} collective-permute-done((bf16[8,16,128]{2,1,0:T(8,128)(2,1)S(1)}, bf16[8,16,128]{2,1,0:T(8,128)(2,1)S(1)}, u32[]{:S(2)}, u32[]{:S(2)}) %collective-permute-start.5) | collective-permute-done | bytes 32800 | tf_op jit(solution)/shard_map/ppermute | solution.py:350
  24.1 10.0 %pose.1 = (bf16[8,16,128]{2,1,0:T(8,128)(2,1)S(1)}, bf16[8,16,128]{2,1,0:T(8,128)(2,1)S(1)}, bf16[8,16,128]{2,1,0:T(8,128)(2,1)S(1)}, bf16[8,16,128]{2,1,0:T(8,128)(2,1)S(1)}) custom-call(s32[4]{0:T(128)S(1)} %pad_add_fusion.place_ref.own_ref, bf16[8,16,128]{2,1,0:T(8,128)(2,1)S(1)} %get-tuple-element.80.x0_ref, ...), custom_call_target="tpu_custom_call" | custom-call | flops 2022400000 | bytes 17825792 | tf_op jit(solution)/shard_map/pose/pallas_call | solution.py:507
  34.2 0.7 %collective-permute-start.7 = (bf16[8,16,128]{2,1,0:T(8,128)(2,1)S(1)}, bf16[8,16,128]{2,1,0:T(8,128)(2,1)S(1)}, u32[]{:S(2)}, u32[]{:S(2)}) collective-permute-start(bf16[8,16,128]{2,1,0:T(8,128)(2,1)S(1)} %get-tuple-element.89), channel_id=1, source_target_pairs={{0,8},{4,12},{8,0},{12,4},{16,24},{20,28},{24,16},{28,20},{32,40},... | collective-permute-start | bytes 98312 | tf_op jit(solution)/shard_map/ppermute | solution.py:350
  35.0 1.2 %prepare_16.1 = (bf16[8,4,128,128]{3,2,1,0:T(8,128)(2,1)S(1)}, bf16[8,4,128,128]{3,2,1,0:T(8,128)(2,1)S(1)}) custom-call(bf16[32,4,128,128]{3,2,1,0:T(8,128)(2,1)S(1)} %get-tuple-element.62.feat_ref, f32[1,128]{1,0:T(1,128)S(1)} %get-tuple-element.63.gain_ref, bf16[256,256]{1,0:T(8,128)(2,1)S(1)} %get-tuple-element.64.mean_ref.refs_9_), custom_call_target="tpu_custom_call" | custom-call | flops 1000000000 | bytes 800000 | tf_op jit(solution)/shard_map/prepare_16/pallas_call | solution.py:636
  36.3 0.8 %collective-permute-done.7.x2_ref = bf16[8,16,128]{2,1,0:T(8,128)(2,1)S(1)} collective-permute-done((bf16[8,16,128]{2,1,0:T(8,128)(2,1)S(1)}, bf16[8,16,128]{2,1,0:T(8,128)(2,1)S(1)}, u32[]{:S(2)}, u32[]{:S(2)}) %collective-permute-start.7) | collective-permute-done | bytes 32800 | tf_op jit(solution)/shard_map/ppermute | solution.py:350
  37.1 1.2 %collective-permute-done.8.x3_ref = bf16[8,16,128]{2,1,0:T(8,128)(2,1)S(1)} collective-permute-done((bf16[8,16,128]{2,1,0:T(8,128)(2,1)S(1)}, bf16[8,16,128]{2,1,0:T(8,128)(2,1)S(1)}, u32[]{:S(2)}, u32[]{:S(2)}) %collective-permute-start.8) | collective-permute-done | bytes 32800 | tf_op jit(solution)/shard_map/ppermute | solution.py:350
  38.3 0.7 %strip_grads.1 = (f32[32,3,8,128]{3,2,1,0:T(8,128)S(1)}, bf16[3,32,128]{2,1,0:T(8,128)(2,1)S(1)}, bf16[3,32,128]{2,1,0:T(8,128)(2,1)S(1)}) custom-call(s32[4]{0:T(128)S(1)} %pad_add_fusion.place_ref.own_ref, bf16[8,16,128]{2,1,0:T(8,128)(2,1)S(1)} %get-tuple-element.93.x0_ref, bf16[8,16,128]{2,1,0:T(8,128)(2,1)S(1)} %collective-permute-done.6.x1_ref, ...), custom_call_target="tpu_custom_call" | custom-call | tf_op jit(solution)/shard_map/strip_grads/pallas_call | solution.py:562
  39.0 2.2 %collective-permute-start.10 = (bf16[3,32,128]{2,1,0:T(8,128)(2,1)S(1)}, bf16[3,32,128]{2,1,0:T(8,128)(2,1)S(1)}, u32[]{:S(2)}, u32[]{:S(2)}) collective-permute-start(bf16[3,32,128]{2,1,0:T(8,128)(2,1)S(1)} %get-tuple-element.98), channel_id=1, source_target_pairs={{0,0},{4,8},{8,4},{12,16},{16,12},{20,24},{24,20},{28,32},{32,28},... | collective-permute-start | bytes 73736 | tf_op jit(solution)/shard_map/ppermute | solution.py:358
  41.3 4.0 %collective-permute-start.9 = (bf16[3,32,128]{2,1,0:T(8,128)(2,1)S(1)}, bf16[3,32,128]{2,1,0:T(8,128)(2,1)S(1)}, u32[]{:S(2)}, u32[]{:S(2)}) collective-permute-start(bf16[3,32,128]{2,1,0:T(8,128)(2,1)S(1)} %get-tuple-element.97), channel_id=1, source_target_pairs={{0,4},{4,0},{8,12},{12,8},{16,20},{20,16},{24,28},{28,24},{32,36},... | collective-permute-start | bytes 73736 | tf_op jit(solution)/shard_map/ppermute | solution.py:358
  45.2 1.2 %prepare_24.1 = (bf16[8,4,128,128]{3,2,1,0:T(8,128)(2,1)S(1)}, bf16[8,4,128,128]{3,2,1,0:T(8,128)(2,1)S(1)}) custom-call(bf16[32,4,128,128]{3,2,1,0:T(8,128)(2,1)S(1)} %get-tuple-element.62.feat_ref, f32[1,128]{1,0:T(1,128)S(1)} %get-tuple-element.63.gain_ref, bf16[256,256]{1,0:T(8,128)(2,1)S(1)} %get-tuple-element.64.mean_ref.refs_9_), custom_call_target="tpu_custom_call" | custom-call | flops 1000000000 | bytes 800000 | tf_op jit(solution)/shard_map/prepare_24/pallas_call | solution.py:636
  47.2 1.8 %collective-permute-start.11 = (f32[2,3,8,128]{3,2,1,0:T(8,128)S(1)}, f32[2,3,8,128]{3,2,1,0:T(8,128)S(1)}, u32[]{:S(2)}, u32[]{:S(2)}) collective-permute-start(f32[2,3,8,128]{3,2,1,0:T(8,128)S(1)} %get-tuple-element.107), channel_id=1, source_target_pairs={{1,0},{2,1},{3,2},{0,3},{5,4},{6,5},{7,6},{4,7},{9,8},{10,9},{11,1... | collective-permute-start | bytes 73736 | tf_op jit(solution)/shard_map/ppermute | solution.py:817
  48.9 5.1 %conv_back.1.prior_hbm = bf16[32,4,128,128]{3,2,1,0:T(8,128)(2,1)} custom-call(bf16[8,4,128,128]{3,2,1,0:T(8,128)(2,1)S(1)} %get-tuple-element.109.refs_0_, bf16[8,4,128,128]{3,2,1,0:T(8,128)(2,1)S(1)} %get-tuple-element.110.refs_1_, bf16[8,4,128,128]{3,2,1,0:T(8,128)(2,1)S(1)} %get-tuple-element.111.refs_2_, ...), custom_call_target="tpu_custom_call" | custom-call | flops 33554432 | bytes 9437184 | tf_op jit(solution)/shard_map/conv_back/pallas_call | solution.py:720
  54.0 1.8 %conv_last.1 = bf16[32,4,128,128]{3,2,1,0:T(8,128)(2,1)} custom-call(s32[4]{0:T(128)S(1)} %pad_add_fusion.place_ref.own_ref, bf16[8,4,128,128]{3,2,1,0:T(8,128)(2,1)S(1)} %get-tuple-element.101.refs_6_.slope_ref, bf16[8,4,128,128]{3,2,1,0:T(8,128)(2,1)S(1)} %get-tuple-element.102.refs_7_.normed_ref, ...), custom_call_target="tpu_custom_call", output_to_operand_aliasing={{}: (7, {})} | custom-call | tf_op jit(solution)/shard_map/conv_last/pallas_call | solution.py:736
  (40 shorter events, 2.0 us)
Async XLA Ops:
  2.7 6.1 %collective-permute-start = (f32[2,3,8,128]{3,2,1,0:T(8,128)S(1)}, f32[2,3,8,128]{3,2,1,0:T(8,128)S(1)}, u32[]{:S(2)}, u32[]{:S(2)}) collective-permute-start(f32[2,3,8,128]{3,2,1,0:T(8,128)S(1)} %get-tuple-element.67), channel_id=1, source_target_pairs={{0,1},{1,2},{2,3},{3,0},{4,5},{5,6},{6,7},{7,4},{8,9},{9,10},{10,1... | collective-permute-start | bytes 73736 | tf_op jit(solution)/shard_map/ppermute | solution.py:788
  9.4 6.1 %collective-permute-start.1 = (bf16[3,32,128]{2,1,0:T(8,128)(2,1)S(1)}, bf16[3,32,128]{2,1,0:T(8,128)(2,1)S(1)}, u32[]{:S(2)}, u32[]{:S(2)}) collective-permute-start(bf16[3,32,128]{2,1,0:T(8,128)(2,1)S(1)} %get-tuple-element.68), channel_id=1, source_target_pairs={{0,4},{4,0},{8,12},{12,8},{16,20},{20,16},{24,28},{28,24},{32,36},... | collective-permute-start | bytes 73736 | tf_op jit(solution)/shard_map/ppermute | solution.py:358
  10.4 13.6 %copy-start = (bf16[768,1280]{1,0:T(8,128)(2,1)S(1)}, bf16[768,1280]{1,0:T(8,128)(2,1)}, u32[]{:S(2)}) copy-start(bf16[768,1280]{1,0:T(8,128)(2,1)} %patch.1) | copy-start | bytes 5898244
  10.4 13.6 %copy-start.1 = (bf16[768,768]{1,0:T(8,128)(2,1)S(1)}, bf16[768,768]{1,0:T(8,128)(2,1)}, u32[]{:S(2)}) copy-start(bf16[768,768]{1,0:T(8,128)(2,1)} %constant.29.clone.order) | copy-start | bytes 3538948
  10.4 13.6 %copy-start.2 = (bf16[768,768]{1,0:T(8,128)(2,1)S(1)}, bf16[768,768]{1,0:T(8,128)(2,1)}, u32[]{:S(2)}) copy-start(bf16[768,768]{1,0:T(8,128)(2,1)} %constant.30.clone.order_t) | copy-start | bytes 3538948
  10.4 13.6 %copy-start.3 = (bf16[1280,272]{0,1:T(8,128)(2,1)S(1)}, bf16[1280,272]{0,1:T(8,128)(2,1)}, u32[]{:S(2)}) copy-start(bf16[1280,272]{0,1:T(8,128)(2,1)} %param.35) | copy-start | bytes 2088964
  10.4 13.6 %copy-start.4 = (bf16[64,1280]{1,0:T(8,128)(2,1)S(1)}, bf16[64,1280]{1,0:T(8,128)(2,1)}, u32[]{:S(2)}) copy-start(bf16[64,1280]{1,0:T(8,128)(2,1)} %position.1) | copy-start | bytes 491524
  10.4 13.6 %copy-start.5 = (bf16[17,272]{1,0:T(8,128)(2,1)S(1)}, bf16[17,272]{1,0:T(8,128)(2,1)}, u32[]{:S(2)}) copy-start(bf16[17,272]{1,0:T(8,128)(2,1)} %constant.28.clone.key_spread_ref) | copy-start | bytes 27748
  10.4 13.6 %copy-start.6 = (s32[32,17]{0,1:T(8,128)S(1)}, s32[32,17]{0,1:T(8,128)}, u32[]{:S(2)}) copy-start(s32[32,17]{0,1:T(8,128)} %param.27) | copy-start | bytes 6532
  10.5 13.6 %copy-start.7 = (s32[32,17]{0,1:T(8,128)S(1)}, s32[32,17]{0,1:T(8,128)}, u32[]{:S(2)}) copy-start(s32[32,17]{0,1:T(8,128)} %param.28) | copy-start | bytes 6532
  10.5 13.6 %copy-start.8 = (s32[32,17]{0,1:T(8,128)S(1)}, s32[32,17]{0,1:T(8,128)}, u32[]{:S(2)}) copy-start(s32[32,17]{0,1:T(8,128)} %param.29) | copy-start | bytes 6532
  10.5 13.6 %copy-start.9 = (f32[1280]{0:T(1024)S(1)}, f32[1280]{0:T(1024)}, u32[]{:S(2)}) copy-start(f32[1280]{0:T(1024)} %param.32) | copy-start | bytes 15364
  10.5 13.6 %copy-start.10 = (s32[1,32,3]{1,0,2:T(1,128)S(1)}, s32[1,32,3]{1,0,2:T(1,128)}, u32[]{:S(2)}) copy-start(s32[1,32,3]{1,0,2:T(1,128)} %param.25) | copy-start | bytes 1156
  10.5 13.6 %copy-start.11 = (s32[1,32]{1,0:T(1,128)S(1)}, s32[1,32]{1,0:T(1,128)}, u32[]{:S(2)}) copy-start(s32[1,32]{1,0:T(1,128)} %counts_ref.1) | copy-start | bytes 388
  10.5 5.4 %collective-permute-start.2 = (bf16[3,32,128]{2,1,0:T(8,128)(2,1)S(1)}, bf16[3,32,128]{2,1,0:T(8,128)(2,1)S(1)}, u32[]{:S(2)}, u32[]{:S(2)}) collective-permute-start(bf16[3,32,128]{2,1,0:T(8,128)(2,1)S(1)} %get-tuple-element.69), channel_id=1, source_target_pairs={{0,0},{4,8},{8,4},{12,16},{16,12},{20,24},{24,20},{28,32},{32,28},... | collective-permute-start | bytes 73736 | tf_op jit(solution)/shard_map/ppermute | solution.py:358
  16.7 5.3 %collective-permute-start.3 = (bf16[8,16,128]{2,1,0:T(8,128)(2,1)S(1)}, bf16[8,16,128]{2,1,0:T(8,128)(2,1)S(1)}, u32[]{:S(2)}, u32[]{:S(2)}) collective-permute-start(bf16[8,16,128]{2,1,0:T(8,128)(2,1)S(1)} %get-tuple-element.75), channel_id=1, source_target_pairs={{0,4},{4,8},{8,12},{12,0},{16,20},{20,24},{24,28},{28,16},{32,36},... | collective-permute-start | bytes 98312 | tf_op jit(solution)/shard_map/ppermute | solution.py:350
  18.3 4.4 %collective-permute-start.4 = (bf16[8,16,128]{2,1,0:T(8,128)(2,1)S(1)}, bf16[8,16,128]{2,1,0:T(8,128)(2,1)S(1)}, u32[]{:S(2)}, u32[]{:S(2)}) collective-permute-start(bf16[8,16,128]{2,1,0:T(8,128)(2,1)S(1)} %get-tuple-element.76), channel_id=1, source_target_pairs={{0,8},{4,12},{8,0},{12,4},{16,24},{20,28},{24,16},{28,20},{32,40},... | collective-permute-start | bytes 98312 | tf_op jit(solution)/shard_map/ppermute | solution.py:350
  20.7 3.3 %collective-permute-start.5 = (bf16[8,16,128]{2,1,0:T(8,128)(2,1)S(1)}, bf16[8,16,128]{2,1,0:T(8,128)(2,1)S(1)}, u32[]{:S(2)}, u32[]{:S(2)}) collective-permute-start(bf16[8,16,128]{2,1,0:T(8,128)(2,1)S(1)} %get-tuple-element.77), channel_id=1, source_target_pairs={{0,12},{4,0},{8,4},{12,8},{16,28},{20,16},{24,20},{28,24},{32,44},... | collective-permute-start | bytes 98312 | tf_op jit(solution)/shard_map/ppermute | solution.py:350
  34.1 2.1 %collective-permute-start.6 = (bf16[8,16,128]{2,1,0:T(8,128)(2,1)S(1)}, bf16[8,16,128]{2,1,0:T(8,128)(2,1)S(1)}, u32[]{:S(2)}, u32[]{:S(2)}) collective-permute-start(bf16[8,16,128]{2,1,0:T(8,128)(2,1)S(1)} %get-tuple-element.88), channel_id=1, source_target_pairs={{0,4},{4,8},{8,12},{12,0},{16,20},{20,24},{24,28},{28,16},{32,36},... | collective-permute-start | bytes 98312 | tf_op jit(solution)/shard_map/ppermute | solution.py:350
  34.2 2.8 %collective-permute-start.7 = (bf16[8,16,128]{2,1,0:T(8,128)(2,1)S(1)}, bf16[8,16,128]{2,1,0:T(8,128)(2,1)S(1)}, u32[]{:S(2)}, u32[]{:S(2)}) collective-permute-start(bf16[8,16,128]{2,1,0:T(8,128)(2,1)S(1)} %get-tuple-element.89), channel_id=1, source_target_pairs={{0,8},{4,12},{8,0},{12,4},{16,24},{20,28},{24,16},{28,20},{32,40},... | collective-permute-start | bytes 98312 | tf_op jit(solution)/shard_map/ppermute | solution.py:350
  34.9 3.4 %collective-permute-start.8 = (bf16[8,16,128]{2,1,0:T(8,128)(2,1)S(1)}, bf16[8,16,128]{2,1,0:T(8,128)(2,1)S(1)}, u32[]{:S(2)}, u32[]{:S(2)}) collective-permute-start(bf16[8,16,128]{2,1,0:T(8,128)(2,1)S(1)} %get-tuple-element.90), channel_id=1, source_target_pairs={{0,12},{4,0},{8,4},{12,8},{16,28},{20,16},{24,20},{28,24},{32,44},... | collective-permute-start | bytes 98312 | tf_op jit(solution)/shard_map/ppermute | solution.py:350
  39.0 7.4 %collective-permute-start.10 = (bf16[3,32,128]{2,1,0:T(8,128)(2,1)S(1)}, bf16[3,32,128]{2,1,0:T(8,128)(2,1)S(1)}, u32[]{:S(2)}, u32[]{:S(2)}) collective-permute-start(bf16[3,32,128]{2,1,0:T(8,128)(2,1)S(1)} %get-tuple-element.98), channel_id=1, source_target_pairs={{0,0},{4,8},{8,4},{12,16},{16,12},{20,24},{24,20},{28,32},{32,28},... | collective-permute-start | bytes 73736 | tf_op jit(solution)/shard_map/ppermute | solution.py:358
  41.3 5.2 %collective-permute-start.9 = (bf16[3,32,128]{2,1,0:T(8,128)(2,1)S(1)}, bf16[3,32,128]{2,1,0:T(8,128)(2,1)S(1)}, u32[]{:S(2)}, u32[]{:S(2)}) collective-permute-start(bf16[3,32,128]{2,1,0:T(8,128)(2,1)S(1)} %get-tuple-element.97), channel_id=1, source_target_pairs={{0,4},{4,0},{8,12},{12,8},{16,20},{20,16},{24,28},{28,24},{32,36},... | collective-permute-start | bytes 73736 | tf_op jit(solution)/shard_map/ppermute | solution.py:358
  47.2 6.9 %collective-permute-start.11 = (f32[2,3,8,128]{3,2,1,0:T(8,128)S(1)}, f32[2,3,8,128]{3,2,1,0:T(8,128)S(1)}, u32[]{:S(2)}, u32[]{:S(2)}) collective-permute-start(f32[2,3,8,128]{3,2,1,0:T(8,128)S(1)} %get-tuple-element.107), channel_id=1, source_target_pairs={{1,0},{2,1},{3,2},{0,3},{5,4},{6,5},{7,6},{4,7},{9,8},{10,9},{11,1... | collective-permute-start | bytes 73736 | tf_op jit(solution)/shard_map/ppermute | solution.py:817
  (1 other events, 7.2 us)

commit v7 on v6

--- a/solution.py
+++ b/solution.py
@@ -20,7 +20,7 @@
 GROUP = 4
 FORWARD_FRAMES = 16
 BACK_FRAMES = 8
-BACK_ROWS = 4
+BACK_ROWS = 8
 NORM_EPS = 1e-06
 F32 = jnp.float32
 BF16 = jnp.bfloat16

time: 56.1 us -> 56 us (level)
  no operation moved by 1% of the time
where the time goes in v7:
time: 56 us; the launch traced here: 55.8 us
  Pallas kernels  31.7 us (57%)
  starting transfers between devices  18.9 us (34%)
  waiting for transfers between devices  4.52 us (8%)
    pallas_call x1, Pallas kernels, pose(): pl.pallas_call(pose_kernel, in_specs=[SMEM] + [VMEM] * 18, out_specs=[VME...  10 us
    ppermute x2, starting transfers between devices, swap_rims(): lax.ppermute(across, 'tile', others)  5.97 us
    ppermute x2, starting transfers between devices, swap_rims(): lax.ppermute(inside, 'tile', pairs)  4.99 us
    pallas_call x1, Pallas kernels, conv_backward(): pl.pallas_call(back_kernel, in_specs=[VMEM] * (len(kept) * 2 + 3), out_sp...  4.94 us
    pallas_call x4, Pallas kernels, prepare(): pl.pallas_call(functools.partial(prepare_kernel, start), in_specs=[VMEM]...  4.92 us
    ppermute x6, starting transfers between devices, swap_turns(): out.append(lax.ppermute(parts[turn], 'tile', pairs))  4.91 us
    pallas_call x1, Pallas kernels, conv_main(): pl.pallas_call(conv_kernel, in_specs=[VMEM] * 4 + [ANYWHERE] * 2, out_spe...  4.76 us
    ppermute x6, waiting for transfers between devices, swap_turns(): out.append(lax.ppermute(parts[turn], 'tile', pairs))  4.1 us
  transfers between devices with their start and end apart: 12, of which 5 were waited for; matrix products, arithmetic and copies ran while one was open for 0% of the time, Pallas kernels for 26%

profile of v7, /device:TPU:25, one launch (start us, length us, event | category | flops | bytes accessed | tf_op | source)
XLA Modules:
  0.0 55.8 jit_solution(16400813605050553914)
XLA Ops:
  0.1 2.6 %conv_tail.1 = (f32[2,3,8,128]{3,2,1,0:T(8,128)S(1)}, bf16[32,4,128,128]{3,2,1,0:T(8,128)(2,1)S(1)}, bf16[1024,256]{1,0:T(8,128)(2,1)S(1)}, bf16[256,1024]{1,0:T...) custom-call(bf16[32,4,128,128]{3,2,1,0:T(8,128)(2,1)} %feat_hbm, f32[1,128]{1,0:T(1,128)} %bitcast.17, ...), custom_call_target="tpu_custom_call" | custom-call | tf_op jit(solution)/shard_map/conv_tail/pallas_call | solution.py:227
  2.7 1.3 %collective-permute-start = (f32[2,3,8,128]{3,2,1,0:T(8,128)S(1)}, f32[2,3,8,128]{3,2,1,0:T(8,128)S(1)}, u32[]{:S(2)}, u32[]{:S(2)}) collective-permute-start(f32[2,3,8,128]{3,2,1,0:T(8,128)S(1)} %get-tuple-element.67), channel_id=1, source_target_pairs={{0,1},{1,2},{2,3},{3,0},{4,5},{5,6},{6,7},{7,4},{8,9},{9,10},{10,1... | collective-permute-start | bytes 73736 | tf_op jit(solution)/shard_map/ppermute | solution.py:788
  4.0 4.8 %conv_main.1 = (f32[32,3,8,128]{3,2,1,0:T(8,128)S(1)}, bf16[1280,2560]{1,0:T(8,128)(2,1)S(1)}, bf16[2560,1280]{1,0:T(8,128)(2,1)S(1)}) custom-call(bf16[32,4,128,128]{3,2,1,0:T(8,128)(2,1)S(1)} %get-tuple-element.62.feat_ref, f32[1,128]{1,0:T(1,128)S(1)} %get-tuple-element.63.gain_ref, bf16[256,256]{1,0:T(8,128)(2,1)S(1)} %get-tuple-element.64.mean_ref.refs_9_, ...), custom_call_target="tpu_custom_call" | custom-call | flops 33554432 | bytes 20971520 | tf_op jit(solution)/shard_map/conv_main/pallas_call | solution.py:253
  9.4 1.0 %collective-permute-start.1 = (bf16[3,32,128]{2,1,0:T(8,128)(2,1)S(1)}, bf16[3,32,128]{2,1,0:T(8,128)(2,1)S(1)}, u32[]{:S(2)}, u32[]{:S(2)}) collective-permute-start(bf16[3,32,128]{2,1,0:T(8,128)(2,1)S(1)} %get-tuple-element.68), channel_id=1, source_target_pairs={{0,4},{4,0},{8,12},{12,8},{16,20},{20,16},{24,28},{28,24},{32,36},... | collective-permute-start | bytes 73736 | tf_op jit(solution)/shard_map/ppermute | solution.py:358
  10.5 3.7 %collective-permute-start.2 = (bf16[3,32,128]{2,1,0:T(8,128)(2,1)S(1)}, bf16[3,32,128]{2,1,0:T(8,128)(2,1)S(1)}, u32[]{:S(2)}, u32[]{:S(2)}) collective-permute-start(bf16[3,32,128]{2,1,0:T(8,128)(2,1)S(1)} %get-tuple-element.69), channel_id=1, source_target_pairs={{0,0},{4,8},{8,4},{12,16},{16,12},{20,24},{24,20},{28,32},{32,28},... | collective-permute-start | bytes 73736 | tf_op jit(solution)/shard_map/ppermute | solution.py:358
  14.3 1.2 %prepare_0.1 = (bf16[8,4,128,128]{3,2,1,0:T(8,128)(2,1)S(1)}, bf16[8,4,128,128]{3,2,1,0:T(8,128)(2,1)S(1)}) custom-call(bf16[32,4,128,128]{3,2,1,0:T(8,128)(2,1)S(1)} %get-tuple-element.62.feat_ref, f32[1,128]{1,0:T(1,128)S(1)} %get-tuple-element.63.gain_ref, bf16[256,256]{1,0:T(8,128)(2,1)S(1)} %get-tuple-element.64.mean_ref.refs_9_), custom_call_target="tpu_custom_call" | custom-call | flops 1000000000 | bytes 800000 | tf_op jit(solution)/shard_map/prepare_0/pallas_call | solution.py:636
  15.9 0.7 %colours.1 = (bf16[8,16,128]{2,1,0:T(8,128)(2,1)S(1)}, bf16[8,16,128]{2,1,0:T(8,128)(2,1)S(1)}, bf16[8,16,128]{2,1,0:T(8,128)(2,1)S(1)}, bf16[8,16,128]{2,1,0:T(8,128)(2,1)S(1)}) custom-call(s32[4]{0:T(128)S(1)} %pad_add_fusion.place_ref.own_ref, f32[3]{0:T(128)S(1)} %copy-done.12, f32[32,3,8,128]{3,2,1,0:T(8,128)S(1)} %get-tuple-element.66.sums_ref, ...), custom_call_target="tpu_custom_call" | custom-call | tf_op jit(solution)/shard_map/colours/pallas_call | solution.py:333
  16.7 1.6 %collective-permute-start.3 = (bf16[8,16,128]{2,1,0:T(8,128)(2,1)S(1)}, bf16[8,16,128]{2,1,0:T(8,128)(2,1)S(1)}, u32[]{:S(2)}, u32[]{:S(2)}) collective-permute-start(bf16[8,16,128]{2,1,0:T(8,128)(2,1)S(1)} %get-tuple-element.75), channel_id=1, source_target_pairs={{0,4},{4,8},{8,12},{12,0},{16,20},{20,24},{24,28},{28,16},{32,36},... | collective-permute-start | bytes 98312 | tf_op jit(solution)/shard_map/ppermute | solution.py:350
  18.3 2.4 %collective-permute-start.4 = (bf16[8,16,128]{2,1,0:T(8,128)(2,1)S(1)}, bf16[8,16,128]{2,1,0:T(8,128)(2,1)S(1)}, u32[]{:S(2)}, u32[]{:S(2)}) collective-permute-start(bf16[8,16,128]{2,1,0:T(8,128)(2,1)S(1)} %get-tuple-element.76), channel_id=1, source_target_pairs={{0,8},{4,12},{8,0},{12,4},{16,24},{20,28},{24,16},{28,20},{32,40},... | collective-permute-start | bytes 98312 | tf_op jit(solution)/shard_map/ppermute | solution.py:350
  20.7 1.2 %prepare_8.1 = (bf16[8,4,128,128]{3,2,1,0:T(8,128)(2,1)S(1)}, bf16[8,4,128,128]{3,2,1,0:T(8,128)(2,1)S(1)}) custom-call(bf16[32,4,128,128]{3,2,1,0:T(8,128)(2,1)S(1)} %get-tuple-element.62.feat_ref, f32[1,128]{1,0:T(1,128)S(1)} %get-tuple-element.63.gain_ref, bf16[256,256]{1,0:T(8,128)(2,1)S(1)} %get-tuple-element.64.mean_ref.refs_9_), custom_call_target="tpu_custom_call" | custom-call | flops 1000000000 | bytes 800000 | tf_op jit(solution)/shard_map/prepare_8/pallas_call | solution.py:636
  22.0 0.8 %collective-permute-done.4.x2_ref = bf16[8,16,128]{2,1,0:T(8,128)(2,1)S(1)} collective-permute-done((bf16[8,16,128]{2,1,0:T(8,128)(2,1)S(1)}, bf16[8,16,128]{2,1,0:T(8,128)(2,1)S(1)}, u32[]{:S(2)}, u32[]{:S(2)}) %collective-permute-start.4) | collective-permute-done | bytes 32800 | tf_op jit(solution)/shard_map/ppermute | solution.py:350
  22.7 1.3 %collective-permute-done.5.x3_ref = bf16[8,16,128]{2,1,0:T(8,128)(2,1)S(1)} collective-permute-done((bf16[8,16,128]{2,1,0:T(8,128)(2,1)S(1)}, bf16[8,16,128]{2,1,0:T(8,128)(2,1)S(1)}, u32[]{:S(2)}, u32[]{:S(2)}) %collective-permute-start.5) | collective-permute-done | bytes 32800 | tf_op jit(solution)/shard_map/ppermute | solution.py:350
  24.1 10.0 %pose.1 = (bf16[8,16,128]{2,1,0:T(8,128)(2,1)S(1)}, bf16[8,16,128]{2,1,0:T(8,128)(2,1)S(1)}, bf16[8,16,128]{2,1,0:T(8,128)(2,1)S(1)}, bf16[8,16,128]{2,1,0:T(8,128)(2,1)S(1)}) custom-call(s32[4]{0:T(128)S(1)} %pad_add_fusion.place_ref.own_ref, bf16[8,16,128]{2,1,0:T(8,128)(2,1)S(1)} %get-tuple-element.80.x0_ref, ...), custom_call_target="tpu_custom_call" | custom-call | flops 2022400000 | bytes 17825792 | tf_op jit(solution)/shard_map/pose/pallas_call | solution.py:507
  34.2 0.7 %collective-permute-start.7 = (bf16[8,16,128]{2,1,0:T(8,128)(2,1)S(1)}, bf16[8,16,128]{2,1,0:T(8,128)(2,1)S(1)}, u32[]{:S(2)}, u32[]{:S(2)}) collective-permute-start(bf16[8,16,128]{2,1,0:T(8,128)(2,1)S(1)} %get-tuple-element.89), channel_id=1, source_target_pairs={{0,8},{4,12},{8,0},{12,4},{16,24},{20,28},{24,16},{28,20},{32,40},... | collective-permute-start | bytes 98312 | tf_op jit(solution)/shard_map/ppermute | solution.py:350
  35.0 1.2 %prepare_16.1 = (bf16[8,4,128,128]{3,2,1,0:T(8,128)(2,1)S(1)}, bf16[8,4,128,128]{3,2,1,0:T(8,128)(2,1)S(1)}) custom-call(bf16[32,4,128,128]{3,2,1,0:T(8,128)(2,1)S(1)} %get-tuple-element.62.feat_ref, f32[1,128]{1,0:T(1,128)S(1)} %get-tuple-element.63.gain_ref, bf16[256,256]{1,0:T(8,128)(2,1)S(1)} %get-tuple-element.64.mean_ref.refs_9_), custom_call_target="tpu_custom_call" | custom-call | flops 1000000000 | bytes 800000 | tf_op jit(solution)/shard_map/prepare_16/pallas_call | solution.py:636
  36.3 0.8 %collective-permute-done.7.x2_ref = bf16[8,16,128]{2,1,0:T(8,128)(2,1)S(1)} collective-permute-done((bf16[8,16,128]{2,1,0:T(8,128)(2,1)S(1)}, bf16[8,16,128]{2,1,0:T(8,128)(2,1)S(1)}, u32[]{:S(2)}, u32[]{:S(2)}) %collective-permute-start.7) | collective-permute-done | bytes 32800 | tf_op jit(solution)/shard_map/ppermute | solution.py:350
  37.1 1.2 %collective-permute-done.8.x3_ref = bf16[8,16,128]{2,1,0:T(8,128)(2,1)S(1)} collective-permute-done((bf16[8,16,128]{2,1,0:T(8,128)(2,1)S(1)}, bf16[8,16,128]{2,1,0:T(8,128)(2,1)S(1)}, u32[]{:S(2)}, u32[]{:S(2)}) %collective-permute-start.8) | collective-permute-done | bytes 32800 | tf_op jit(solution)/shard_map/ppermute | solution.py:350
  38.3 0.7 %strip_grads.1 = (f32[32,3,8,128]{3,2,1,0:T(8,128)S(1)}, bf16[3,32,128]{2,1,0:T(8,128)(2,1)S(1)}, bf16[3,32,128]{2,1,0:T(8,128)(2,1)S(1)}) custom-call(s32[4]{0:T(128)S(1)} %pad_add_fusion.place_ref.own_ref, bf16[8,16,128]{2,1,0:T(8,128)(2,1)S(1)} %get-tuple-element.93.x0_ref, bf16[8,16,128]{2,1,0:T(8,128)(2,1)S(1)} %collective-permute-done.6.x1_ref, ...), custom_call_target="tpu_custom_call" | custom-call | tf_op jit(solution)/shard_map/strip_grads/pallas_call | solution.py:562
  39.0 2.2 %collective-permute-start.10 = (bf16[3,32,128]{2,1,0:T(8,128)(2,1)S(1)}, bf16[3,32,128]{2,1,0:T(8,128)(2,1)S(1)}, u32[]{:S(2)}, u32[]{:S(2)}) collective-permute-start(bf16[3,32,128]{2,1,0:T(8,128)(2,1)S(1)} %get-tuple-element.98), channel_id=1, source_target_pairs={{0,0},{4,8},{8,4},{12,16},{16,12},{20,24},{24,20},{28,32},{32,28},... | collective-permute-start | bytes 73736 | tf_op jit(solution)/shard_map/ppermute | solution.py:358
  41.3 4.0 %collective-permute-start.9 = (bf16[3,32,128]{2,1,0:T(8,128)(2,1)S(1)}, bf16[3,32,128]{2,1,0:T(8,128)(2,1)S(1)}, u32[]{:S(2)}, u32[]{:S(2)}) collective-permute-start(bf16[3,32,128]{2,1,0:T(8,128)(2,1)S(1)} %get-tuple-element.97), channel_id=1, source_target_pairs={{0,4},{4,0},{8,12},{12,8},{16,20},{20,16},{24,28},{28,24},{32,36},... | collective-permute-start | bytes 73736 | tf_op jit(solution)/shard_map/ppermute | solution.py:358
  45.2 1.2 %prepare_24.1 = (bf16[8,4,128,128]{3,2,1,0:T(8,128)(2,1)S(1)}, bf16[8,4,128,128]{3,2,1,0:T(8,128)(2,1)S(1)}) custom-call(bf16[32,4,128,128]{3,2,1,0:T(8,128)(2,1)S(1)} %get-tuple-element.62.feat_ref, f32[1,128]{1,0:T(1,128)S(1)} %get-tuple-element.63.gain_ref, bf16[256,256]{1,0:T(8,128)(2,1)S(1)} %get-tuple-element.64.mean_ref.refs_9_), custom_call_target="tpu_custom_call" | custom-call | flops 1000000000 | bytes 800000 | tf_op jit(solution)/shard_map/prepare_24/pallas_call | solution.py:636
  47.2 1.8 %collective-permute-start.11 = (f32[2,3,8,128]{3,2,1,0:T(8,128)S(1)}, f32[2,3,8,128]{3,2,1,0:T(8,128)S(1)}, u32[]{:S(2)}, u32[]{:S(2)}) collective-permute-start(f32[2,3,8,128]{3,2,1,0:T(8,128)S(1)} %get-tuple-element.107), channel_id=1, source_target_pairs={{1,0},{2,1},{3,2},{0,3},{5,4},{6,5},{7,6},{4,7},{9,8},{10,9},{11,1... | collective-permute-start | bytes 73736 | tf_op jit(solution)/shard_map/ppermute | solution.py:817
  48.9 4.9 %conv_back.1.prior_hbm = bf16[32,4,128,128]{3,2,1,0:T(8,128)(2,1)} custom-call(bf16[8,4,128,128]{3,2,1,0:T(8,128)(2,1)S(1)} %get-tuple-element.109.refs_0_, bf16[8,4,128,128]{3,2,1,0:T(8,128)(2,1)S(1)} %get-tuple-element.110.refs_1_, bf16[8,4,128,128]{3,2,1,0:T(8,128)(2,1)S(1)} %get-tuple-element.111.refs_2_, ...), custom_call_target="tpu_custom_call" | custom-call | flops 33554432 | bytes 9437184 | tf_op jit(solution)/shard_map/conv_back/pallas_call | solution.py:720
  53.9 1.8 %conv_last.1 = bf16[32,4,128,128]{3,2,1,0:T(8,128)(2,1)} custom-call(s32[4]{0:T(128)S(1)} %pad_add_fusion.place_ref.own_ref, bf16[8,4,128,128]{3,2,1,0:T(8,128)(2,1)S(1)} %get-tuple-element.101.refs_6_.slope_ref, bf16[8,4,128,128]{3,2,1,0:T(8,128)(2,1)S(1)} %get-tuple-element.102.refs_7_.normed_ref, ...), custom_call_target="tpu_custom_call", output_to_operand_aliasing={{}: (7, {})} | custom-call | tf_op jit(solution)/shard_map/conv_last/pallas_call | solution.py:736
  (40 shorter events, 2.0 us)
Async XLA Ops:
  2.7 6.1 %collective-permute-start = (f32[2,3,8,128]{3,2,1,0:T(8,128)S(1)}, f32[2,3,8,128]{3,2,1,0:T(8,128)S(1)}, u32[]{:S(2)}, u32[]{:S(2)}) collective-permute-start(f32[2,3,8,128]{3,2,1,0:T(8,128)S(1)} %get-tuple-element.67), channel_id=1, source_target_pairs={{0,1},{1,2},{2,3},{3,0},{4,5},{5,6},{6,7},{7,4},{8,9},{9,10},{10,1... | collective-permute-start | bytes 73736 | tf_op jit(solution)/shard_map/ppermute | solution.py:788
  9.4 6.1 %collective-permute-start.1 = (bf16[3,32,128]{2,1,0:T(8,128)(2,1)S(1)}, bf16[3,32,128]{2,1,0:T(8,128)(2,1)S(1)}, u32[]{:S(2)}, u32[]{:S(2)}) collective-permute-start(bf16[3,32,128]{2,1,0:T(8,128)(2,1)S(1)} %get-tuple-element.68), channel_id=1, source_target_pairs={{0,4},{4,0},{8,12},{12,8},{16,20},{20,16},{24,28},{28,24},{32,36},... | collective-permute-start | bytes 73736 | tf_op jit(solution)/shard_map/ppermute | solution.py:358
  10.4 13.6 %copy-start = (bf16[768,1280]{1,0:T(8,128)(2,1)S(1)}, bf16[768,1280]{1,0:T(8,128)(2,1)}, u32[]{:S(2)}) copy-start(bf16[768,1280]{1,0:T(8,128)(2,1)} %patch.1) | copy-start | bytes 5898244
  10.4 13.6 %copy-start.1 = (bf16[768,768]{1,0:T(8,128)(2,1)S(1)}, bf16[768,768]{1,0:T(8,128)(2,1)}, u32[]{:S(2)}) copy-start(bf16[768,768]{1,0:T(8,128)(2,1)} %constant.29.clone.order) | copy-start | bytes 3538948
  10.4 13.6 %copy-start.2 = (bf16[768,768]{1,0:T(8,128)(2,1)S(1)}, bf16[768,768]{1,0:T(8,128)(2,1)}, u32[]{:S(2)}) copy-start(bf16[768,768]{1,0:T(8,128)(2,1)} %constant.30.clone.order_t) | copy-start | bytes 3538948
  10.4 13.6 %copy-start.3 = (bf16[1280,272]{0,1:T(8,128)(2,1)S(1)}, bf16[1280,272]{0,1:T(8,128)(2,1)}, u32[]{:S(2)}) copy-start(bf16[1280,272]{0,1:T(8,128)(2,1)} %param.35) | copy-start | bytes 2088964
  10.4 13.6 %copy-start.4 = (bf16[64,1280]{1,0:T(8,128)(2,1)S(1)}, bf16[64,1280]{1,0:T(8,128)(2,1)}, u32[]{:S(2)}) copy-start(bf16[64,1280]{1,0:T(8,128)(2,1)} %position.1) | copy-start | bytes 491524
  10.4 13.6 %copy-start.5 = (bf16[17,272]{1,0:T(8,128)(2,1)S(1)}, bf16[17,272]{1,0:T(8,128)(2,1)}, u32[]{:S(2)}) copy-start(bf16[17,272]{1,0:T(8,128)(2,1)} %constant.28.clone.key_spread_ref) | copy-start | bytes 27748
  10.4 13.6 %copy-start.6 = (s32[32,17]{0,1:T(8,128)S(1)}, s32[32,17]{0,1:T(8,128)}, u32[]{:S(2)}) copy-start(s32[32,17]{0,1:T(8,128)} %param.27) | copy-start | bytes 6532
  10.5 13.6 %copy-start.7 = (s32[32,17]{0,1:T(8,128)S(1)}, s32[32,17]{0,1:T(8,128)}, u32[]{:S(2)}) copy-start(s32[32,17]{0,1:T(8,128)} %param.28) | copy-start | bytes 6532
  10.5 13.6 %copy-start.8 = (s32[32,17]{0,1:T(8,128)S(1)}, s32[32,17]{0,1:T(8,128)}, u32[]{:S(2)}) copy-start(s32[32,17]{0,1:T(8,128)} %param.29) | copy-start | bytes 6532
  10.5 13.6 %copy-start.9 = (f32[1280]{0:T(1024)S(1)}, f32[1280]{0:T(1024)}, u32[]{:S(2)}) copy-start(f32[1280]{0:T(1024)} %param.32) | copy-start | bytes 15364
  10.5 13.6 %copy-start.10 = (s32[1,32,3]{1,0,2:T(1,128)S(1)}, s32[1,32,3]{1,0,2:T(1,128)}, u32[]{:S(2)}) copy-start(s32[1,32,3]{1,0,2:T(1,128)} %param.25) | copy-start | bytes 1156
  10.5 13.6 %copy-start.11 = (s32[1,32]{1,0:T(1,128)S(1)}, s32[1,32]{1,0:T(1,128)}, u32[]{:S(2)}) copy-start(s32[1,32]{1,0:T(1,128)} %counts_ref.1) | copy-start | bytes 388
  10.5 5.4 %collective-permute-start.2 = (bf16[3,32,128]{2,1,0:T(8,128)(2,1)S(1)}, bf16[3,32,128]{2,1,0:T(8,128)(2,1)S(1)}, u32[]{:S(2)}, u32[]{:S(2)}) collective-permute-start(bf16[3,32,128]{2,1,0:T(8,128)(2,1)S(1)} %get-tuple-element.69), channel_id=1, source_target_pairs={{0,0},{4,8},{8,4},{12,16},{16,12},{20,24},{24,20},{28,32},{32,28},... | collective-permute-start | bytes 73736 | tf_op jit(solution)/shard_map/ppermute | solution.py:358
  16.7 5.3 %collective-permute-start.3 = (bf16[8,16,128]{2,1,0:T(8,128)(2,1)S(1)}, bf16[8,16,128]{2,1,0:T(8,128)(2,1)S(1)}, u32[]{:S(2)}, u32[]{:S(2)}) collective-permute-start(bf16[8,16,128]{2,1,0:T(8,128)(2,1)S(1)} %get-tuple-element.75), channel_id=1, source_target_pairs={{0,4},{4,8},{8,12},{12,0},{16,20},{20,24},{24,28},{28,16},{32,36},... | collective-permute-start | bytes 98312 | tf_op jit(solution)/shard_map/ppermute | solution.py:350
  18.3 4.4 %collective-permute-start.4 = (bf16[8,16,128]{2,1,0:T(8,128)(2,1)S(1)}, bf16[8,16,128]{2,1,0:T(8,128)(2,1)S(1)}, u32[]{:S(2)}, u32[]{:S(2)}) collective-permute-start(bf16[8,16,128]{2,1,0:T(8,128)(2,1)S(1)} %get-tuple-element.76), channel_id=1, source_target_pairs={{0,8},{4,12},{8,0},{12,4},{16,24},{20,28},{24,16},{28,20},{32,40},... | collective-permute-start | bytes 98312 | tf_op jit(solution)/shard_map/ppermute | solution.py:350
  20.7 3.3 %collective-permute-start.5 = (bf16[8,16,128]{2,1,0:T(8,128)(2,1)S(1)}, bf16[8,16,128]{2,1,0:T(8,128)(2,1)S(1)}, u32[]{:S(2)}, u32[]{:S(2)}) collective-permute-start(bf16[8,16,128]{2,1,0:T(8,128)(2,1)S(1)} %get-tuple-element.77), channel_id=1, source_target_pairs={{0,12},{4,0},{8,4},{12,8},{16,28},{20,16},{24,20},{28,24},{32,44},... | collective-permute-start | bytes 98312 | tf_op jit(solution)/shard_map/ppermute | solution.py:350
  34.1 2.1 %collective-permute-start.6 = (bf16[8,16,128]{2,1,0:T(8,128)(2,1)S(1)}, bf16[8,16,128]{2,1,0:T(8,128)(2,1)S(1)}, u32[]{:S(2)}, u32[]{:S(2)}) collective-permute-start(bf16[8,16,128]{2,1,0:T(8,128)(2,1)S(1)} %get-tuple-element.88), channel_id=1, source_target_pairs={{0,4},{4,8},{8,12},{12,0},{16,20},{20,24},{24,28},{28,16},{32,36},... | collective-permute-start | bytes 98312 | tf_op jit(solution)/shard_map/ppermute | solution.py:350
  34.2 2.8 %collective-permute-start.7 = (bf16[8,16,128]{2,1,0:T(8,128)(2,1)S(1)}, bf16[8,16,128]{2,1,0:T(8,128)(2,1)S(1)}, u32[]{:S(2)}, u32[]{:S(2)}) collective-permute-start(bf16[8,16,128]{2,1,0:T(8,128)(2,1)S(1)} %get-tuple-element.89), channel_id=1, source_target_pairs={{0,8},{4,12},{8,0},{12,4},{16,24},{20,28},{24,16},{28,20},{32,40},... | collective-permute-start | bytes 98312 | tf_op jit(solution)/shard_map/ppermute | solution.py:350
  34.9 3.4 %collective-permute-start.8 = (bf16[8,16,128]{2,1,0:T(8,128)(2,1)S(1)}, bf16[8,16,128]{2,1,0:T(8,128)(2,1)S(1)}, u32[]{:S(2)}, u32[]{:S(2)}) collective-permute-start(bf16[8,16,128]{2,1,0:T(8,128)(2,1)S(1)} %get-tuple-element.90), channel_id=1, source_target_pairs={{0,12},{4,0},{8,4},{12,8},{16,28},{20,16},{24,20},{28,24},{32,44},... | collective-permute-start | bytes 98312 | tf_op jit(solution)/shard_map/ppermute | solution.py:350
  39.0 7.4 %collective-permute-start.10 = (bf16[3,32,128]{2,1,0:T(8,128)(2,1)S(1)}, bf16[3,32,128]{2,1,0:T(8,128)(2,1)S(1)}, u32[]{:S(2)}, u32[]{:S(2)}) collective-permute-start(bf16[3,32,128]{2,1,0:T(8,128)(2,1)S(1)} %get-tuple-element.98), channel_id=1, source_target_pairs={{0,0},{4,8},{8,4},{12,16},{16,12},{20,24},{24,20},{28,32},{32,28},... | collective-permute-start | bytes 73736 | tf_op jit(solution)/shard_map/ppermute | solution.py:358
  41.3 5.2 %collective-permute-start.9 = (bf16[3,32,128]{2,1,0:T(8,128)(2,1)S(1)}, bf16[3,32,128]{2,1,0:T(8,128)(2,1)S(1)}, u32[]{:S(2)}, u32[]{:S(2)}) collective-permute-start(bf16[3,32,128]{2,1,0:T(8,128)(2,1)S(1)} %get-tuple-element.97), channel_id=1, source_target_pairs={{0,4},{4,0},{8,12},{12,8},{16,20},{20,16},{24,28},{28,24},{32,36},... | collective-permute-start | bytes 73736 | tf_op jit(solution)/shard_map/ppermute | solution.py:358
  47.2 6.7 %collective-permute-start.11 = (f32[2,3,8,128]{3,2,1,0:T(8,128)S(1)}, f32[2,3,8,128]{3,2,1,0:T(8,128)S(1)}, u32[]{:S(2)}, u32[]{:S(2)}) collective-permute-start(f32[2,3,8,128]{3,2,1,0:T(8,128)S(1)} %get-tuple-element.107), channel_id=1, source_target_pairs={{1,0},{2,1},{3,2},{0,3},{5,4},{6,5},{7,6},{4,7},{9,8},{10,9},{11,1... | collective-permute-start | bytes 73736 | tf_op jit(solution)/shard_map/ppermute | solution.py:817
  (1 other events, 7.2 us)
